TPU v7x, 128 devices: a whole 4x4x4 slice. The times are simulated.
128 devices in a mesh: blk: 32 (over y_hi, z, x), grp: 4 (over y_lo, core).
Axes of the slice: x: 4, y: 4 (y_hi: 2, y_lo: 2; y = y_hi * 2 + y_lo), z: 4, core: 2. Of those that a mesh axis runs over, the one named last changes fastest.
Arguments:
- coulomb_factors: bfloat16 [49152, 4096], P('blk', 'grp'), may hold values from -0.0546875 to 0.0546875
- energy_gaps: float32 [49152], P('blk'), may hold values from 0.2 to 5
- frequencies: float32 [2], replicated, may hold values from 0.3 to 2.5
Outputs:
- polar: float32 [4096, 2, 4096], P('blk', None, 'grp')
All inputs are finite; a program needn't handle non-finite values.
Results may differ from a plain program's by a relative error of at most 0.00085.
Values may be sent and summed in bfloat16 or wider, within the bound.
No kernel may reach another device: no remote copies, remote signals or barrier semaphores. Data moves between devices by JAX's collectives and lax.ppermute only.
A program may use at most 128 MiB of HBM per device.

v0:
```python
import jax
import jax.numpy as jnp
from jax import lax
from jax.sharding import PartitionSpec as P

FREQ = 2


def contract(whole, operand):
    return lax.dot_general(
        whole, operand, (((0,), (0,)), ((), ())), preferred_element_type=jnp.float32
    )


def on_device(coulomb_factors, energy_gaps, frequencies):
    row_count = coulomb_factors.shape[0]
    width = coulomb_factors.shape[1]
    weights = 4.0 * energy_gaps[:, None] / (energy_gaps[:, None] ** 2 + frequencies[None, :] ** 2)
    scaled = (coulomb_factors[:, None, :].astype(jnp.float32) * weights[:, :, None]).astype(
        jnp.bfloat16
    )
    whole = lax.all_gather(coulomb_factors, "grp", axis=1, tiled=True)
    flat = scaled.reshape(row_count, FREQ * width)
    owned = lax.psum_scatter(contract(whole, flat), "blk", scatter_dimension=0, tiled=True)
    return owned.reshape(owned.shape[0], FREQ, width)


def solution(mesh):
    in_specs = (P("blk", "grp"), P("blk"), P())
    out_specs = P("blk", None, "grp")
    return jax.shard_map(
        on_device, mesh=mesh, in_specs=in_specs, out_specs=out_specs, check_vma=False
    )
```

profile of v0, /device:TPU:1, one launch (start us, length us, event | category | flops | bytes accessed | tf_op | source)
XLA Modules:
  0.0 539.0 jit_solution(2985658799473110151)
XLA Ops:
  6.5 0.0 copy-start.1
  6.5 0.0 copy-start
  6.5 0.0 all-gather.2.cloned.1.call-start
  6.5 0.7 all-gather.2.cloned.1.call-update
  7.3 0.0 reduce-scatter.2.cloned.1.call-start
  7.3 5.3 convert_element_type.11
  12.6 0.0 copy-done.1
  12.6 0.0 copy-done
  12.6 0.1 add_divide_fusion
  12.7 0.3 copy.5
  13.0 7.1 %multiply_convert_fusion = bf16[1536,2,1024]{2,1,0:T(2,128)(2,1)S(1)} fusion(f32[1536,2]{1,0:T(8,128)S(1)} %copy.5, f32[1536,1024]{1,0:T(8,128)} %convert_element_type.11), kind=kLoop, calls=%fused_computation.1 | loop fusion | flops 6291456 | bytes 12595200 | tf_op jit(solution)/shard_map/convert_element_type | solution.py:19
  20.2 5.8 %copy.7 = bf16[192,8,2,1024]{3,1,2,0:T(8,128)(2,1)} copy(bf16[192,8,2,1024]{3,2,1,0:T(2,128)(2,1)S(1)} %bitcast.7) | data formatting | bytes 12582912
  25.9 103.0 %all-gather.2.cloned.1.call-done = bf16[1536,4096]{1,0:T(8,128)(2,1)} async-done(((bf16[1536,1024]{1,0:T(8,128)(2,1)}), bf16[1536,4096]{1,0:T(8,128)(2,1)}) %all-gather.2.cloned.1.call-update) | async-done | bytes 12582928 | tf_op jit(solution)/shard_map/all_gather | solution.py:22
  129.0 34.0 %convolution_bitcast_fusion = f32[4096,2048]{0,1:T(8,128)} fusion(bf16[1536,2048]{1,0:T(8,128)(2,1)} %bitcast.8, bf16[1536,4096]{1,0:T(8,128)(2,1)} %all-gather.2.cloned.1.call-done), kind=kOutput, calls=%fused_computation | convolution fusion | flops 25769803776 | bytes 52428800 | tf_op jit(solution)/shard_map/dot_general | solution.py:10
  163.0 0.0 reduce-scatter.2.cloned.1.call-update
  163.0 366.9 %reduce-scatter.2.cloned.1.call-done = f32[128,2048]{0,1:T(8,128)} async-done(((f32[4096,2048]{0,1:T(8,128)}), f32[128,2048]{0,1:T(8,128)}) %reduce-scatter.2.cloned.1.call-update) | async-done | bytes 1048592 | tf_op jit(solution)/shard_map/reduce_scatter | solution.py:24
  529.9 2.3 copy.6
  (2 shorter events, 0.0 us)
Async XLA Ops:
  6.5 6.1 %copy-start.1 = (f32[2]{0:T(128)S(1)}, f32[2]{0:T(128)}, u32[]{:S(2)}) copy-start(f32[2]{0:T(128)} %param.5) | copy-start | bytes 28
  6.5 6.1 %copy-start = (f32[1536]{0:T(1024)S(1)}, f32[1536]{0:T(1024)}, u32[]{:S(2)}) copy-start(f32[1536]{0:T(1024)} %param.4) | copy-start | bytes 18436
  6.5 122.4 %all-gather.2.cloned.1.call-start = ((), (), s32[]{:S(2)}) async-start(), calls=%async_computation.1 | async-start | bytes 15728640 | tf_op jit(solution)/shard_map/all_gather | solution.py:22
  7.3 522.6 %reduce-scatter.2.cloned.1.call-start = ((), (), s32[]{:S(2)}) async-start(), calls=%async_computation.2 | async-start | bytes 34603008 | tf_op jit(solution)/shard_map/reduce_scatter | solution.py:24
Sparse Core Ops, SparseCore 0:
  9.0 119.8 all-gather.1
  163.1 366.6 reduce-scatter.1
where the time goes:
time: 539 us
  waiting for transfers between devices  471 us (87%)
  matrix products  34 us (6%)
  between operations  13.4 us (2%)
  other arithmetic  12.5 us (2%)
  local copies, waits for them, and re-layouts  8.31 us (2%)
    reduce_scatter x1, waiting for transfers between devices, on_device(): lax.psum_scatter(contract(whole, flat), 'blk', scatter_dimension=0, tiled...  367 us
    all_gather x1, waiting for transfers between devices, on_device(): whole = lax.all_gather(coulomb_factors, 'grp', axis=1, tiled=True)  103 us
    dot_general x1, matrix products, contract(): lax.dot_general(whole, operand, (((0,), (0,)), ((), ())), preferred_eleme...  34 us
  transfers between devices with their start and end apart: 2, of which 2 were waited for; matrix products, arithmetic and copies ran while one was open for 3% of the time, Pallas kernels for 0%

commit v1 on v0

v1 whole, which is shorter than its diff:
```python
import functools

import jax
import jax.numpy as jnp
import numpy as np
from jax import lax
from jax.experimental import pallas as pl
from jax.experimental.pallas import tpu as pltpu
from jax.sharding import PartitionSpec as P

AXES = ("blk", "grp")
FREQ = 2
T = 128
FAR = (2, 3, 1, 0)
VMEM = 56 * 1024 * 1024


def parts_of(d):
    x, z, y_hi, grp = (d >> 2) & 3, (d >> 4) & 3, d >> 6, d & 3
    return (y_hi, x, z, grp) if grp & 1 == 0 else (y_hi, z, x, grp)


def device(y_hi, s1, s2, grp):
    x, z = (s1, s2) if grp & 1 == 0 else (s2, s1)
    return (((y_hi * 4 + z) * 4 + x) << 2) + grp


def shift_perm(d1=0, d2=0, dy=0):
    pairs = []
    for d in range(128):
        y_hi, s1, s2, grp = parts_of(d)
        pairs.append((d, device(y_hi ^ dy, (s1 + d1) & 3, (s2 + d2) & 3, grp)))
    return pairs


def group_perm(source):
    return [(blk * 4 + source(grp), blk * 4 + grp) for blk in range(32) for grp in range(4)]


def messages(d):
    y_hi, s1, s2, g = parts_of(d)
    far, mate, core = FAR[g], g ^ 1, g & 1
    own = lambda half: 8 * g + 4 * half
    return [
        ((8 * far + s1) * 4 + g, y_hi * 4 + s2),
        ((8 * far + 4 + s1) * 4 + g, y_hi * 4 + s2),
        ((own(0) + s2) * 4 + far, y_hi * 4 + s1),
        ((own(1) + s2) * 4 + far, y_hi * 4 + s1),
        ((own(0) + s1) * 4 + g, y_hi * 4 + s2),
        ((own(1) + s2) * 4 + g, y_hi * 4 + s1),
        ((8 * mate + 4 * y_hi + s1) * 4 + g, core * 4 + s2),
        ((own(y_hi) + s2) * 4 + mate, core * 4 + s1),
    ]


@functools.cache
def rounds():
    left = [messages(d) for d in range(128)]
    todo = [set(range(8)) for _ in range(128)]
    perms, sent, filled = [], np.zeros((8, 128), np.int32), np.zeros((8, 128), np.int32)
    for k in range(8):
        taken = {}

        def place(d, seen):
            for m in sorted(todo[d]):
                to = left[d][m][0]
                if to in seen:
                    continue
                seen.add(to)
                if to not in taken or place(taken[to][0], seen):
                    taken[to] = (d, m)
                    return True
            return False

        for d in range(128):
            place(d, set())
        perms.append([(d, to) for to, (d, _) in sorted(taken.items())])
        for to, (d, m) in taken.items():
            todo[d].remove(m)
            sent[k, d] = m
            filled[k, to] = left[d][m][1]
    return perms, sent, filled


def permute(value, pairs):
    return lax.ppermute(value, AXES, pairs)


def params():
    return pltpu.CompilerParams(vmem_limit_bytes=VMEM)


def product(lhs, rhs):
    return lax.dot_general(lhs, rhs, (((0,), (0,)), ((), ())), preferred_element_type=jnp.float32)


def scatter_blocks(place, total, outs, n):
    for d in range(4):
        rows = pl.ds(pl.multiple_of(((place[0] + d) & 3) * T, T), T)
        for e in range(4):
            columns = pl.ds(pl.multiple_of(((place[1] + e) & 3) * T, T), T)
            outs[d][e, n] = total[rows, columns].astype(outs[d].dtype)


def block_shapes(count):
    return [jax.ShapeDtypeStruct((4, count, T, T), jnp.float32 if d == 0 else jnp.bfloat16) for d in range(4)]


def own_kernel(place, own, weights, scaled, *rest):
    outs, total = rest[:4], rest[4]
    t = pl.program_id(0)
    h, f = t // 2, t % 2
    weight = jnp.where(f == 0, weights[:, 0:1], weights[:, 1:2])
    columns = pl.ds(pl.multiple_of(h * 512, 512), 512)
    scaled[...] = (own[:, columns].astype(jnp.float32) * weight).astype(jnp.bfloat16)
    total[...] = product(own[:, :512], scaled[...])
    scatter_blocks(place, total, outs, f * 3 + h)

    @pl.when(h == 1)
    def _():
        total[...] = product(own[:, 512:], scaled[...])
        scatter_blocks(place, total, outs, f * 3 + 2)


def own_products(place, own, weights):
    rows = own.shape[0]
    whole = lambda *shape: pl.BlockSpec(shape, lambda t, place: (0,) * len(shape))
    return pl.pallas_call(
        own_kernel,
        out_shape=[jax.ShapeDtypeStruct((rows, 2048), jnp.bfloat16)] + block_shapes(6),
        grid_spec=pltpu.PrefetchScalarGridSpec(
            num_scalar_prefetch=1,
            grid=(4,),
            in_specs=[whole(rows, 1024), whole(rows, FREQ)],
            out_specs=[pl.BlockSpec((rows, 512), lambda t, place: (0, (t % 2) * 2 + t // 2))] + [whole(4, 6, T, T)] * 4,
            scratch_shapes=[pltpu.VMEM((512, 512), jnp.float32)],
        ),
        compiler_params=params(),
        cost_estimate=pl.CostEstimate(flops=2 * 6 * 512 * 512 * rows, bytes_accessed=14 * 2**20, transcendentals=0),
        name="own_products",
    )(place, own, weights)


def cross_kernel(place, other, scaled, *rest):
    outs, total = rest[:4], rest[4]
    total[...] = product(other[...], scaled[...])
    scatter_blocks(place, total, outs, 0)


def cross_products(place, other, scaled, mate):
    rows = other.shape[0]
    if mate:
        left = lambda t, place: (0, t // 2)
        right = lambda t, place: (0, place[3] * 2 + t % 2)
    else:
        left = lambda t, place: (0, 0)
        right = lambda t, place: (0, t)
    return pl.pallas_call(
        cross_kernel,
        out_shape=block_shapes(4),
        grid_spec=pltpu.PrefetchScalarGridSpec(
            num_scalar_prefetch=1,
            grid=(4,),
            in_specs=[pl.BlockSpec((rows, 512), left), pl.BlockSpec((rows, 512), right)],
            out_specs=[pl.BlockSpec((4, 1, T, T), lambda t, place: (0, t, 0, 0))] * 4,
            scratch_shapes=[pltpu.VMEM((512, 512), jnp.float32)],
        ),
        compiler_params=params(),
        cost_estimate=pl.CostEstimate(flops=2 * 4 * 512 * 512 * rows, bytes_accessed=12 * 2**20, transcendentals=0),
        name="cross_products",
    )(place, other, scaled)


def first_sum_kernel(kept, a, b, c, *outs):
    for e in range(4):
        outs[e][...] = kept[e] + (a[e].astype(jnp.float32) + b[e].astype(jnp.float32)) + c[e].astype(jnp.float32)


def first_sum(kept, a, b, c):
    count = kept.shape[1]
    wide = pl.BlockSpec((4, 1, T, T), lambda t: (0, t, 0, 0))
    return pl.pallas_call(
        first_sum_kernel,
        out_shape=[jax.ShapeDtypeStruct((count, T, T), jnp.float32)] * 4,
        grid=(count,),
        in_specs=[wide] * 4,
        out_specs=[pl.BlockSpec((1, T, T), lambda t: (t, 0, 0))] * 4,
        compiler_params=params(),
        cost_estimate=pl.CostEstimate(flops=12 * count * T * T, bytes_accessed=56 * count * T * T, transcendentals=0),
        name="first_sum",
    )(kept, a, b, c)


def second_sum_kernel(place, kept, a, b, c, keep, send, total):
    total[...] = (kept[...] + a[...]) + (b[...] + c[...])
    half = total.shape[0] // 2
    for n in range(half):
        keep[n] = total[place[2] * half + n]
        send[n] = total[(1 - place[2]) * half + n]


def second_sum(place, kept, a, b, c):
    count = kept.shape[0]
    vmem = pl.BlockSpec(memory_space=pltpu.VMEM)
    return pl.pallas_call(
        second_sum_kernel,
        out_shape=[jax.ShapeDtypeStruct((count // 2, T, T), jnp.float32)] * 2,
        in_specs=[pl.BlockSpec(memory_space=pltpu.SMEM)] + [vmem] * 4,
        out_specs=[vmem] * 2,
        scratch_shapes=[pltpu.VMEM((count, T, T), jnp.float32)],
        compiler_params=params(),
        cost_estimate=pl.CostEstimate(flops=3 * count * T * T, bytes_accessed=20 * count * T * T, transcendentals=0),
        name="second_sum",
    )(place, kept, a, b, c)


def pack_kernel(place, order, far0, far0_in, far1, far1_in, tri, tri_in, mate, mate_in, *rest):
    outs, ready, total = rest[:8], rest[8], rest[9]
    y_hi = place[2]
    far = [[far0[h] + far0_in[h] for h in range(2)], [far1[h] + far1_in[h] for h in range(2)]]
    for half in range(2):
        for h in range(2):
            ready[half, h] = far[half][h]
            ready[2 + h, half] = far[half][h].T
    own = [tri[j] + tri_in[j] for j in range(3)]
    ready[4, 0] = own[0]
    ready[4, 1] = own[1]
    ready[5, 0] = own[1].T
    ready[5, 1] = own[2].T
    total[...] = mate[...] + mate_in[...]
    for h in range(2):
        ready[6, h] = total[2 * y_hi + h]
        ready[7, h] = total[2 * h + y_hi].T
    for k in range(8):
        outs[k][...] = ready[order[k]]


def pack(place, order, *arrays):
    vmem, smem = pl.BlockSpec(memory_space=pltpu.VMEM), pl.BlockSpec(memory_space=pltpu.SMEM)
    return pl.pallas_call(
        pack_kernel,
        out_shape=[jax.ShapeDtypeStruct((2, T, T), jnp.float32)] * 8,
        in_specs=[smem] * 2 + [vmem] * 8,
        out_specs=[vmem] * 8,
        scratch_shapes=[pltpu.VMEM((8, 2, T, T), jnp.float32), pltpu.VMEM((4, T, T), jnp.float32)],
        compiler_params=params(),
        cost_estimate=pl.CostEstimate(flops=2 * 2**20, bytes_accessed=3 * 2**20, transcendentals=0),
        name="pack",
    )(place, order, *arrays)


def unpack_kernel(slot, *rest):
    arrived, out, ready = rest[:8], rest[8], rest[9]
    for k in range(8):
        ready[slot[k]] = arrived[k][...]
    for f in range(FREQ):
        for i in range(4):
            for h in range(2):
                out[:, f, (4 * h + i) * T : (4 * h + i + 1) * T] = ready[f * 4 + i, h]


def unpack(slot, arrived):
    vmem, smem = pl.BlockSpec(memory_space=pltpu.VMEM), pl.BlockSpec(memory_space=pltpu.SMEM)
    return pl.pallas_call(
        unpack_kernel,
        out_shape=jax.ShapeDtypeStruct((T, FREQ, 1024), jnp.float32),
        in_specs=[smem] + [vmem] * 8,
        out_specs=vmem,
        scratch_shapes=[pltpu.VMEM((8, 2, T, T), jnp.float32)],
        compiler_params=params(),
        cost_estimate=pl.CostEstimate(flops=2**20, bytes_accessed=2 * 2**20, transcendentals=0),
        name="unpack",
    )(slot, *arrived)


def reduced(kept, *send):
    first = first_sum(kept, *(permute(v, shift_perm(d1=d + 1)) for d, v in enumerate(send)))
    return first[0], *(permute(v, shift_perm(d2=e + 1)) for e, v in enumerate(first[1:]))


def on_device(own, energy_gaps, frequencies):
    blk, grp = lax.axis_index("blk"), lax.axis_index("grp")
    x, z, y_hi, core = blk & 3, (blk >> 2) & 3, blk >> 4, grp & 1
    place = jnp.stack([jnp.where(core == 0, x, z), jnp.where(core == 0, z, x), y_hi, core]).astype(jnp.int32)
    perms, sent, filled = rounds()
    me = blk * 4 + grp
    order = lax.dynamic_index_in_dim(jnp.asarray(sent.T), me, 0, keepdims=False)
    slot = lax.dynamic_index_in_dim(jnp.asarray(filled.T), me, 0, keepdims=False)

    weights = 4.0 * energy_gaps[:, None] / (energy_gaps[:, None] ** 2 + frequencies[None, :] ** 2)
    mate = permute(own, group_perm(lambda g: g ^ 1))
    far = [permute(own[:, 512 * h : 512 * (h + 1)], group_perm(lambda g: FAR[g])) for h in range(2)]
    scaled, *tri = own_products(place, own, weights)
    tri = reduced(*tri)
    side = reduced(*cross_products(place, mate, scaled, True))
    cross = [reduced(*cross_products(place, far[h], scaled, False)) for h in range(2)]

    swap = shift_perm(dy=1)
    inputs = []
    for part in cross + [tri]:
        keep, send = second_sum(place, *part)
        inputs += [keep, permute(send, swap)]
    total = (side[0] + side[1]) + (side[2] + side[3])
    inputs += [total, permute(total, swap)]
    packed = pack(place, order, *inputs)
    return unpack(slot, [permute(v, p) for v, p in zip(packed, perms)])


def solution(mesh):
    in_specs = (P("blk", "grp"), P("blk"), P())
    out_specs = P("blk", None, "grp")
    return jax.shard_map(
        on_device, mesh=mesh, in_specs=in_specs, out_specs=out_specs, check_vma=False
    )
```

time: 539 us -> 207 us (0.38)
  the two profiles are of different devices: /device:TPU:1 before, /device:TPU:38 now
where the time goes in v1:
time: 207 us; the launch traced here: 206 us
  starting transfers between devices  71.2 us (34%)
  Pallas kernels  68.9 us (33%)
  waiting for transfers between devices  55.7 us (27%)
  local copies, waits for them, and re-layouts  8.21 us (4%)
  other arithmetic  2.07 us (1%)
    ppermute x39, starting transfers between devices, permute(): return lax.ppermute(value, AXES, pairs)  71.2 us
    ppermute x39, waiting for transfers between devices, permute(): return lax.ppermute(value, AXES, pairs)  55.7 us
    pallas_call x3, Pallas kernels, cross_products(): pl.pallas_call(cross_kernel, out_shape=block_shapes(4), grid_spec=pltpu.P...  26.3 us
    pallas_call x4, Pallas kernels, first_sum(): pl.pallas_call(first_sum_kernel, out_shape=[jax.ShapeDtypeStruct((count,...  16.3 us
    pallas_call x1, Pallas kernels, own_products(): pl.pallas_call(own_kernel, out_shape=[jax.ShapeDtypeStruct((rows, 2048),...  14.5 us
    pallas_call x3, Pallas kernels, second_sum(): pl.pallas_call(second_sum_kernel, out_shape=[jax.ShapeDtypeStruct((count...  6.23 us
  transfers between devices with their start and end apart: 39, of which 9 were waited for; matrix products, arithmetic and copies ran while one was open for 3% of the time, Pallas kernels for 31%

profile of v1, /device:TPU:38, one launch (start us, length us, event | category | flops | bytes accessed | tf_op | source)
XLA Modules:
  0.0 206.4 jit_solution(16578260140013199837)
XLA Ops:
  0.0 2.1 %fusion = (bf16[1536,512]{1,0:T(8,128)(2,1)S(1)}, bf16[1536,512]{1,0:T(8,128)(2,1)S(1)}) fusion(bf16[1536,1024]{1,0:T(8,128)(2,1)} %own.1), kind=kLoop, calls=%fused_computation.6 | loop fusion | bytes 6291456 | tf_op jit(solution)/shard_map/slice | solution.py:292
  2.1 1.7 collective-permute-start.8
  4.7 1.4 add_divide_fusion.weights
  6.0 14.5 %own_products.1 = (bf16[1536,2048]{1,0:T(8,128)(2,1)}, f32[4,6,128,128]{3,2,1,0:T(8,128)}, bf16[4,6,128,128]{3,2,1,0:T(8,128)(2,1)}, bf16[4,6,128,128]{3,2,1,0:T(8,128)(2,1)}, bf16[4,6,128,128]{3,2,1,0:T(8,128)(2,1)}) custom-call(s32[4]{0:T(128)} %pad_add_fusion.place, bf16[1536,1024]{1,0:T(8,128)(2,1)} %own.1, f32[1536,2]{1,0:T(8,128)} %add_divide_fusion.weights), custom_call_target="tpu_custom_call" | custom-call | flops 4831838208 | bytes 14680064 | tf_op jit(solution)/shard_map/own_products/pallas_call | solution.py:128
  21.0 2.4 %collective-permute-start.17 = (bf16[4,6,128,128]{3,2,1,0:T(8,128)(2,1)}, bf16[4,6,128,128]{3,2,1,0:T(8,128)(2,1)S(1)}, u32[]{:S(2)}, u32[]{:S(2)}) collective-permute-start(bf16[4,6,128,128]{3,2,1,0:T(8,128)(2,1)} %get-tuple-element.75), channel_id=1, source_target_pairs={{0,8},{1,33},{2,10},{3,35},{4,12},{5,37},{6,14},{7,39},{8,0},{9,41... | collective-permute-start | bytes 2359304 | tf_op jit(solution)/shard_map/ppermute | solution.py:86
  23.5 16.0 %collective-permute-done.8.other = bf16[1536,512]{1,0:T(8,128)(2,1)} collective-permute-done((bf16[1536,512]{1,0:T(8,128)(2,1)S(1)}, bf16[1536,512]{1,0:T(8,128)(2,1)}, u32[]{:S(2)}, u32[]{:S(2)}) %collective-permute-start.8) | collective-permute-done | bytes 1572896 | tf_op jit(solution)/shard_map/ppermute | solution.py:86
  40.3 8.7 %cross_products.4 = (f32[4,4,128,128]{3,2,1,0:T(8,128)}, bf16[4,4,128,128]{3,2,1,0:T(8,128)(2,1)}, bf16[4,4,128,128]{3,2,1,0:T(8,128)(2,1)}, bf16[4,4,128,128]{3,2,1,0:T(8,128)(2,1)}) custom-call(s32[4]{0:T(128)} %pad_add_fusion.place, bf16[1536,512]{1,0:T(8,128)(2,1)} %collective-permute-done.8.other, bf16[1536,2048]{1,0:T(8,128)(2,1)} %get-tuple-element.52.scaled), custom_call_target="tpu_custom_call" | custom-call | flops 3221225472 | bytes 12582912 | tf_op jit(solution)/shard_map/cross_products/pallas_call | solution.py:158
  50.2 2.7 %collective-permute-done.18.c = bf16[4,6,128,128]{3,2,1,0:T(8,128)(2,1)S(1)} collective-permute-done((bf16[4,6,128,128]{3,2,1,0:T(8,128)(2,1)}, bf16[4,6,128,128]{3,2,1,0:T(8,128)(2,1)S(1)}, u32[]{:S(2)}, u32[]{:S(2)}) %collective-permute-start.18) | collective-permute-done | bytes 786464 | tf_op jit(solution)/shard_map/ppermute | solution.py:86
  53.8 5.1 %first_sum.6 = (f32[6,128,128]{2,1,0:T(8,128)}, f32[6,128,128]{2,1,0:T(8,128)}, f32[6,128,128]{2,1,0:T(8,128)}, f32[6,128,128]{2,1,0:T(8,128)}) custom-call(f32[4,6,128,128]{3,2,1,0:T(8,128)} %get-tuple-element.73.kept, bf16[4,6,128,128]{3,2,1,0:T(8,128)(2,1)} %copy-done.1, bf16[4,6,128,128]{3,2,1,0:T(8,128)(2,1)} %copy-done.2, ...), custom_call_target="tpu_custom_call" | custom-call | flops 1179648 | bytes 5505024 | tf_op jit(solution)/shard_map/first_sum/pallas_call | solution.py:182
  58.9 1.9 collective-permute-start.19
  60.9 3.2 %collective-permute-start.9 = (bf16[4,4,128,128]{3,2,1,0:T(8,128)(2,1)S(1)}, bf16[4,4,128,128]{3,2,1,0:T(8,128)(2,1)S(1)}, u32[]{:S(2)}, u32[]{:S(2)}) collective-permute-start(bf16[4,4,128,128]{3,2,1,0:T(8,128)(2,1)S(1)} %copy-done.36), channel_id=1, source_target_pairs={{0,4},{1,17},{2,6},{3,19},{4,8},{5,21},{6,10},{7,23},{8,12},{9,25}... | collective-permute-start | bytes 1572872 | tf_op jit(solution)/shard_map/ppermute | solution.py:86
  64.1 9.0 %cross_products.5 = (f32[4,4,128,128]{3,2,1,0:T(8,128)}, bf16[4,4,128,128]{3,2,1,0:T(8,128)(2,1)}, bf16[4,4,128,128]{3,2,1,0:T(8,128)(2,1)}, bf16[4,4,128,128]{3,2,1,0:T(8,128)(2,1)}) custom-call(s32[4]{0:T(128)} %pad_add_fusion.place, bf16[1536,1024]{1,0:T(8,128)(2,1)} %collective-permute-done.23.other, bf16[1536,2048]{1,0:T(8,128)(2,1)} %get-tuple-element.52.scaled), custom_call_target="tpu_custom_call" | custom-call | flops 3221225472 | bytes 12582912 | tf_op jit(solution)/shard_map/cross_products/pallas_call | solution.py:158
  75.3 8.6 %cross_products.3 = (f32[4,4,128,128]{3,2,1,0:T(8,128)}, bf16[4,4,128,128]{3,2,1,0:T(8,128)(2,1)}, bf16[4,4,128,128]{3,2,1,0:T(8,128)(2,1)}, bf16[4,4,128,128]{3,2,1,0:T(8,128)(2,1)}) custom-call(s32[4]{0:T(128)} %pad_add_fusion.place, bf16[1536,512]{1,0:T(8,128)(2,1)} %collective-permute-done.other, bf16[1536,2048]{1,0:T(8,128)(2,1)} %get-tuple-element.52.scaled), custom_call_target="tpu_custom_call" | custom-call | flops 3221225472 | bytes 12582912 | tf_op jit(solution)/shard_map/cross_products/pallas_call | solution.py:158
  84.0 2.9 %collective-permute-start.1 = (bf16[4,4,128,128]{3,2,1,0:T(8,128)(2,1)}, bf16[4,4,128,128]{3,2,1,0:T(8,128)(2,1)S(1)}, u32[]{:S(2)}, u32[]{:S(2)}) collective-permute-start(bf16[4,4,128,128]{3,2,1,0:T(8,128)(2,1)} %get-tuple-element.54), channel_id=1, source_target_pairs={{0,4},{1,17},{2,6},{3,19},{4,8},{5,21},{6,10},{7,23},{8,12},{9,25}... | collective-permute-start | bytes 1572872 | tf_op jit(solution)/shard_map/ppermute | solution.py:86
  86.9 1.4 collective-permute-start.2
  88.3 1.9 collective-permute-start.20
  90.2 1.9 collective-permute-start.21
  92.2 1.3 collective-permute-start.3
  93.5 3.7 %first_sum.5 = (f32[4,128,128]{2,1,0:T(8,128)}, f32[4,128,128]{2,1,0:T(8,128)}, f32[4,128,128]{2,1,0:T(8,128)}, f32[4,128,128]{2,1,0:T(8,128)}) custom-call(f32[4,4,128,128]{3,2,1,0:T(8,128)} %get-tuple-element.63.kept, bf16[4,4,128,128]{3,2,1,0:T(8,128)(2,1)} %copy-done.8, bf16[4,4,128,128]{3,2,1,0:T(8,128)(2,1)} %copy-done.4, ...), custom_call_target="tpu_custom_call" | custom-call | flops 786432 | bytes 3670016 | tf_op jit(solution)/shard_map/first_sum/pallas_call | solution.py:182
  97.2 3.7 %first_sum.7 = (f32[4,128,128]{2,1,0:T(8,128)}, f32[4,128,128]{2,1,0:T(8,128)}, f32[4,128,128]{2,1,0:T(8,128)}, f32[4,128,128]{2,1,0:T(8,128)}) custom-call(f32[4,4,128,128]{3,2,1,0:T(8,128)} %get-tuple-element.83.kept, bf16[4,4,128,128]{3,2,1,0:T(8,128)(2,1)} %copy-done.9, bf16[4,4,128,128]{3,2,1,0:T(8,128)(2,1)} %copy-done.10, ...), custom_call_target="tpu_custom_call" | custom-call | flops 786432 | bytes 3670016 | tf_op jit(solution)/shard_map/first_sum/pallas_call | solution.py:182
  102.0 1.6 collective-permute-start.12
  103.6 4.6 %collective-permute-done.21.c = f32[6,128,128]{2,1,0:T(8,128)S(1)} collective-permute-done((f32[6,128,128]{2,1,0:T(8,128)S(1)}, f32[6,128,128]{2,1,0:T(8,128)S(1)}, u32[]{:S(2)}, u32[]{:S(2)}) %collective-permute-start.21) | collective-permute-done | bytes 393248 | tf_op jit(solution)/shard_map/ppermute | solution.py:86
  108.1 1.9 collective-permute-start.27
  110.1 1.8 collective-permute-start.28
  113.7 3.7 %first_sum.4 = (f32[4,128,128]{2,1,0:T(8,128)}, f32[4,128,128]{2,1,0:T(8,128)}, f32[4,128,128]{2,1,0:T(8,128)}, f32[4,128,128]{2,1,0:T(8,128)}) custom-call(f32[4,4,128,128]{3,2,1,0:T(8,128)} %get-tuple-element.53.kept, bf16[4,4,128,128]{3,2,1,0:T(8,128)(2,1)} %copy-done.5, bf16[4,4,128,128]{3,2,1,0:T(8,128)(2,1)} %copy-done.7, ...), custom_call_target="tpu_custom_call" | custom-call | flops 786432 | bytes 3670016 | tf_op jit(solution)/shard_map/first_sum/pallas_call | solution.py:182
  117.5 2.4 %collective-permute-start.14 = (f32[4,128,128]{2,1,0:T(8,128)S(1)}, f32[4,128,128]{2,1,0:T(8,128)S(1)}, u32[]{:S(2)}, u32[]{:S(2)}) collective-permute-start(f32[4,128,128]{2,1,0:T(8,128)S(1)} %copy-done.40), channel_id=1, source_target_pairs={{0,48},{1,13},{2,50},{3,15},{4,52},{5,1},{6,54},{7,3},{8,56},{9,5}... | collective-permute-start | bytes 786440 | tf_op jit(solution)/shard_map/ppermute | solution.py:86
  119.9 2.3 %collective-permute-start.4 = (f32[4,128,128]{2,1,0:T(8,128)}, f32[4,128,128]{2,1,0:T(8,128)S(1)}, u32[]{:S(2)}, u32[]{:S(2)}) collective-permute-start(f32[4,128,128]{2,1,0:T(8,128)} %get-tuple-element.58), channel_id=1, source_target_pairs={{0,16},{1,5},{2,18},{3,7},{4,20},{5,9},{6,22},{7,11},{8,24},{9,13}... | collective-permute-start | bytes 786440 | tf_op jit(solution)/shard_map/ppermute | solution.py:86
  122.3 3.0 %collective-permute-start.5 = (f32[4,128,128]{2,1,0:T(8,128)}, f32[4,128,128]{2,1,0:T(8,128)S(1)}, u32[]{:S(2)}, u32[]{:S(2)}) collective-permute-start(f32[4,128,128]{2,1,0:T(8,128)} %get-tuple-element.59), channel_id=1, source_target_pairs={{0,32},{1,9},{2,34},{3,11},{4,36},{5,13},{6,38},{7,15},{8,40},{9,1... | collective-permute-start | bytes 786440 | tf_op jit(solution)/shard_map/ppermute | solution.py:86
  125.3 3.3 %collective-permute-start.30 = (f32[4,128,128]{2,1,0:T(8,128)S(1)}, f32[4,128,128]{2,1,0:T(8,128)S(1)}, u32[]{:S(2)}, u32[]{:S(2)}) collective-permute-start(f32[4,128,128]{2,1,0:T(8,128)S(1)} %add_add_fusion.mate), channel_id=1, source_target_pairs={{0,64},{1,65},{2,66},{3,67},{4,68},{5,69},{6,70},{7,71},{8,72},{9,... | collective-permute-start | bytes 786440 | tf_op jit(solution)/shard_map/ppermute | solution.py:86
  128.6 2.3 %second_sum.5 = (f32[3,128,128]{2,1,0:T(8,128)}, f32[3,128,128]{2,1,0:T(8,128)}) custom-call(s32[4]{0:T(128)} %pad_add_fusion.place, f32[6,128,128]{2,1,0:T(8,128)} %get-tuple-element.77.kept, f32[6,128,128]{2,1,0:T(8,128)} %copy-done.13, f32[6,128,128]{2,1,0:T(8,128)} %copy-done.14, f32[6,128,128]{2,1,0:T(8,128)} %copy-done.15), custom_call_target="tpu_custom_call" | custom-call | flops 294912 | bytes 1966080 | tf_op jit(solution)/shard_map/second_sum/pallas_call | solution.py:205
  131.6 2.0 second_sum.4
  133.6 3.0 %collective-permute-start.15 = (f32[2,128,128]{2,1,0:T(8,128)}, f32[2,128,128]{2,1,0:T(8,128)S(1)}, u32[]{:S(2)}, u32[]{:S(2)}) collective-permute-start(f32[2,128,128]{2,1,0:T(8,128)} %get-tuple-element.72), channel_id=1, source_target_pairs={{0,64},{1,65},{2,66},{3,67},{4,68},{5,69},{6,70},{7,71},{8,72},{9,... | collective-permute-start | bytes 393224 | tf_op jit(solution)/shard_map/ppermute | solution.py:86
  137.4 2.0 second_sum.3
  140.0 1.2 dynamic-slice_bitcast_fusion.order
  141.2 4.8 %collective-permute-done.7.far0_in = f32[2,128,128]{2,1,0:T(8,128)S(1)} collective-permute-done((f32[2,128,128]{2,1,0:T(8,128)}, f32[2,128,128]{2,1,0:T(8,128)S(1)}, u32[]{:S(2)}, u32[]{:S(2)}) %collective-permute-start.7) | collective-permute-done | bytes 131104 | tf_op jit(solution)/shard_map/ppermute | solution.py:86
  146.8 2.6 %pack.1 = (f32[2,128,128]{2,1,0:T(8,128)}, f32[2,128,128]{2,1,0:T(8,128)}, f32[2,128,128]{2,1,0:T(8,128)}, f32[2,128,128]{2,1,0:T(8,128)}, f32[2,128,128]{2,1,0:...) custom-call(s32[4]{0:T(128)} %pad_add_fusion.place, ...), custom_call_target="tpu_custom_call" | custom-call | flops 2097152 | bytes 3145728 | tf_op jit(solution)/shard_map/pack/pallas_call | solution.py:240
  149.4 3.9 %collective-permute-start.31 = (f32[2,128,128]{2,1,0:T(8,128)}, f32[2,128,128]{2,1,0:T(8,128)S(1)}, u32[]{:S(2)}, u32[]{:S(2)}) collective-permute-start(f32[2,128,128]{2,1,0:T(8,128)} %get-tuple-element.91), channel_id=1, source_target_pairs={{0,0},{13,1},{64,2},{79,3},{20,4},{29,5},{24,6},{23,7},{104,8},{33... | collective-permute-start | bytes 393224 | tf_op jit(solution)/shard_map/ppermute | solution.py:86
  153.3 4.0 %collective-permute-start.32 = (f32[2,128,128]{2,1,0:T(8,128)}, f32[2,128,128]{2,1,0:T(8,128)S(1)}, u32[]{:S(2)}, u32[]{:S(2)}) collective-permute-start(f32[2,128,128]{2,1,0:T(8,128)} %get-tuple-element.92), channel_id=1, source_target_pairs={{64,0},{9,1},{72,2},{67,3},{100,4},{21,5},{20,6},{19,7},{120,8},{4... | collective-permute-start | bytes 393224 | tf_op jit(solution)/shard_map/ppermute | solution.py:86
  157.3 2.1 %collective-permute-start.33 = (f32[2,128,128]{2,1,0:T(8,128)}, f32[2,128,128]{2,1,0:T(8,128)S(1)}, u32[]{:S(2)}, u32[]{:S(2)}) collective-permute-start(f32[2,128,128]{2,1,0:T(8,128)} %get-tuple-element.93), channel_id=1, source_target_pairs={{16,0},{1,1},{76,2},{15,3},{36,4},{25,5},{92,6},{87,7},{56,8},{37,... | collective-permute-start | bytes 393224 | tf_op jit(solution)/shard_map/ppermute | solution.py:86
  159.5 5.2 %collective-permute-start.34 = (f32[2,128,128]{2,1,0:T(8,128)}, f32[2,128,128]{2,1,0:T(8,128)S(1)}, u32[]{:S(2)}, u32[]{:S(2)}) collective-permute-start(f32[2,128,128]{2,1,0:T(8,128)} %get-tuple-element.94), channel_id=1, source_target_pairs={{80,0},{8,1},{0,2},{11,3},{116,4},{17,5},{84,6},{95,7},{24,8},{41,... | collective-permute-start | bytes 393224 | tf_op jit(solution)/shard_map/ppermute | solution.py:86
  164.7 3.9 %collective-permute-start.35 = (f32[2,128,128]{2,1,0:T(8,128)}, f32[2,128,128]{2,1,0:T(8,128)S(1)}, u32[]{:S(2)}, u32[]{:S(2)}) collective-permute-start(f32[2,128,128]{2,1,0:T(8,128)} %get-tuple-element.95), channel_id=1, source_target_pairs={{112,0},{12,1},{68,2},{71,3},{52,4},{28,5},{88,6},{83,7},{72,8},{3... | collective-permute-start | bytes 393224 | tf_op jit(solution)/shard_map/ppermute | solution.py:86
  168.6 2.4 %collective-permute-start.36 = (f32[2,128,128]{2,1,0:T(8,128)}, f32[2,128,128]{2,1,0:T(8,128)S(1)}, u32[]{:S(2)}, u32[]{:S(2)}) collective-permute-start(f32[2,128,128]{2,1,0:T(8,128)} %get-tuple-element.96), channel_id=1, source_target_pairs={{96,0},{4,1},{8,2},{3,3},{84,4},{20,5},{28,6},{27,7},{40,8},{45,9}... | collective-permute-start | bytes 393224 | tf_op jit(solution)/shard_map/ppermute | solution.py:86
  171.0 16.8 %collective-permute-done.32.rest_1_ = f32[2,128,128]{2,1,0:T(8,128)S(1)} collective-permute-done((f32[2,128,128]{2,1,0:T(8,128)}, f32[2,128,128]{2,1,0:T(8,128)S(1)}, u32[]{:S(2)}, u32[]{:S(2)}) %collective-permute-start.32) | collective-permute-done | bytes 131104 | tf_op jit(solution)/shard_map/ppermute | solution.py:86
  187.8 1.9 collective-permute-start.37
  189.7 1.9 collective-permute-start.38
  191.7 1.3 dynamic-slice_bitcast_fusion.1.slot
  193.0 9.1 %collective-permute-done.37.rest_6_ = f32[2,128,128]{2,1,0:T(8,128)S(1)} collective-permute-done((f32[2,128,128]{2,1,0:T(8,128)}, f32[2,128,128]{2,1,0:T(8,128)S(1)}, u32[]{:S(2)}, u32[]{:S(2)}) %collective-permute-start.37) | collective-permute-done | bytes 131104 | tf_op jit(solution)/shard_map/ppermute | solution.py:86
  203.4 3.0 %unpack.1 = f32[128,2,1024]{2,1,0:T(2,128)} custom-call(s32[8]{0:T(128)} %dynamic-slice_bitcast_fusion.1.slot, f32[2,128,128]{2,1,0:T(8,128)} %copy-done.26, f32[2,128,128]{2,1,0:T(8,128)} %copy-done.27, f32[2,128,128]{2,1,0:T(8,128)} %copy-done.28, f32[2,128,128]{2,1,0:T(8,128)} %copy-done.29, f32[2,128,128]{2,1,0:T(8,128)} %copy-done.30, ...), custom_call_target="tpu_custom_call" | custom-call | flops 1048576 | bytes 2097152 | tf_op jit(solution)/shard_map/unpack/pallas_call | solution.py:264
  (139 shorter events, 13.7 us)
Async XLA Ops:
  0.0 60.9 %collective-permute-start.23 = (bf16[1536,1024]{1,0:T(8,128)(2,1)}, bf16[1536,1024]{1,0:T(8,128)(2,1)}, u32[]{:S(2)}, u32[]{:S(2)}) collective-permute-start(bf16[1536,1024]{1,0:T(8,128)(2,1)} %own.1), channel_id=1, source_target_pairs={{1,0},{0,1},{3,2},{2,3},{5,4},{4,5},{7,6},{6,7},{9,8},{8,9},{11,10... | collective-permute-start | bytes 9437192 | tf_op jit(solution)/shard_map/ppermute | solution.py:86
  2.1 37.4 %collective-permute-start.8 = (bf16[1536,512]{1,0:T(8,128)(2,1)S(1)}, bf16[1536,512]{1,0:T(8,128)(2,1)}, u32[]{:S(2)}, u32[]{:S(2)}) collective-permute-start(bf16[1536,512]{1,0:T(8,128)(2,1)S(1)} %get-tuple-element.99), channel_id=1, source_target_pairs={{2,0},{3,1},{1,2},{0,3},{6,4},{7,5},{5,6},{4,7},{10,8},{11,9},{9,1... | collective-permute-start | bytes 4718600 | tf_op jit(solution)/shard_map/ppermute | solution.py:86
  3.9 69.4 %collective-permute-start = (bf16[1536,512]{1,0:T(8,128)(2,1)S(1)}, bf16[1536,512]{1,0:T(8,128)(2,1)}, u32[]{:S(2)}, u32[]{:S(2)}) collective-permute-start(bf16[1536,512]{1,0:T(8,128)(2,1)S(1)} %get-tuple-element.100), channel_id=1, source_target_pairs={{2,0},{3,1},{1,2},{0,3},{6,4},{7,5},{5,6},{4,7},{10,8},{11,9},{9,1... | collective-permute-start | bytes 4718600 | tf_op jit(solution)/shard_map/ppermute | solution.py:86
  20.6 28.4 %collective-permute-start.16 = (bf16[4,6,128,128]{3,2,1,0:T(8,128)(2,1)}, bf16[4,6,128,128]{3,2,1,0:T(8,128)(2,1)S(1)}, u32[]{:S(2)}, u32[]{:S(2)}) collective-permute-start(bf16[4,6,128,128]{3,2,1,0:T(8,128)(2,1)} %get-tuple-element.74), channel_id=1, source_target_pairs={{0,4},{1,17},{2,6},{3,19},{4,8},{5,21},{6,10},{7,23},{8,12},{9,25}... | collective-permute-start | bytes 2359304 | tf_op jit(solution)/shard_map/ppermute | solution.py:86
  21.0 29.1 %collective-permute-start.17 = (bf16[4,6,128,128]{3,2,1,0:T(8,128)(2,1)}, bf16[4,6,128,128]{3,2,1,0:T(8,128)(2,1)S(1)}, u32[]{:S(2)}, u32[]{:S(2)}) collective-permute-start(bf16[4,6,128,128]{3,2,1,0:T(8,128)(2,1)} %get-tuple-element.75), channel_id=1, source_target_pairs={{0,8},{1,33},{2,10},{3,35},{4,12},{5,37},{6,14},{7,39},{8,0},{9,41... | collective-permute-start | bytes 2359304 | tf_op jit(solution)/shard_map/ppermute | solution.py:86
  39.5 13.4 %collective-permute-start.18 = (bf16[4,6,128,128]{3,2,1,0:T(8,128)(2,1)}, bf16[4,6,128,128]{3,2,1,0:T(8,128)(2,1)S(1)}, u32[]{:S(2)}, u32[]{:S(2)}) collective-permute-start(bf16[4,6,128,128]{3,2,1,0:T(8,128)(2,1)} %get-tuple-element.76), channel_id=1, source_target_pairs={{0,12},{1,49},{2,14},{3,51},{4,0},{5,53},{6,2},{7,55},{8,4},{9,57}... | collective-permute-start | bytes 2359304 | tf_op jit(solution)/shard_map/ppermute | solution.py:86
  49.0 25.2 %collective-permute-start.10 = (bf16[4,4,128,128]{3,2,1,0:T(8,128)(2,1)}, bf16[4,4,128,128]{3,2,1,0:T(8,128)(2,1)S(1)}, u32[]{:S(2)}, u32[]{:S(2)}) collective-permute-start(bf16[4,4,128,128]{3,2,1,0:T(8,128)(2,1)} %get-tuple-element.65), channel_id=1, source_target_pairs={{0,8},{1,33},{2,10},{3,35},{4,12},{5,37},{6,14},{7,39},{8,0},{9,41... | collective-permute-start | bytes 1572872 | tf_op jit(solution)/shard_map/ppermute | solution.py:86
  58.9 14.2 %collective-permute-start.19 = (f32[6,128,128]{2,1,0:T(8,128)}, f32[6,128,128]{2,1,0:T(8,128)S(1)}, u32[]{:S(2)}, u32[]{:S(2)}) collective-permute-start(f32[6,128,128]{2,1,0:T(8,128)} %get-tuple-element.78), channel_id=1, source_target_pairs={{0,16},{1,5},{2,18},{3,7},{4,20},{5,9},{6,22},{7,11},{8,24},{9,13}... | collective-permute-start | bytes 1179656 | tf_op jit(solution)/shard_map/ppermute | solution.py:86
  60.9 23.1 %collective-permute-start.11 = (bf16[4,4,128,128]{3,2,1,0:T(8,128)(2,1)S(1)}, bf16[4,4,128,128]{3,2,1,0:T(8,128)(2,1)S(1)}, u32[]{:S(2)}, u32[]{:S(2)}) collective-permute-start(bf16[4,4,128,128]{3,2,1,0:T(8,128)(2,1)S(1)} %copy-done.37), channel_id=1, source_target_pairs={{0,12},{1,49},{2,14},{3,51},{4,0},{5,53},{6,2},{7,55},{8,4},{9,57}... | collective-permute-start | bytes 1572872 | tf_op jit(solution)/shard_map/ppermute | solution.py:86
  60.9 26.0 %collective-permute-start.9 = (bf16[4,4,128,128]{3,2,1,0:T(8,128)(2,1)S(1)}, bf16[4,4,128,128]{3,2,1,0:T(8,128)(2,1)S(1)}, u32[]{:S(2)}, u32[]{:S(2)}) collective-permute-start(bf16[4,4,128,128]{3,2,1,0:T(8,128)(2,1)S(1)} %copy-done.36), channel_id=1, source_target_pairs={{0,4},{1,17},{2,6},{3,19},{4,8},{5,21},{6,10},{7,23},{8,12},{9,25}... | collective-permute-start | bytes 1572872 | tf_op jit(solution)/shard_map/ppermute | solution.py:86
  73.1 15.2 %collective-permute-start.24 = (bf16[4,4,128,128]{3,2,1,0:T(8,128)(2,1)}, bf16[4,4,128,128]{3,2,1,0:T(8,128)(2,1)S(1)}, u32[]{:S(2)}, u32[]{:S(2)}) collective-permute-start(bf16[4,4,128,128]{3,2,1,0:T(8,128)(2,1)} %get-tuple-element.84), channel_id=1, source_target_pairs={{0,4},{1,17},{2,6},{3,19},{4,8},{5,21},{6,10},{7,23},{8,12},{9,25}... | collective-permute-start | bytes 1572872 | tf_op jit(solution)/shard_map/ppermute | solution.py:86
  73.2 17.0 %collective-permute-start.25 = (bf16[4,4,128,128]{3,2,1,0:T(8,128)(2,1)}, bf16[4,4,128,128]{3,2,1,0:T(8,128)(2,1)S(1)}, u32[]{:S(2)}, u32[]{:S(2)}) collective-permute-start(bf16[4,4,128,128]{3,2,1,0:T(8,128)(2,1)} %get-tuple-element.85), channel_id=1, source_target_pairs={{0,8},{1,33},{2,10},{3,35},{4,12},{5,37},{6,14},{7,39},{8,0},{9,41... | collective-permute-start | bytes 1572872 | tf_op jit(solution)/shard_map/ppermute | solution.py:86
  74.2 14.1 %copy-start.39 = (f32[6,128,128]{2,1,0:T(8,128)S(1)}, f32[6,128,128]{2,1,0:T(8,128)}, u32[]{:S(2)}) copy-start(f32[6,128,128]{2,1,0:T(8,128)} %get-tuple-element.79) | copy-start | bytes 1179652
  74.2 16.1 %copy-start.38 = (f32[6,128,128]{2,1,0:T(8,128)S(1)}, f32[6,128,128]{2,1,0:T(8,128)}, u32[]{:S(2)}) copy-start(f32[6,128,128]{2,1,0:T(8,128)} %get-tuple-element.80) | copy-start | bytes 1179652
  74.2 18.0 %collective-permute-start.26 = (bf16[4,4,128,128]{3,2,1,0:T(8,128)(2,1)}, bf16[4,4,128,128]{3,2,1,0:T(8,128)(2,1)S(1)}, u32[]{:S(2)}, u32[]{:S(2)}) collective-permute-start(bf16[4,4,128,128]{3,2,1,0:T(8,128)(2,1)} %get-tuple-element.86), channel_id=1, source_target_pairs={{0,12},{1,49},{2,14},{3,51},{4,0},{5,53},{6,2},{7,55},{8,4},{9,57}... | collective-permute-start | bytes 1572872 | tf_op jit(solution)/shard_map/ppermute | solution.py:86
  84.0 26.1 %collective-permute-start.1 = (bf16[4,4,128,128]{3,2,1,0:T(8,128)(2,1)}, bf16[4,4,128,128]{3,2,1,0:T(8,128)(2,1)S(1)}, u32[]{:S(2)}, u32[]{:S(2)}) collective-permute-start(bf16[4,4,128,128]{3,2,1,0:T(8,128)(2,1)} %get-tuple-element.54), channel_id=1, source_target_pairs={{0,4},{1,17},{2,6},{3,19},{4,8},{5,21},{6,10},{7,23},{8,12},{9,25}... | collective-permute-start | bytes 1572872 | tf_op jit(solution)/shard_map/ppermute | solution.py:86
  86.9 24.9 %collective-permute-start.2 = (bf16[4,4,128,128]{3,2,1,0:T(8,128)(2,1)}, bf16[4,4,128,128]{3,2,1,0:T(8,128)(2,1)S(1)}, u32[]{:S(2)}, u32[]{:S(2)}) collective-permute-start(bf16[4,4,128,128]{3,2,1,0:T(8,128)(2,1)} %get-tuple-element.55), channel_id=1, source_target_pairs={{0,8},{1,33},{2,10},{3,35},{4,12},{5,37},{6,14},{7,39},{8,0},{9,41... | collective-permute-start | bytes 1572872 | tf_op jit(solution)/shard_map/ppermute | solution.py:86
  88.3 13.6 %collective-permute-start.20 = (f32[6,128,128]{2,1,0:T(8,128)S(1)}, f32[6,128,128]{2,1,0:T(8,128)S(1)}, u32[]{:S(2)}, u32[]{:S(2)}) collective-permute-start(f32[6,128,128]{2,1,0:T(8,128)S(1)} %copy-done.39), channel_id=1, source_target_pairs={{0,32},{1,9},{2,34},{3,11},{4,36},{5,13},{6,38},{7,15},{8,40},{9,1... | collective-permute-start | bytes 1179656 | tf_op jit(solution)/shard_map/ppermute | solution.py:86
  90.2 17.9 %collective-permute-start.21 = (f32[6,128,128]{2,1,0:T(8,128)S(1)}, f32[6,128,128]{2,1,0:T(8,128)S(1)}, u32[]{:S(2)}, u32[]{:S(2)}) collective-permute-start(f32[6,128,128]{2,1,0:T(8,128)S(1)} %copy-done.38), channel_id=1, source_target_pairs={{0,48},{1,13},{2,50},{3,15},{4,52},{5,1},{6,54},{7,3},{8,56},{9,5}... | collective-permute-start | bytes 1179656 | tf_op jit(solution)/shard_map/ppermute | solution.py:86
  92.2 20.4 %collective-permute-start.3 = (bf16[4,4,128,128]{3,2,1,0:T(8,128)(2,1)}, bf16[4,4,128,128]{3,2,1,0:T(8,128)(2,1)S(1)}, u32[]{:S(2)}, u32[]{:S(2)}) collective-permute-start(bf16[4,4,128,128]{3,2,1,0:T(8,128)(2,1)} %get-tuple-element.56), channel_id=1, source_target_pairs={{0,12},{1,49},{2,14},{3,51},{4,0},{5,53},{6,2},{7,55},{8,4},{9,57}... | collective-permute-start | bytes 1572872 | tf_op jit(solution)/shard_map/ppermute | solution.py:86
  97.2 15.4 %copy-start.41 = (f32[4,128,128]{2,1,0:T(8,128)S(1)}, f32[4,128,128]{2,1,0:T(8,128)}, u32[]{:S(2)}) copy-start(f32[4,128,128]{2,1,0:T(8,128)} %get-tuple-element.69) | copy-start | bytes 786436
  101.0 16.5 %copy-start.40 = (f32[4,128,128]{2,1,0:T(8,128)S(1)}, f32[4,128,128]{2,1,0:T(8,128)}, u32[]{:S(2)}) copy-start(f32[4,128,128]{2,1,0:T(8,128)} %get-tuple-element.70) | copy-start | bytes 786436
  101.0 24.3 %copy-start.17 = (f32[4,128,128]{2,1,0:T(8,128)S(1)}, f32[4,128,128]{2,1,0:T(8,128)}, u32[]{:S(2)}) copy-start(f32[4,128,128]{2,1,0:T(8,128)} %get-tuple-element.87) | copy-start | bytes 786436
  101.9 26.7 %copy-start.14 = (f32[6,128,128]{2,1,0:T(8,128)}, f32[6,128,128]{2,1,0:T(8,128)S(1)}, u32[]{:S(2)}) copy-start(f32[6,128,128]{2,1,0:T(8,128)S(1)} %collective-permute-done.20.b) | copy-start | bytes 1179652
  102.0 15.5 %collective-permute-start.12 = (f32[4,128,128]{2,1,0:T(8,128)S(1)}, f32[4,128,128]{2,1,0:T(8,128)S(1)}, u32[]{:S(2)}, u32[]{:S(2)}) collective-permute-start(f32[4,128,128]{2,1,0:T(8,128)S(1)} %copy-done.42), channel_id=1, source_target_pairs={{0,16},{1,5},{2,18},{3,7},{4,20},{5,9},{6,22},{7,11},{8,24},{9,13}... | collective-permute-start | bytes 786440 | tf_op jit(solution)/shard_map/ppermute | solution.py:86
  108.1 20.5 %copy-start.15 = (f32[6,128,128]{2,1,0:T(8,128)}, f32[6,128,128]{2,1,0:T(8,128)S(1)}, u32[]{:S(2)}) copy-start(f32[6,128,128]{2,1,0:T(8,128)S(1)} %collective-permute-done.21.c) | copy-start | bytes 1179652
  108.1 11.8 %collective-permute-start.27 = (f32[4,128,128]{2,1,0:T(8,128)}, f32[4,128,128]{2,1,0:T(8,128)S(1)}, u32[]{:S(2)}, u32[]{:S(2)}) collective-permute-start(f32[4,128,128]{2,1,0:T(8,128)} %get-tuple-element.88), channel_id=1, source_target_pairs={{0,16},{1,5},{2,18},{3,7},{4,20},{5,9},{6,22},{7,11},{8,24},{9,13}... | collective-permute-start | bytes 786440 | tf_op jit(solution)/shard_map/ppermute | solution.py:86
  110.1 12.2 %collective-permute-start.28 = (f32[4,128,128]{2,1,0:T(8,128)}, f32[4,128,128]{2,1,0:T(8,128)S(1)}, u32[]{:S(2)}, u32[]{:S(2)}) collective-permute-start(f32[4,128,128]{2,1,0:T(8,128)} %get-tuple-element.89), channel_id=1, source_target_pairs={{0,32},{1,9},{2,34},{3,11},{4,36},{5,13},{6,38},{7,15},{8,40},{9,1... | collective-permute-start | bytes 786440 | tf_op jit(solution)/shard_map/ppermute | solution.py:86
  111.8 13.4 %collective-permute-start.29 = (f32[4,128,128]{2,1,0:T(8,128)}, f32[4,128,128]{2,1,0:T(8,128)S(1)}, u32[]{:S(2)}, u32[]{:S(2)}) collective-permute-start(f32[4,128,128]{2,1,0:T(8,128)} %get-tuple-element.90), channel_id=1, source_target_pairs={{0,48},{1,13},{2,50},{3,15},{4,52},{5,1},{6,54},{7,3},{8,56},{9,5}... | collective-permute-start | bytes 786440 | tf_op jit(solution)/shard_map/ppermute | solution.py:86
  112.6 12.8 %collective-permute-start.13 = (f32[4,128,128]{2,1,0:T(8,128)S(1)}, f32[4,128,128]{2,1,0:T(8,128)S(1)}, u32[]{:S(2)}, u32[]{:S(2)}) collective-permute-start(f32[4,128,128]{2,1,0:T(8,128)S(1)} %copy-done.41), channel_id=1, source_target_pairs={{0,32},{1,9},{2,34},{3,11},{4,36},{5,13},{6,38},{7,15},{8,40},{9,1... | collective-permute-start | bytes 786440 | tf_op jit(solution)/shard_map/ppermute | solution.py:86
  117.5 13.4 %collective-permute-start.14 = (f32[4,128,128]{2,1,0:T(8,128)S(1)}, f32[4,128,128]{2,1,0:T(8,128)S(1)}, u32[]{:S(2)}, u32[]{:S(2)}) collective-permute-start(f32[4,128,128]{2,1,0:T(8,128)S(1)} %copy-done.40), channel_id=1, source_target_pairs={{0,48},{1,13},{2,50},{3,15},{4,52},{5,1},{6,54},{7,3},{8,56},{9,5}... | collective-permute-start | bytes 786440 | tf_op jit(solution)/shard_map/ppermute | solution.py:86
  119.9 13.7 %collective-permute-start.4 = (f32[4,128,128]{2,1,0:T(8,128)}, f32[4,128,128]{2,1,0:T(8,128)S(1)}, u32[]{:S(2)}, u32[]{:S(2)}) collective-permute-start(f32[4,128,128]{2,1,0:T(8,128)} %get-tuple-element.58), channel_id=1, source_target_pairs={{0,16},{1,5},{2,18},{3,7},{4,20},{5,9},{6,22},{7,11},{8,24},{9,13}... | collective-permute-start | bytes 786440 | tf_op jit(solution)/shard_map/ppermute | solution.py:86
  122.3 14.3 %collective-permute-start.5 = (f32[4,128,128]{2,1,0:T(8,128)}, f32[4,128,128]{2,1,0:T(8,128)S(1)}, u32[]{:S(2)}, u32[]{:S(2)}) collective-permute-start(f32[4,128,128]{2,1,0:T(8,128)} %get-tuple-element.59), channel_id=1, source_target_pairs={{0,32},{1,9},{2,34},{3,11},{4,36},{5,13},{6,38},{7,15},{8,40},{9,1... | collective-permute-start | bytes 786440 | tf_op jit(solution)/shard_map/ppermute | solution.py:86
  125.2 11.3 %collective-permute-start.6 = (f32[4,128,128]{2,1,0:T(8,128)}, f32[4,128,128]{2,1,0:T(8,128)S(1)}, u32[]{:S(2)}, u32[]{:S(2)}) collective-permute-start(f32[4,128,128]{2,1,0:T(8,128)} %get-tuple-element.60), channel_id=1, source_target_pairs={{0,48},{1,13},{2,50},{3,15},{4,52},{5,1},{6,54},{7,3},{8,56},{9,5}... | collective-permute-start | bytes 786440 | tf_op jit(solution)/shard_map/ppermute | solution.py:86
  125.3 20.7 %collective-permute-start.30 = (f32[4,128,128]{2,1,0:T(8,128)S(1)}, f32[4,128,128]{2,1,0:T(8,128)S(1)}, u32[]{:S(2)}, u32[]{:S(2)}) collective-permute-start(f32[4,128,128]{2,1,0:T(8,128)S(1)} %add_add_fusion.mate), channel_id=1, source_target_pairs={{0,64},{1,65},{2,66},{3,67},{4,68},{5,69},{6,70},{7,71},{8,72},{9,... | collective-permute-start | bytes 786440 | tf_op jit(solution)/shard_map/ppermute | solution.py:86
  130.9 10.3 %collective-permute-start.22 = (f32[3,128,128]{2,1,0:T(8,128)}, f32[3,128,128]{2,1,0:T(8,128)S(1)}, u32[]{:S(2)}, u32[]{:S(2)}) collective-permute-start(f32[3,128,128]{2,1,0:T(8,128)} %get-tuple-element.82), channel_id=1, source_target_pairs={{0,64},{1,65},{2,66},{3,67},{4,68},{5,69},{6,70},{7,71},{8,72},{9,... | collective-permute-start | bytes 589832 | tf_op jit(solution)/shard_map/ppermute | solution.py:86
  133.6 7.6 %collective-permute-start.15 = (f32[2,128,128]{2,1,0:T(8,128)}, f32[2,128,128]{2,1,0:T(8,128)S(1)}, u32[]{:S(2)}, u32[]{:S(2)}) collective-permute-start(f32[2,128,128]{2,1,0:T(8,128)} %get-tuple-element.72), channel_id=1, source_target_pairs={{0,64},{1,65},{2,66},{3,67},{4,68},{5,69},{6,70},{7,71},{8,72},{9,... | collective-permute-start | bytes 393224 | tf_op jit(solution)/shard_map/ppermute | solution.py:86
  139.4 6.7 %collective-permute-start.7 = (f32[2,128,128]{2,1,0:T(8,128)}, f32[2,128,128]{2,1,0:T(8,128)S(1)}, u32[]{:S(2)}, u32[]{:S(2)}) collective-permute-start(f32[2,128,128]{2,1,0:T(8,128)} %get-tuple-element.62), channel_id=1, source_target_pairs={{0,64},{1,65},{2,66},{3,67},{4,68},{5,69},{6,70},{7,71},{8,72},{9,... | collective-permute-start | bytes 393224 | tf_op jit(solution)/shard_map/ppermute | solution.py:86
  149.4 19.2 %collective-permute-start.31 = (f32[2,128,128]{2,1,0:T(8,128)}, f32[2,128,128]{2,1,0:T(8,128)S(1)}, u32[]{:S(2)}, u32[]{:S(2)}) collective-permute-start(f32[2,128,128]{2,1,0:T(8,128)} %get-tuple-element.91), channel_id=1, source_target_pairs={{0,0},{13,1},{64,2},{79,3},{20,4},{29,5},{24,6},{23,7},{104,8},{33... | collective-permute-start | bytes 393224 | tf_op jit(solution)/shard_map/ppermute | solution.py:86
  153.3 34.5 %collective-permute-start.32 = (f32[2,128,128]{2,1,0:T(8,128)}, f32[2,128,128]{2,1,0:T(8,128)S(1)}, u32[]{:S(2)}, u32[]{:S(2)}) collective-permute-start(f32[2,128,128]{2,1,0:T(8,128)} %get-tuple-element.92), channel_id=1, source_target_pairs={{64,0},{9,1},{72,2},{67,3},{100,4},{21,5},{20,6},{19,7},{120,8},{4... | collective-permute-start | bytes 393224 | tf_op jit(solution)/shard_map/ppermute | solution.py:86
  157.3 32.4 %collective-permute-start.33 = (f32[2,128,128]{2,1,0:T(8,128)}, f32[2,128,128]{2,1,0:T(8,128)S(1)}, u32[]{:S(2)}, u32[]{:S(2)}) collective-permute-start(f32[2,128,128]{2,1,0:T(8,128)} %get-tuple-element.93), channel_id=1, source_target_pairs={{16,0},{1,1},{76,2},{15,3},{36,4},{25,5},{92,6},{87,7},{56,8},{37,... | collective-permute-start | bytes 393224 | tf_op jit(solution)/shard_map/ppermute | solution.py:86
  159.5 33.5 %collective-permute-start.34 = (f32[2,128,128]{2,1,0:T(8,128)}, f32[2,128,128]{2,1,0:T(8,128)S(1)}, u32[]{:S(2)}, u32[]{:S(2)}) collective-permute-start(f32[2,128,128]{2,1,0:T(8,128)} %get-tuple-element.94), channel_id=1, source_target_pairs={{80,0},{8,1},{0,2},{11,3},{116,4},{17,5},{84,6},{95,7},{24,8},{41,... | collective-permute-start | bytes 393224 | tf_op jit(solution)/shard_map/ppermute | solution.py:86
  164.7 28.3 %collective-permute-start.35 = (f32[2,128,128]{2,1,0:T(8,128)}, f32[2,128,128]{2,1,0:T(8,128)S(1)}, u32[]{:S(2)}, u32[]{:S(2)}) collective-permute-start(f32[2,128,128]{2,1,0:T(8,128)} %get-tuple-element.95), channel_id=1, source_target_pairs={{112,0},{12,1},{68,2},{71,3},{52,4},{28,5},{88,6},{83,7},{72,8},{3... | collective-permute-start | bytes 393224 | tf_op jit(solution)/shard_map/ppermute | solution.py:86
  168.6 34.0 %copy-start.26 = (f32[2,128,128]{2,1,0:T(8,128)}, f32[2,128,128]{2,1,0:T(8,128)S(1)}, u32[]{:S(2)}) copy-start(f32[2,128,128]{2,1,0:T(8,128)S(1)} %collective-permute-done.31.rest_0_) | copy-start | bytes 393220
  168.6 24.4 %collective-permute-start.36 = (f32[2,128,128]{2,1,0:T(8,128)}, f32[2,128,128]{2,1,0:T(8,128)S(1)}, u32[]{:S(2)}, u32[]{:S(2)}) collective-permute-start(f32[2,128,128]{2,1,0:T(8,128)} %get-tuple-element.96), channel_id=1, source_target_pairs={{96,0},{4,1},{8,2},{3,3},{84,4},{20,5},{28,6},{27,7},{40,8},{45,9}... | collective-permute-start | bytes 393224 | tf_op jit(solution)/shard_map/ppermute | solution.py:86
  187.8 14.8 %copy-start.27 = (f32[2,128,128]{2,1,0:T(8,128)}, f32[2,128,128]{2,1,0:T(8,128)S(1)}, u32[]{:S(2)}) copy-start(f32[2,128,128]{2,1,0:T(8,128)S(1)} %collective-permute-done.32.rest_1_) | copy-start | bytes 393220
  187.8 14.3 %collective-permute-start.37 = (f32[2,128,128]{2,1,0:T(8,128)}, f32[2,128,128]{2,1,0:T(8,128)S(1)}, u32[]{:S(2)}, u32[]{:S(2)}) collective-permute-start(f32[2,128,128]{2,1,0:T(8,128)} %get-tuple-element.97), channel_id=1, source_target_pairs={{32,0},{0,1},{4,2},{7,3},{68,4},{24,5},{16,6},{91,7},{8,8},{44,9},... | collective-permute-start | bytes 393224 | tf_op jit(solution)/shard_map/ppermute | solution.py:86
  189.7 12.8 %collective-permute-start.38 = (f32[2,128,128]{2,1,0:T(8,128)}, f32[2,128,128]{2,1,0:T(8,128)S(1)}, u32[]{:S(2)}, u32[]{:S(2)}) collective-permute-start(f32[2,128,128]{2,1,0:T(8,128)} %get-tuple-element.98), channel_id=1, source_target_pairs={{48,0},{5,1},{12,2},{75,3},{4,4},{16,5},{80,6},{31,7},{88,8},{32,9... | collective-permute-start | bytes 393224 | tf_op jit(solution)/shard_map/ppermute | solution.py:86
  (35 other events, 192.8 us)

commit v2 on v0

v2 whole, which is shorter than its diff:
```python
import functools

import jax
import jax.numpy as jnp
import numpy as np
from jax import lax
from jax.experimental import pallas as pl
from jax.experimental.pallas import tpu as pltpu
from jax.sharding import PartitionSpec as P

AXES = ("blk", "grp")
FREQ = 2
T = 128
FAR = (2, 3, 1, 0)
VMEM = 24 * 1024 * 1024


def parts_of(d):
    x, z, y_hi, grp = (d >> 2) & 3, (d >> 4) & 3, d >> 6, d & 3
    return (y_hi, x, z, grp) if grp & 1 == 0 else (y_hi, z, x, grp)


def device(y_hi, s1, s2, grp):
    x, z = (s1, s2) if grp & 1 == 0 else (s2, s1)
    return (((y_hi * 4 + z) * 4 + x) << 2) + grp


def shift_perm(d1=0, d2=0, dy=0):
    pairs = []
    for d in range(128):
        y_hi, s1, s2, grp = parts_of(d)
        pairs.append((d, device(y_hi ^ dy, (s1 + d1) & 3, (s2 + d2) & 3, grp)))
    return pairs


def group_perm(source):
    return [(blk * 4 + source(grp), blk * 4 + grp) for blk in range(32) for grp in range(4)]


def block_of(core, s1, s2):
    skew = (s1 + s2) & 3
    return (s1, skew) if core == 0 else (skew, s2)


def messages(d):
    y_hi, s1, s2, g = parts_of(d)
    s1, s2 = block_of(g & 1, s1, s2)
    row = lambda group, half, block, grp: (8 * group + 4 * half + block) * 4 + grp
    if y_hi == g >> 1:
        return [
            (row(g, 0, s1, g), s2),
            (row(g, 1, s2, g), s1),
            (row(g, 0, s2, g ^ 1), s1),
            (row(g, 1, s2, g ^ 1), s1),
        ]
    far = FAR[g]
    return [
        (row(far, 0, s1, g), s2),
        (row(far, 1, s1, g), s2),
        (row(g, 0, s2, far), s1),
        (row(g, 1, s2, far), s1),
    ]


@functools.cache
def rounds():
    left = [messages(d) for d in range(128)]
    todo = [set(range(4)) for _ in range(128)]
    perms, sent, filled = [], np.zeros((4, 128), np.int32), np.zeros((4, 128), np.int32)
    for k in range(4):
        taken = {}

        def place(d, seen):
            for m in sorted(todo[d]):
                to = left[d][m][0]
                if to in seen:
                    continue
                seen.add(to)
                if to not in taken or place(taken[to][0], seen):
                    taken[to] = (d, m)
                    return True
            return False

        for d in range(128):
            place(d, set())
        perms.append([(d, to) for to, (d, _) in sorted(taken.items())])
        for to, (d, m) in taken.items():
            todo[d].remove(m)
            sent[k, d] = m
            filled[k, to] = left[d][m][1]
    return perms, sent, filled


def permute(value, pairs):
    return lax.ppermute(value, AXES, pairs)


def call(kernel, out_shape, scalars, arrays, scratch=(), flops=0, name=None):
    vmem, smem = pl.BlockSpec(memory_space=pltpu.VMEM), pl.BlockSpec(memory_space=pltpu.SMEM)
    size = 0
    return pl.pallas_call(
        kernel,
        out_shape=out_shape,
        in_specs=[smem] * len(scalars) + [vmem] * len(arrays),
        out_specs=[vmem] * len(out_shape),
        scratch_shapes=list(scratch),
        compiler_params=pltpu.CompilerParams(vmem_limit_bytes=VMEM),
        cost_estimate=pl.CostEstimate(flops=flops, bytes_accessed=size, transcendentals=0),
        name=name,
    )(*scalars, *arrays)


def floats(*shape):
    return jax.ShapeDtypeStruct(shape, jnp.float32)


def product(lhs, rhs):
    return lax.dot_general(lhs, rhs, (((0,), (0,)), ((), ())), preferred_element_type=jnp.float32)


def scatter_blocks(place, total, outs, n):
    for d in range(4):
        for e in range(4):
            s1, s2 = (place[0] + d) & 3, (place[1] + e) & 3
            skew = (s1 + s2) & 3
            rows = pl.ds(pl.multiple_of(jnp.where(place[3] == 0, s1, skew) * T, T), T)
            columns = pl.ds(pl.multiple_of(jnp.where(place[3] == 0, skew, s2) * T, T), T)
            outs[d][e, n] = total[rows, columns].astype(outs[d].dtype)


def block_shapes(count):
    return [jax.ShapeDtypeStruct((4, count, T, T), jnp.float32 if d == 0 else jnp.bfloat16) for d in range(4)]


def own_kernel(place, own, weights, scaled, *rest):
    outs, total = rest[:4], rest[4]

    def step(t, _):
        h, f = t // 2, t % 2
        weight = jnp.where(f == 0, weights[:, 0:1], weights[:, 1:2])
        columns = pl.ds(pl.multiple_of(h * 512, 512), 512)
        part = 2 * f + h
        scaled[part] = (own[:, columns].astype(jnp.float32) * weight).astype(jnp.bfloat16)
        total[...] = product(own[:, :512], scaled[part])
        scatter_blocks(place, total, outs, f * 3 + h)

        @pl.when(h == 1)
        def _():
            total[...] = product(own[:, 512:], scaled[part])
            scatter_blocks(place, total, outs, f * 3 + 2)

        return 0

    lax.fori_loop(0, 4, step, 0)


def own_products(place, own, weights):
    rows = own.shape[0]
    return call(
        own_kernel,
        [jax.ShapeDtypeStruct((4, rows, 512), jnp.bfloat16)] + block_shapes(6),
        [place],
        [own, weights],
        [pltpu.VMEM((512, 512), jnp.float32)],
        flops=2 * 6 * 512 * 512 * rows,
        name="own_products",
    )


def mate_kernel(place, other, scaled, *rest):
    outs, total = rest[:4], rest[4]

    def step(t, _):
        columns = pl.ds(pl.multiple_of(t // 2 * 512, 512), 512)
        total[...] = product(other[:, columns], scaled[2 * place[3] + t % 2])
        scatter_blocks(place, total, outs, t)
        return 0

    lax.fori_loop(0, 4, step, 0)


def far_kernel(place, other, scaled, *rest):
    outs, total = rest[:4], rest[4]

    def step(t, _):
        total[...] = product(other[...], scaled[t])
        scatter_blocks(place, total, outs, t)
        return 0

    lax.fori_loop(0, 4, step, 0)


def cross_products(kernel, place, other, scaled, name):
    return call(
        kernel,
        block_shapes(4),
        [place],
        [other, scaled],
        [pltpu.VMEM((512, 512), jnp.float32)],
        flops=2 * 4 * 512 * 512 * other.shape[0],
        name=name,
    )


def first_sum_kernel(kept, a, b, c, *outs):
    for e in range(4):
        outs[e][...] = kept[e] + (a[e].astype(jnp.float32) + b[e].astype(jnp.float32)) + c[e].astype(jnp.float32)


def first_sum(kept, a, b, c):
    count = kept.shape[1]
    return call(first_sum_kernel, [floats(count, T, T)] * 4, [], [kept, a, b, c], flops=12 * count * T * T, name="first_sum")


def pack_kernel(place, order, near, twin, far0, far0_in, far1, far1_in, *rest):
    outs, ready = rest[:4], rest[4]
    at_home = place[4] == 1

    @pl.when(at_home)
    def _():
        core = place[3]
        for f in range(FREQ):
            low, both, high = (near[3 * f + j] for j in range(3))
            ready[0, f, 0] = low
            ready[0, f, 1] = both
            ready[1, f, 0] = both.T
            ready[1, f, 1] = high.T
        for k in range(2):
            for h in range(2):
                ready[2 + k, core, h] = near[6 + 2 * h + k].T
                ready[2 + k, 1 - core, h] = twin[2 * k + h]

    @pl.when(jnp.logical_not(at_home))
    def _():
        for half, (part, arrived) in enumerate(((far0, far0_in), (far1, far1_in))):
            for f in range(FREQ):
                for h in range(2):
                    value = part[2 * f + h] + arrived[2 * f + h]
                    ready[half, f, h] = value
                    ready[2 + h, f, half] = value.T

    for k in range(4):
        outs[k][...] = ready[order[k]]


def pack(place, order, *arrays):
    return call(
        pack_kernel,
        [floats(FREQ, 2, T, T)] * 4,
        [place, order],
        arrays,
        [pltpu.VMEM((4, FREQ, 2, T, T), jnp.float32)],
        flops=2**20,
        name="pack",
    )


def unpack_kernel(slot, a, b, c, d, out):
    for k, arrived in enumerate((a, b, c, d)):
        for f in range(FREQ):
            for h in range(2):
                out[:, f, pl.ds(pl.multiple_of(512 * h + slot[k] * T, T), T)] = arrived[f, h]


def unpack(slot, arrived):
    return call(unpack_kernel, [floats(T, FREQ, 1024)], [slot], arrived, flops=2**18, name="unpack")[0]


def after(value, earlier):
    return value if earlier is None else lax.optimization_barrier((value, earlier))[0]


def send_first(send, earlier):
    return [permute(after(v, w), shift_perm(d1=d + 1)) for d, (v, w) in enumerate(zip(send, earlier))]


def send_second(send, earlier):
    return [permute(after(v, w), shift_perm(d2=e + 1)) for e, (v, w) in enumerate(zip(send, earlier))]


def across(value, at_home):
    pairs = [(s, d) for s, d in shift_perm(dy=1) if ((d >> 6) == (d & 3) >> 1) == at_home]
    return permute(value, pairs)


def on_device(own, energy_gaps, frequencies):
    blk, grp = lax.axis_index("blk"), lax.axis_index("grp")
    x, z, y_hi, core = blk & 3, (blk >> 2) & 3, blk >> 4, grp & 1
    home = jnp.where(y_hi == grp >> 1, 1, 0)
    place = jnp.stack([jnp.where(core == 0, x, z), jnp.where(core == 0, z, x), y_hi, core, home]).astype(jnp.int32)
    perms, sent, filled = rounds()
    me = blk * 4 + grp
    order = lax.dynamic_index_in_dim(jnp.asarray(sent.T), me, 0, keepdims=False)
    slot = lax.dynamic_index_in_dim(jnp.asarray(filled.T), me, 0, keepdims=False)

    weights = 4.0 * energy_gaps[:, None] / (energy_gaps[:, None] ** 2 + frequencies[None, :] ** 2)
    swap = group_perm(lambda g: g ^ 1)
    halves = [own[:, :512], own[:, 512:]]
    own, *halves = lax.optimization_barrier((own, *halves))
    far_perm = group_perm(lambda g: FAR[g])
    other = permute(own, swap)
    far0 = permute(halves[0], far_perm)
    far1 = permute(after(halves[1], far0), far_perm)

    scaled, tri, *send = own_products(place, own, weights)
    tri_sent = send_first(send, [None] * 3)
    mate, *send = cross_products(mate_kernel, place, other, scaled, "mate_products")
    mate_sent = send_first(send, tri_sent)
    tri, *tri_send = first_sum(tri, *tri_sent)
    mate, *mate_send = first_sum(mate, *mate_sent)
    sums = [jnp.concatenate(v) for v in zip([tri, *tri_send], [mate, *mate_send])]
    near, near_send = sums[0], sums[1:]

    far0, *send = cross_products(far_kernel, place, far0, scaled, "far_products")
    far0_sent = send_first(send, mate_sent)
    near_sent = send_second(near_send, far0_sent)
    far0, *send = first_sum(far0, *far0_sent)
    far0_sent = send_second(send, near_sent)
    far1, *send = cross_products(far_kernel, place, far1, scaled, "far_products")
    far1_sent = send_first(send, far0_sent)
    far1, *send = first_sum(far1, *far1_sent)
    far1_sent = send_second(send, [None] * 3)

    near = near + near_sent[0] + near_sent[1] + near_sent[2]
    near = near + across(near, True)
    far0 = far0 + far0_sent[0] + far0_sent[1] + far0_sent[2]
    far1 = far1 + far1_sent[0] + far1_sent[1] + far1_sent[2]
    twin = permute(near[6:], swap)
    inputs = [near, twin, far0, across(far0, False), far1, across(far1, False)]
    packed = pack(place, order, *inputs)
    return unpack(slot, [permute(v, p) for v, p in zip(packed, perms)])


def solution(mesh):
    in_specs = (P("blk", "grp"), P("blk"), P())
    out_specs = P("blk", None, "grp")
    return jax.shard_map(
        on_device, mesh=mesh, in_specs=in_specs, out_specs=out_specs, check_vma=False
    )
```

time: 539 us -> 163 us (0.30)
  the two profiles are of different devices: /device:TPU:1 before, /device:TPU:19 now
where the time goes in v2:
time: 163 us
  starting transfers between devices  75.1 us (46%)
  waiting for transfers between devices  47.1 us (29%)
  Pallas kernels  31.6 us (19%)
  local copies, waits for them, and re-layouts  6.57 us (4%)
  other arithmetic  1.87 us (1%)
    ppermute x32, starting transfers between devices, permute(): return lax.ppermute(value, AXES, pairs)  75.1 us
    ppermute x32, waiting for transfers between devices, permute(): return lax.ppermute(value, AXES, pairs)  47.1 us
    pallas_call x10, Pallas kernels, call(): pl.pallas_call(kernel, out_shape=out_shape, in_specs=[smem] * len(scalars...  31.6 us
    slice x1, local copies, waits for them, and re-layouts, on_device(): halves = [own[:, :512], own[:, 512:]]  3.92 us
  transfers between devices with their start and end apart: 32, of which 13 were waited for; matrix products, arithmetic and copies ran while one was open for 2% of the time, Pallas kernels for 18%

profile of v2, /device:TPU:19, one launch (start us, length us, event | category | flops | bytes accessed | tf_op | source)
XLA Modules:
  0.0 162.5 jit_solution(17898437214198887978)
XLA Ops:
  0.0 3.9 %fusion.2 = (bf16[1536,512]{1,0:T(8,128)(2,1)}, bf16[1536,512]{1,0:T(8,128)(2,1)}) fusion(bf16[1536,1024]{1,0:T(8,128)(2,1)} %own), kind=kLoop, calls=%fused_computation.12 | loop fusion | bytes 6291456 | tf_op jit(solution)/shard_map/slice | solution.py:298
  3.9 0.7 collective-permute-start.3
  4.6 0.9 collective-permute-start.7
  5.5 1.4 add_divide_fusion.weights
  7.0 1.1 copy-done.1
  8.1 9.8 %own_products.1 = (bf16[4,1536,512]{2,1,0:T(8,128)(2,1)S(1)}, f32[4,6,128,128]{3,2,1,0:T(8,128)S(1)}, bf16[4,6,128,128]{3,2,1,0:T(8,128)(2,1)S(1)}, bf16[4,6,128...) custom-call(s32[5]{0:T(128)S(1)} %stack.23.place, bf16[1536,1024]{1,0:T(8,128)(2,1)S(1)} %copy-done, ...), custom_call_target="tpu_custom_call" | custom-call | flops 4831838208 | tf_op jit(solution)/shard_map/own_products/pallas_call | solution.py:101
  17.9 3.7 %collective-permute-start.1 = (bf16[4,6,128,128]{3,2,1,0:T(8,128)(2,1)S(1)}, bf16[4,6,128,128]{3,2,1,0:T(8,128)(2,1)S(1)}, u32[]{:S(2)}, u32[]{:S(2)}) collective-permute-start(bf16[4,6,128,128]{3,2,1,0:T(8,128)(2,1)S(1)} %get-tuple-element.64), channel_id=1, source_target_pairs={{0,8},{1,33},{2,10},{3,35},{4,12},{5,37},{6,14},{7,39},{8,0},{9,41... | collective-permute-start | bytes 2359304 | tf_op jit(solution)/shard_map/ppermute | solution.py:95
  21.6 0.7 collective-permute-start
  22.3 1.9 %collective-permute-start.2 = (bf16[4,6,128,128]{3,2,1,0:T(8,128)(2,1)S(1)}, bf16[4,6,128,128]{3,2,1,0:T(8,128)(2,1)S(1)}, u32[]{:S(2)}, u32[]{:S(2)}) collective-permute-start(bf16[4,6,128,128]{3,2,1,0:T(8,128)(2,1)S(1)} %get-tuple-element.65), channel_id=1, source_target_pairs={{0,12},{1,49},{2,14},{3,51},{4,0},{5,53},{6,2},{7,55},{8,4},{9,57}... | collective-permute-start | bytes 2359304 | tf_op jit(solution)/shard_map/ppermute | solution.py:95
  24.2 6.7 %mate_products.1 = (f32[4,4,128,128]{3,2,1,0:T(8,128)S(1)}, bf16[4,4,128,128]{3,2,1,0:T(8,128)(2,1)S(1)}, bf16[4,4,128,128]{3,2,1,0:T(8,128)(2,1)S(1)}, bf16[4,4,128,128]{3,2,1,0:T(8,128)(2,1)S(1)}) custom-call(s32[5]{0:T(128)S(1)} %stack.23.place, bf16[1536,1024]{1,0:T(8,128)(2,1)} %collective-permute-done.3.other, ...), custom_call_target="tpu_custom_call" | custom-call | flops 3221225472 | tf_op jit(solution)/shard_map/mate_products/pallas_call | solution.py:101
  31.0 3.2 %collective-permute-start.5 = (bf16[4,4,128,128]{3,2,1,0:T(8,128)(2,1)S(1)}, bf16[4,4,128,128]{3,2,1,0:T(8,128)(2,1)S(1)}, u32[]{:S(2)}, u32[]{:S(2)}) collective-permute-start(bf16[4,4,128,128]{3,2,1,0:T(8,128)(2,1)S(1)} %get-tuple-element.72), channel_id=1, source_target_pairs={{0,8},{1,33},{2,10},{3,35},{4,12},{5,37},{6,14},{7,39},{8,0},{9,41... | collective-permute-start | bytes 1572872 | tf_op jit(solution)/shard_map/ppermute | solution.py:95
  34.2 5.1 %collective-permute-done.a = bf16[4,6,128,128]{3,2,1,0:T(8,128)(2,1)S(1)} collective-permute-done((bf16[4,6,128,128]{3,2,1,0:T(8,128)(2,1)S(1)}, bf16[4,6,128,128]{3,2,1,0:T(8,128)(2,1)S(1)}, u32[]{:S(2)}, u32[]{:S(2)}) %collective-permute-start) | collective-permute-done | bytes 786464 | tf_op jit(solution)/shard_map/ppermute | solution.py:95
  39.4 1.9 %collective-permute-start.4 = (bf16[4,4,128,128]{3,2,1,0:T(8,128)(2,1)S(1)}, bf16[4,4,128,128]{3,2,1,0:T(8,128)(2,1)S(1)}, u32[]{:S(2)}, u32[]{:S(2)}) collective-permute-start(bf16[4,4,128,128]{3,2,1,0:T(8,128)(2,1)S(1)} %get-tuple-element.70), channel_id=1, source_target_pairs={{0,4},{1,17},{2,6},{3,19},{4,8},{5,21},{6,10},{7,23},{8,12},{9,25}... | collective-permute-start | bytes 1572872 | tf_op jit(solution)/shard_map/ppermute | solution.py:95
  41.3 1.2 collective-permute-start.6
  42.7 6.0 %far_products.2 = (f32[4,4,128,128]{3,2,1,0:T(8,128)S(1)}, bf16[4,4,128,128]{3,2,1,0:T(8,128)(2,1)S(1)}, bf16[4,4,128,128]{3,2,1,0:T(8,128)(2,1)S(1)}, bf16[4,4,128,128]{3,2,1,0:T(8,128)(2,1)S(1)}) custom-call(s32[5]{0:T(128)S(1)} %stack.23.place, bf16[1536,512]{1,0:T(8,128)(2,1)} %collective-permute-done.7.other, ...), custom_call_target="tpu_custom_call" | custom-call | flops 3221225472 | tf_op jit(solution)/shard_map/far_products/pallas_call | solution.py:101
  48.7 3.7 %collective-permute-start.10 = (bf16[4,4,128,128]{3,2,1,0:T(8,128)(2,1)S(1)}, bf16[4,4,128,128]{3,2,1,0:T(8,128)(2,1)S(1)}, u32[]{:S(2)}, u32[]{:S(2)}) collective-permute-start(bf16[4,4,128,128]{3,2,1,0:T(8,128)(2,1)S(1)} %get-tuple-element.85), channel_id=1, source_target_pairs={{0,8},{1,33},{2,10},{3,35},{4,12},{5,37},{6,14},{7,39},{8,0},{9,41... | collective-permute-start | bytes 1572872 | tf_op jit(solution)/shard_map/ppermute | solution.py:95
  52.4 0.7 collective-permute-start.8
  53.2 1.9 %collective-permute-start.12 = (bf16[4,4,128,128]{3,2,1,0:T(8,128)(2,1)S(1)}, bf16[4,4,128,128]{3,2,1,0:T(8,128)(2,1)S(1)}, u32[]{:S(2)}, u32[]{:S(2)}) collective-permute-start(bf16[4,4,128,128]{3,2,1,0:T(8,128)(2,1)S(1)} %get-tuple-element.90), channel_id=1, source_target_pairs={{0,12},{1,49},{2,14},{3,51},{4,0},{5,53},{6,2},{7,55},{8,4},{9,57}... | collective-permute-start | bytes 1572872 | tf_op jit(solution)/shard_map/ppermute | solution.py:95
  55.7 3.4 %collective-permute-done.10.b = bf16[4,4,128,128]{3,2,1,0:T(8,128)(2,1)S(1)} collective-permute-done((bf16[4,4,128,128]{3,2,1,0:T(8,128)(2,1)S(1)}, bf16[4,4,128,128]{3,2,1,0:T(8,128)(2,1)S(1)}, u32[]{:S(2)}, u32[]{:S(2)}) %collective-permute-start.10) | collective-permute-done | bytes 524320 | tf_op jit(solution)/shard_map/ppermute | solution.py:95
  59.1 5.5 %collective-permute-done.8.a = bf16[4,4,128,128]{3,2,1,0:T(8,128)(2,1)S(1)} collective-permute-done((bf16[4,4,128,128]{3,2,1,0:T(8,128)(2,1)S(1)}, bf16[4,4,128,128]{3,2,1,0:T(8,128)(2,1)S(1)}, u32[]{:S(2)}, u32[]{:S(2)}) %collective-permute-start.8) | collective-permute-done | bytes 524320 | tf_op jit(solution)/shard_map/ppermute | solution.py:95
  65.0 2.8 %collective-permute-start.11 = (f32[10,128,128]{2,1,0:T(8,128)S(1)}, f32[10,128,128]{2,1,0:T(8,128)S(1)}, u32[]{:S(2)}, u32[]{:S(2)}) collective-permute-start(f32[10,128,128]{2,1,0:T(8,128)S(1)} %pad_maximum_fusion.1), channel_id=1, source_target_pairs={{0,32},{1,9},{2,34},{3,11},{4,36},{5,13},{6,38},{7,15},{8,40},{9,1... | collective-permute-start | bytes 1966088 | tf_op jit(solution)/shard_map/ppermute | solution.py:95
  68.6 5.7 %collective-permute-done.9 = f32[10,128,128]{2,1,0:T(8,128)S(1)} collective-permute-done((f32[10,128,128]{2,1,0:T(8,128)S(1)}, f32[10,128,128]{2,1,0:T(8,128)S(1)}, u32[]{:S(2)}, u32[]{:S(2)}) %collective-permute-start.9) | collective-permute-done | bytes 655392 | tf_op jit(solution)/shard_map/ppermute | solution.py:95
  74.7 1.5 collective-permute-done.11
  76.2 9.5 %collective-permute-start.17 = (f32[4,128,128]{2,1,0:T(8,128)S(1)}, f32[4,128,128]{2,1,0:T(8,128)S(1)}, u32[]{:S(2)}, u32[]{:S(2)}) collective-permute-start(f32[4,128,128]{2,1,0:T(8,128)S(1)} %get-tuple-element.97), channel_id=1, source_target_pairs={{0,32},{1,9},{2,34},{3,11},{4,36},{5,13},{6,38},{7,15},{8,40},{9,1... | collective-permute-start | bytes 786440 | tf_op jit(solution)/shard_map/ppermute | solution.py:95
  85.8 5.1 %far_products.3 = (f32[4,4,128,128]{3,2,1,0:T(8,128)S(1)}, bf16[4,4,128,128]{3,2,1,0:T(8,128)(2,1)S(1)}, bf16[4,4,128,128]{3,2,1,0:T(8,128)(2,1)S(1)}, bf16[4,4,128,128]{3,2,1,0:T(8,128)(2,1)S(1)}) custom-call(s32[5]{0:T(128)S(1)} %stack.23.place, bf16[1536,512]{1,0:T(8,128)(2,1)S(1)} %collective-permute-done.20.other, ...), custom_call_target="tpu_custom_call" | custom-call | flops 3221225472 | tf_op jit(solution)/shard_map/far_products/pallas_call | solution.py:101
  90.9 1.5 collective-permute-start.21
  92.5 1.3 collective-permute-start.22
  93.7 2.0 %collective-permute-start.23 = (bf16[4,4,128,128]{3,2,1,0:T(8,128)(2,1)S(1)}, bf16[4,4,128,128]{3,2,1,0:T(8,128)(2,1)S(1)}, u32[]{:S(2)}, u32[]{:S(2)}) collective-permute-start(bf16[4,4,128,128]{3,2,1,0:T(8,128)(2,1)S(1)} %get-tuple-element.108), channel_id=1, source_target_pairs={{0,12},{1,49},{2,14},{3,51},{4,0},{5,53},{6,2},{7,55},{8,4},{9,57}... | collective-permute-start | bytes 1572872 | tf_op jit(solution)/shard_map/ppermute | solution.py:95
  95.9 2.0 %collective-permute-start.14 = (f32[10,128,128]{2,1,0:T(8,128)S(1)}, f32[10,128,128]{2,1,0:T(8,128)S(1)}, u32[]{:S(2)}, u32[]{:S(2)}) collective-permute-start(f32[10,128,128]{2,1,0:T(8,128)S(1)} %fusion.1), channel_id=1, source_target_pairs={{2,66},{3,67},{6,70},{7,71},{10,74},{11,75},{14,78},{15,79},{18,82... | collective-permute-start | bytes 1966088 | tf_op jit(solution)/shard_map/ppermute | solution.py:95
  97.9 2.4 %collective-permute-done.21.a = bf16[4,4,128,128]{3,2,1,0:T(8,128)(2,1)S(1)} collective-permute-done((bf16[4,4,128,128]{3,2,1,0:T(8,128)(2,1)S(1)}, bf16[4,4,128,128]{3,2,1,0:T(8,128)(2,1)S(1)}, u32[]{:S(2)}, u32[]{:S(2)}) %collective-permute-start.21) | collective-permute-done | bytes 524320 | tf_op jit(solution)/shard_map/ppermute | solution.py:95
  100.2 5.6 %collective-permute-done.22.b = bf16[4,4,128,128]{3,2,1,0:T(8,128)(2,1)S(1)} collective-permute-done((bf16[4,4,128,128]{3,2,1,0:T(8,128)(2,1)S(1)}, bf16[4,4,128,128]{3,2,1,0:T(8,128)(2,1)S(1)}, u32[]{:S(2)}, u32[]{:S(2)}) %collective-permute-start.22) | collective-permute-done | bytes 524320 | tf_op jit(solution)/shard_map/ppermute | solution.py:95
  105.9 0.9 collective-permute-done.23.c
  107.0 1.5 collective-permute-start.24
  108.5 2.9 %collective-permute-start.25 = (f32[4,128,128]{2,1,0:T(8,128)S(1)}, f32[4,128,128]{2,1,0:T(8,128)S(1)}, u32[]{:S(2)}, u32[]{:S(2)}) collective-permute-start(f32[4,128,128]{2,1,0:T(8,128)S(1)} %get-tuple-element.111), channel_id=1, source_target_pairs={{0,32},{1,9},{2,34},{3,11},{4,36},{5,13},{6,38},{7,15},{8,40},{9,1... | collective-permute-start | bytes 786440 | tf_op jit(solution)/shard_map/ppermute | solution.py:95
  111.5 1.3 collective-permute-start.19
  112.9 5.4 %collective-permute-start.15 = (f32[4,128,128]{2,1,0:T(8,128)S(1)}, f32[4,128,128]{2,1,0:T(8,128)S(1)}, u32[]{:S(2)}, u32[]{:S(2)}) collective-permute-start(f32[4,128,128]{2,1,0:T(8,128)S(1)} %slice.12), channel_id=1, source_target_pairs={{1,0},{0,1},{3,2},{2,3},{5,4},{4,5},{7,6},{6,7},{9,8},{8,9},{11,10... | collective-permute-start | bytes 786440 | tf_op jit(solution)/shard_map/ppermute | solution.py:95
  118.4 1.3 collective-permute-start.27
  119.7 0.7 dynamic-slice_bitcast_fusion.order
  120.5 8.2 %collective-permute-done.27.far1_in = f32[4,128,128]{2,1,0:T(8,128)S(1)} collective-permute-done((f32[4,128,128]{2,1,0:T(8,128)S(1)}, f32[4,128,128]{2,1,0:T(8,128)S(1)}, u32[]{:S(2)}, u32[]{:S(2)}) %collective-permute-start.27) | collective-permute-done | bytes 262176 | tf_op jit(solution)/shard_map/ppermute | solution.py:95
  128.7 0.8 pack.1
  129.5 3.6 %collective-permute-start.28 = (f32[2,2,128,128]{3,2,1,0:T(8,128)S(1)}, f32[2,2,128,128]{3,2,1,0:T(8,128)S(1)}, u32[]{:S(2)}, u32[]{:S(2)}) collective-permute-start(f32[2,2,128,128]{3,2,1,0:T(8,128)S(1)} %get-tuple-element.113), channel_id=1, source_target_pairs={{16,0},{40,1},{92,2},{3,3},{52,4},{56,5},{80,6},{7,7},{24,8},{32,9... | collective-permute-start | bytes 786440 | tf_op jit(solution)/shard_map/ppermute | solution.py:95
  133.1 1.9 %collective-permute-start.29 = (f32[2,2,128,128]{3,2,1,0:T(8,128)S(1)}, f32[2,2,128,128]{3,2,1,0:T(8,128)S(1)}, u32[]{:S(2)}, u32[]{:S(2)}) collective-permute-start(f32[2,2,128,128]{3,2,1,0:T(8,128)S(1)} %get-tuple-element.114), channel_id=1, source_target_pairs={{0,0},{28,1},{64,2},{43,3},{20,4},{16,5},{68,6},{19,7},{56,8},{8,9... | collective-permute-start | bytes 786440 | tf_op jit(solution)/shard_map/ppermute | solution.py:95
  135.0 9.5 %collective-permute-start.30 = (f32[2,2,128,128]{3,2,1,0:T(8,128)S(1)}, f32[2,2,128,128]{3,2,1,0:T(8,128)S(1)}, u32[]{:S(2)}, u32[]{:S(2)}) collective-permute-start(f32[2,2,128,128]{3,2,1,0:T(8,128)S(1)} %get-tuple-element.115), channel_id=1, source_target_pairs={{32,0},{52,1},{116,2},{55,3},{36,4},{4,5},{108,6},{47,7},{40,8},{6... | collective-permute-start | bytes 786440 | tf_op jit(solution)/shard_map/ppermute | solution.py:95
  144.6 6.5 %collective-permute-start.31 = (f32[2,2,128,128]{3,2,1,0:T(8,128)S(1)}, f32[2,2,128,128]{3,2,1,0:T(8,128)S(1)}, u32[]{:S(2)}, u32[]{:S(2)}) collective-permute-start(f32[2,2,128,128]{3,2,1,0:T(8,128)S(1)} %get-tuple-element.116), channel_id=1, source_target_pairs={{48,0},{0,1},{104,2},{31,3},{4,4},{44,5},{120,6},{59,7},{8,8},{20,... | collective-permute-start | bytes 786440 | tf_op jit(solution)/shard_map/ppermute | solution.py:95
  151.1 0.7 dynamic-slice_bitcast_fusion.1.slot
  151.8 6.7 %collective-permute-done.30.c = f32[2,2,128,128]{3,2,1,0:T(8,128)S(1)} collective-permute-done((f32[2,2,128,128]{3,2,1,0:T(8,128)S(1)}, f32[2,2,128,128]{3,2,1,0:T(8,128)S(1)}, u32[]{:S(2)}, u32[]{:S(2)}) %collective-permute-start.30) | collective-permute-done | bytes 262176 | tf_op jit(solution)/shard_map/ppermute | solution.py:95
  158.5 1.8 %collective-permute-done.31.d = f32[2,2,128,128]{3,2,1,0:T(8,128)S(1)} collective-permute-done((f32[2,2,128,128]{3,2,1,0:T(8,128)S(1)}, f32[2,2,128,128]{3,2,1,0:T(8,128)S(1)}, u32[]{:S(2)}, u32[]{:S(2)}) %collective-permute-start.31) | collective-permute-done | bytes 262176 | tf_op jit(solution)/shard_map/ppermute | solution.py:95
  160.3 2.2 %unpack.1 = f32[128,2,1024]{2,1,0:T(2,128)} custom-call(s32[4]{0:T(128)S(1)} %dynamic-slice_bitcast_fusion.1.slot, f32[2,2,128,128]{3,2,1,0:T(8,128)S(1)} %collective-permute-done.28.a, f32[2,2,128,128]{3,2,1,0:T(8,128)S(1)} %collective-permute-done.29.b, f32[2,2,128,128]{3,2,1,0:T(8,128)S(1)} %collective-permute-done.30.c, ...), custom_call_target="tpu_custom_call" | custom-call | flops 262144 | tf_op jit(solution)/shard_map/unpack/pallas_call | solution.py:101
  (51 shorter events, 3.3 us)
Async XLA Ops:
  0.0 3.9 %copy-start = (bf16[1536,1024]{1,0:T(8,128)(2,1)S(1)}, bf16[1536,1024]{1,0:T(8,128)(2,1)}, u32[]{:S(2)}) copy-start(bf16[1536,1024]{1,0:T(8,128)(2,1)} %own) | copy-start | bytes 9437188
  0.0 5.5 %copy-start.4 = (f32[2]{0:T(128)S(1)}, f32[2]{0:T(128)}, u32[]{:S(2)}) copy-start(f32[2]{0:T(128)} %param.7) | copy-start | bytes 28
  0.0 5.5 %copy-start.3 = (f32[1536]{0:T(1024)S(1)}, f32[1536]{0:T(1024)}, u32[]{:S(2)}) copy-start(f32[1536]{0:T(1024)} %param.6) | copy-start | bytes 18436
  3.9 20.3 %collective-permute-start.3 = (bf16[1536,1024]{1,0:T(8,128)(2,1)S(1)}, bf16[1536,1024]{1,0:T(8,128)(2,1)}, u32[]{:S(2)}, u32[]{:S(2)}) collective-permute-start(bf16[1536,1024]{1,0:T(8,128)(2,1)S(1)} %copy-done), channel_id=1, source_target_pairs={{1,0},{0,1},{3,2},{2,3},{5,4},{4,5},{7,6},{6,7},{9,8},{8,9},{11,10... | collective-permute-start | bytes 9437192 | tf_op jit(solution)/shard_map/ppermute | solution.py:95
  4.6 37.9 %collective-permute-start.7 = (bf16[1536,512]{1,0:T(8,128)(2,1)}, bf16[1536,512]{1,0:T(8,128)(2,1)}, u32[]{:S(2)}, u32[]{:S(2)}) collective-permute-start(bf16[1536,512]{1,0:T(8,128)(2,1)} %get-tuple-element.78), channel_id=1, source_target_pairs={{2,0},{3,1},{1,2},{0,3},{6,4},{7,5},{5,6},{4,7},{10,8},{11,9},{9,1... | collective-permute-start | bytes 4718600 | tf_op jit(solution)/shard_map/ppermute | solution.py:95
  7.0 1.1 copy-start.1
  17.9 13.2 %collective-permute-start.1 = (bf16[4,6,128,128]{3,2,1,0:T(8,128)(2,1)S(1)}, bf16[4,6,128,128]{3,2,1,0:T(8,128)(2,1)S(1)}, u32[]{:S(2)}, u32[]{:S(2)}) collective-permute-start(bf16[4,6,128,128]{3,2,1,0:T(8,128)(2,1)S(1)} %get-tuple-element.64), channel_id=1, source_target_pairs={{0,8},{1,33},{2,10},{3,35},{4,12},{5,37},{6,14},{7,39},{8,0},{9,41... | collective-permute-start | bytes 2359304 | tf_op jit(solution)/shard_map/ppermute | solution.py:95
  21.6 17.8 %collective-permute-start = (bf16[4,6,128,128]{3,2,1,0:T(8,128)(2,1)S(1)}, bf16[4,6,128,128]{3,2,1,0:T(8,128)(2,1)S(1)}, u32[]{:S(2)}, u32[]{:S(2)}) collective-permute-start(bf16[4,6,128,128]{3,2,1,0:T(8,128)(2,1)S(1)} %get-tuple-element.63), channel_id=1, source_target_pairs={{0,4},{1,17},{2,6},{3,19},{4,8},{5,21},{6,10},{7,23},{8,12},{9,25}... | collective-permute-start | bytes 2359304 | tf_op jit(solution)/shard_map/ppermute | solution.py:95
  22.3 19.0 %collective-permute-start.2 = (bf16[4,6,128,128]{3,2,1,0:T(8,128)(2,1)S(1)}, bf16[4,6,128,128]{3,2,1,0:T(8,128)(2,1)S(1)}, u32[]{:S(2)}, u32[]{:S(2)}) collective-permute-start(bf16[4,6,128,128]{3,2,1,0:T(8,128)(2,1)S(1)} %get-tuple-element.65), channel_id=1, source_target_pairs={{0,12},{1,49},{2,14},{3,51},{4,0},{5,53},{6,2},{7,55},{8,4},{9,57}... | collective-permute-start | bytes 2359304 | tf_op jit(solution)/shard_map/ppermute | solution.py:95
  24.2 18.3 %copy-start.2 = (bf16[1536,512]{1,0:T(8,128)(2,1)S(1)}, bf16[1536,512]{1,0:T(8,128)(2,1)}, u32[]{:S(2)}) copy-start(bf16[1536,512]{1,0:T(8,128)(2,1)} %get-tuple-element.101) | copy-start | bytes 4718596
  31.0 17.7 %collective-permute-start.5 = (bf16[4,4,128,128]{3,2,1,0:T(8,128)(2,1)S(1)}, bf16[4,4,128,128]{3,2,1,0:T(8,128)(2,1)S(1)}, u32[]{:S(2)}, u32[]{:S(2)}) collective-permute-start(bf16[4,4,128,128]{3,2,1,0:T(8,128)(2,1)S(1)} %get-tuple-element.72), channel_id=1, source_target_pairs={{0,8},{1,33},{2,10},{3,35},{4,12},{5,37},{6,14},{7,39},{8,0},{9,41... | collective-permute-start | bytes 1572872 | tf_op jit(solution)/shard_map/ppermute | solution.py:95
  39.4 13.1 %collective-permute-start.4 = (bf16[4,4,128,128]{3,2,1,0:T(8,128)(2,1)S(1)}, bf16[4,4,128,128]{3,2,1,0:T(8,128)(2,1)S(1)}, u32[]{:S(2)}, u32[]{:S(2)}) collective-permute-start(bf16[4,4,128,128]{3,2,1,0:T(8,128)(2,1)S(1)} %get-tuple-element.70), channel_id=1, source_target_pairs={{0,4},{1,17},{2,6},{3,19},{4,8},{5,21},{6,10},{7,23},{8,12},{9,25}... | collective-permute-start | bytes 1572872 | tf_op jit(solution)/shard_map/ppermute | solution.py:95
  41.3 11.9 %collective-permute-start.6 = (bf16[4,4,128,128]{3,2,1,0:T(8,128)(2,1)S(1)}, bf16[4,4,128,128]{3,2,1,0:T(8,128)(2,1)S(1)}, u32[]{:S(2)}, u32[]{:S(2)}) collective-permute-start(bf16[4,4,128,128]{3,2,1,0:T(8,128)(2,1)S(1)} %get-tuple-element.74), channel_id=1, source_target_pairs={{0,12},{1,49},{2,14},{3,51},{4,0},{5,53},{6,2},{7,55},{8,4},{9,57}... | collective-permute-start | bytes 1572872 | tf_op jit(solution)/shard_map/ppermute | solution.py:95
  42.5 43.3 %collective-permute-start.20 = (bf16[1536,512]{1,0:T(8,128)(2,1)S(1)}, bf16[1536,512]{1,0:T(8,128)(2,1)S(1)}, u32[]{:S(2)}, u32[]{:S(2)}) collective-permute-start(bf16[1536,512]{1,0:T(8,128)(2,1)S(1)} %copy-done.2), channel_id=1, source_target_pairs={{2,0},{3,1},{1,2},{0,3},{6,4},{7,5},{5,6},{4,7},{10,8},{11,9},{9,1... | collective-permute-start | bytes 4718600 | tf_op jit(solution)/shard_map/ppermute | solution.py:95
  48.7 10.4 %collective-permute-start.10 = (bf16[4,4,128,128]{3,2,1,0:T(8,128)(2,1)S(1)}, bf16[4,4,128,128]{3,2,1,0:T(8,128)(2,1)S(1)}, u32[]{:S(2)}, u32[]{:S(2)}) collective-permute-start(bf16[4,4,128,128]{3,2,1,0:T(8,128)(2,1)S(1)} %get-tuple-element.85), channel_id=1, source_target_pairs={{0,8},{1,33},{2,10},{3,35},{4,12},{5,37},{6,14},{7,39},{8,0},{9,41... | collective-permute-start | bytes 1572872 | tf_op jit(solution)/shard_map/ppermute | solution.py:95
  52.4 12.2 %collective-permute-start.8 = (bf16[4,4,128,128]{3,2,1,0:T(8,128)(2,1)S(1)}, bf16[4,4,128,128]{3,2,1,0:T(8,128)(2,1)S(1)}, u32[]{:S(2)}, u32[]{:S(2)}) collective-permute-start(bf16[4,4,128,128]{3,2,1,0:T(8,128)(2,1)S(1)} %get-tuple-element.80), channel_id=1, source_target_pairs={{0,4},{1,17},{2,6},{3,19},{4,8},{5,21},{6,10},{7,23},{8,12},{9,25}... | collective-permute-start | bytes 1572872 | tf_op jit(solution)/shard_map/ppermute | solution.py:95
  53.2 14.7 %collective-permute-start.12 = (bf16[4,4,128,128]{3,2,1,0:T(8,128)(2,1)S(1)}, bf16[4,4,128,128]{3,2,1,0:T(8,128)(2,1)S(1)}, u32[]{:S(2)}, u32[]{:S(2)}) collective-permute-start(bf16[4,4,128,128]{3,2,1,0:T(8,128)(2,1)S(1)} %get-tuple-element.90), channel_id=1, source_target_pairs={{0,12},{1,49},{2,14},{3,51},{4,0},{5,53},{6,2},{7,55},{8,4},{9,57}... | collective-permute-start | bytes 1572872 | tf_op jit(solution)/shard_map/ppermute | solution.py:95
  64.6 9.7 %collective-permute-start.9 = (f32[10,128,128]{2,1,0:T(8,128)S(1)}, f32[10,128,128]{2,1,0:T(8,128)S(1)}, u32[]{:S(2)}, u32[]{:S(2)}) collective-permute-start(f32[10,128,128]{2,1,0:T(8,128)S(1)} %pad_maximum_fusion), channel_id=1, source_target_pairs={{0,16},{1,5},{2,18},{3,7},{4,20},{5,9},{6,22},{7,11},{8,24},{9,13}... | collective-permute-start | bytes 1966088 | tf_op jit(solution)/shard_map/ppermute | solution.py:95
  65.0 11.3 %collective-permute-start.11 = (f32[10,128,128]{2,1,0:T(8,128)S(1)}, f32[10,128,128]{2,1,0:T(8,128)S(1)}, u32[]{:S(2)}, u32[]{:S(2)}) collective-permute-start(f32[10,128,128]{2,1,0:T(8,128)S(1)} %pad_maximum_fusion.1), channel_id=1, source_target_pairs={{0,32},{1,9},{2,34},{3,11},{4,36},{5,13},{6,38},{7,15},{8,40},{9,1... | collective-permute-start | bytes 1966088 | tf_op jit(solution)/shard_map/ppermute | solution.py:95
  67.9 17.9 %collective-permute-start.13 = (f32[10,128,128]{2,1,0:T(8,128)S(1)}, f32[10,128,128]{2,1,0:T(8,128)S(1)}, u32[]{:S(2)}, u32[]{:S(2)}) collective-permute-start(f32[10,128,128]{2,1,0:T(8,128)S(1)} %pad_maximum_fusion.2), channel_id=1, source_target_pairs={{0,48},{1,13},{2,50},{3,15},{4,52},{5,1},{6,54},{7,3},{8,56},{9,5}... | collective-permute-start | bytes 1966088 | tf_op jit(solution)/shard_map/ppermute | solution.py:95
  74.3 16.6 %collective-permute-start.16 = (f32[4,128,128]{2,1,0:T(8,128)S(1)}, f32[4,128,128]{2,1,0:T(8,128)S(1)}, u32[]{:S(2)}, u32[]{:S(2)}) collective-permute-start(f32[4,128,128]{2,1,0:T(8,128)S(1)} %get-tuple-element.95), channel_id=1, source_target_pairs={{0,16},{1,5},{2,18},{3,7},{4,20},{5,9},{6,22},{7,11},{8,24},{9,13}... | collective-permute-start | bytes 786440 | tf_op jit(solution)/shard_map/ppermute | solution.py:95
  76.2 16.2 %collective-permute-start.17 = (f32[4,128,128]{2,1,0:T(8,128)S(1)}, f32[4,128,128]{2,1,0:T(8,128)S(1)}, u32[]{:S(2)}, u32[]{:S(2)}) collective-permute-start(f32[4,128,128]{2,1,0:T(8,128)S(1)} %get-tuple-element.97), channel_id=1, source_target_pairs={{0,32},{1,9},{2,34},{3,11},{4,36},{5,13},{6,38},{7,15},{8,40},{9,1... | collective-permute-start | bytes 786440 | tf_op jit(solution)/shard_map/ppermute | solution.py:95
  85.8 8.0 %collective-permute-start.18 = (f32[4,128,128]{2,1,0:T(8,128)S(1)}, f32[4,128,128]{2,1,0:T(8,128)S(1)}, u32[]{:S(2)}, u32[]{:S(2)}) collective-permute-start(f32[4,128,128]{2,1,0:T(8,128)S(1)} %get-tuple-element.99), channel_id=1, source_target_pairs={{0,48},{1,13},{2,50},{3,15},{4,52},{5,1},{6,54},{7,3},{8,56},{9,5}... | collective-permute-start | bytes 786440 | tf_op jit(solution)/shard_map/ppermute | solution.py:95
  90.9 9.3 %collective-permute-start.21 = (bf16[4,4,128,128]{3,2,1,0:T(8,128)(2,1)S(1)}, bf16[4,4,128,128]{3,2,1,0:T(8,128)(2,1)S(1)}, u32[]{:S(2)}, u32[]{:S(2)}) collective-permute-start(bf16[4,4,128,128]{3,2,1,0:T(8,128)(2,1)S(1)} %get-tuple-element.104), channel_id=1, source_target_pairs={{0,4},{1,17},{2,6},{3,19},{4,8},{5,21},{6,10},{7,23},{8,12},{9,25}... | collective-permute-start | bytes 1572872 | tf_op jit(solution)/shard_map/ppermute | solution.py:95
  92.5 13.4 %collective-permute-start.22 = (bf16[4,4,128,128]{3,2,1,0:T(8,128)(2,1)S(1)}, bf16[4,4,128,128]{3,2,1,0:T(8,128)(2,1)S(1)}, u32[]{:S(2)}, u32[]{:S(2)}) collective-permute-start(bf16[4,4,128,128]{3,2,1,0:T(8,128)(2,1)S(1)} %get-tuple-element.106), channel_id=1, source_target_pairs={{0,8},{1,33},{2,10},{3,35},{4,12},{5,37},{6,14},{7,39},{8,0},{9,41... | collective-permute-start | bytes 1572872 | tf_op jit(solution)/shard_map/ppermute | solution.py:95
  93.7 13.0 %collective-permute-start.23 = (bf16[4,4,128,128]{3,2,1,0:T(8,128)(2,1)S(1)}, bf16[4,4,128,128]{3,2,1,0:T(8,128)(2,1)S(1)}, u32[]{:S(2)}, u32[]{:S(2)}) collective-permute-start(bf16[4,4,128,128]{3,2,1,0:T(8,128)(2,1)S(1)} %get-tuple-element.108), channel_id=1, source_target_pairs={{0,12},{1,49},{2,14},{3,51},{4,0},{5,53},{6,2},{7,55},{8,4},{9,57}... | collective-permute-start | bytes 1572872 | tf_op jit(solution)/shard_map/ppermute | solution.py:95
  95.9 16.9 %collective-permute-start.14 = (f32[10,128,128]{2,1,0:T(8,128)S(1)}, f32[10,128,128]{2,1,0:T(8,128)S(1)}, u32[]{:S(2)}, u32[]{:S(2)}) collective-permute-start(f32[10,128,128]{2,1,0:T(8,128)S(1)} %fusion.1), channel_id=1, source_target_pairs={{2,66},{3,67},{6,70},{7,71},{10,74},{11,75},{14,78},{15,79},{18,82... | collective-permute-start | bytes 1966088 | tf_op jit(solution)/shard_map/ppermute | solution.py:95
  107.0 11.3 %collective-permute-start.24 = (f32[4,128,128]{2,1,0:T(8,128)S(1)}, f32[4,128,128]{2,1,0:T(8,128)S(1)}, u32[]{:S(2)}, u32[]{:S(2)}) collective-permute-start(f32[4,128,128]{2,1,0:T(8,128)S(1)} %get-tuple-element.110), channel_id=1, source_target_pairs={{0,16},{1,5},{2,18},{3,7},{4,20},{5,9},{6,22},{7,11},{8,24},{9,13}... | collective-permute-start | bytes 786440 | tf_op jit(solution)/shard_map/ppermute | solution.py:95
  108.5 9.8 %collective-permute-start.25 = (f32[4,128,128]{2,1,0:T(8,128)S(1)}, f32[4,128,128]{2,1,0:T(8,128)S(1)}, u32[]{:S(2)}, u32[]{:S(2)}) collective-permute-start(f32[4,128,128]{2,1,0:T(8,128)S(1)} %get-tuple-element.111), channel_id=1, source_target_pairs={{0,32},{1,9},{2,34},{3,11},{4,36},{5,13},{6,38},{7,15},{8,40},{9,1... | collective-permute-start | bytes 786440 | tf_op jit(solution)/shard_map/ppermute | solution.py:95
  111.4 7.0 %collective-permute-start.26 = (f32[4,128,128]{2,1,0:T(8,128)S(1)}, f32[4,128,128]{2,1,0:T(8,128)S(1)}, u32[]{:S(2)}, u32[]{:S(2)}) collective-permute-start(f32[4,128,128]{2,1,0:T(8,128)S(1)} %get-tuple-element.112), channel_id=1, source_target_pairs={{0,48},{1,13},{2,50},{3,15},{4,52},{5,1},{6,54},{7,3},{8,56},{9,5}... | collective-permute-start | bytes 786440 | tf_op jit(solution)/shard_map/ppermute | solution.py:95
  111.5 9.0 %collective-permute-start.19 = (f32[4,128,128]{2,1,0:T(8,128)S(1)}, f32[4,128,128]{2,1,0:T(8,128)S(1)}, u32[]{:S(2)}, u32[]{:S(2)}) collective-permute-start(f32[4,128,128]{2,1,0:T(8,128)S(1)} %add_add_fusion.1.far0), channel_id=1, source_target_pairs={{0,64},{1,65},{4,68},{5,69},{8,72},{9,73},{12,76},{13,77},{16,80},... | collective-permute-start | bytes 786440 | tf_op jit(solution)/shard_map/ppermute | solution.py:95
  112.9 7.6 %collective-permute-start.15 = (f32[4,128,128]{2,1,0:T(8,128)S(1)}, f32[4,128,128]{2,1,0:T(8,128)S(1)}, u32[]{:S(2)}, u32[]{:S(2)}) collective-permute-start(f32[4,128,128]{2,1,0:T(8,128)S(1)} %slice.12), channel_id=1, source_target_pairs={{1,0},{0,1},{3,2},{2,3},{5,4},{4,5},{7,6},{6,7},{9,8},{8,9},{11,10... | collective-permute-start | bytes 786440 | tf_op jit(solution)/shard_map/ppermute | solution.py:95
  118.4 10.2 %collective-permute-start.27 = (f32[4,128,128]{2,1,0:T(8,128)S(1)}, f32[4,128,128]{2,1,0:T(8,128)S(1)}, u32[]{:S(2)}, u32[]{:S(2)}) collective-permute-start(f32[4,128,128]{2,1,0:T(8,128)S(1)} %add_add_fusion.far1), channel_id=1, source_target_pairs={{0,64},{1,65},{4,68},{5,69},{8,72},{9,73},{12,76},{13,77},{16,80},... | collective-permute-start | bytes 786440 | tf_op jit(solution)/shard_map/ppermute | solution.py:95
  129.5 22.3 %collective-permute-start.28 = (f32[2,2,128,128]{3,2,1,0:T(8,128)S(1)}, f32[2,2,128,128]{3,2,1,0:T(8,128)S(1)}, u32[]{:S(2)}, u32[]{:S(2)}) collective-permute-start(f32[2,2,128,128]{3,2,1,0:T(8,128)S(1)} %get-tuple-element.113), channel_id=1, source_target_pairs={{16,0},{40,1},{92,2},{3,3},{52,4},{56,5},{80,6},{7,7},{24,8},{32,9... | collective-permute-start | bytes 786440 | tf_op jit(solution)/shard_map/ppermute | solution.py:95
  133.1 18.7 %collective-permute-start.29 = (f32[2,2,128,128]{3,2,1,0:T(8,128)S(1)}, f32[2,2,128,128]{3,2,1,0:T(8,128)S(1)}, u32[]{:S(2)}, u32[]{:S(2)}) collective-permute-start(f32[2,2,128,128]{3,2,1,0:T(8,128)S(1)} %get-tuple-element.114), channel_id=1, source_target_pairs={{0,0},{28,1},{64,2},{43,3},{20,4},{16,5},{68,6},{19,7},{56,8},{8,9... | collective-permute-start | bytes 786440 | tf_op jit(solution)/shard_map/ppermute | solution.py:95
  135.0 23.5 %collective-permute-start.30 = (f32[2,2,128,128]{3,2,1,0:T(8,128)S(1)}, f32[2,2,128,128]{3,2,1,0:T(8,128)S(1)}, u32[]{:S(2)}, u32[]{:S(2)}) collective-permute-start(f32[2,2,128,128]{3,2,1,0:T(8,128)S(1)} %get-tuple-element.115), channel_id=1, source_target_pairs={{32,0},{52,1},{116,2},{55,3},{36,4},{4,5},{108,6},{47,7},{40,8},{6... | collective-permute-start | bytes 786440 | tf_op jit(solution)/shard_map/ppermute | solution.py:95
  144.6 15.8 %collective-permute-start.31 = (f32[2,2,128,128]{3,2,1,0:T(8,128)S(1)}, f32[2,2,128,128]{3,2,1,0:T(8,128)S(1)}, u32[]{:S(2)}, u32[]{:S(2)}) collective-permute-start(f32[2,2,128,128]{3,2,1,0:T(8,128)S(1)} %get-tuple-element.116), channel_id=1, source_target_pairs={{48,0},{0,1},{104,2},{31,3},{4,4},{44,5},{120,6},{59,7},{8,8},{20,... | collective-permute-start | bytes 786440 | tf_op jit(solution)/shard_map/ppermute | solution.py:95

commit v3 on v2

v3 whole, which is shorter than its diff:
```python
import functools

import jax
import jax.numpy as jnp
import numpy as np
from jax import lax
from jax.experimental import pallas as pl
from jax.experimental.pallas import tpu as pltpu
from jax.sharding import PartitionSpec as P

AXES = ("blk", "grp")
FREQ = 2
T = 128
FAR = (2, 3, 1, 0)
VMEM = 8 * 1024 * 1024


def parts_of(d):
    x, z, y_hi, grp = (d >> 2) & 3, (d >> 4) & 3, d >> 6, d & 3
    return (y_hi, x, z, grp) if grp & 1 == 0 else (y_hi, z, x, grp)


def device(y_hi, s1, s2, grp):
    x, z = (s1, s2) if grp & 1 == 0 else (s2, s1)
    return (((y_hi * 4 + z) * 4 + x) << 2) + grp


def shift_perm(d1=0, d2=0, dy=0):
    pairs = []
    for d in range(128):
        y_hi, s1, s2, grp = parts_of(d)
        pairs.append((d, device(y_hi ^ dy, (s1 + d1) & 3, (s2 + d2) & 3, grp)))
    return pairs


def group_perm(source):
    return [(blk * 4 + source(grp), blk * 4 + grp) for blk in range(32) for grp in range(4)]


def block_of(core, s1, s2):
    skew = (s1 + s2) & 3
    return (s1, skew) if core == 0 else (skew, s2)


def messages(d):
    y_hi, s1, s2, g = parts_of(d)
    s1, s2 = block_of(g & 1, s1, s2)
    row = lambda group, half, block, grp: (8 * group + 4 * half + block) * 4 + grp
    if y_hi == g >> 1:
        return [
            (row(g, 0, s1, g), s2),
            (row(g, 1, s2, g), s1),
            (row(g, 0, s2, g ^ 1), s1),
            (row(g, 1, s2, g ^ 1), s1),
        ]
    far = FAR[g]
    return [
        (row(far, 0, s1, g), s2),
        (row(far, 1, s1, g), s2),
        (row(g, 0, s2, far), s1),
        (row(g, 1, s2, far), s1),
    ]


@functools.cache
def rounds():
    left = [messages(d) for d in range(128)]
    todo = [set(range(4)) for _ in range(128)]
    perms, sent, filled = [], np.zeros((4, 128), np.int32), np.zeros((4, 128), np.int32)
    for k in range(4):
        taken = {}

        def place(d, seen):
            for m in sorted(todo[d]):
                to = left[d][m][0]
                if to in seen:
                    continue
                seen.add(to)
                if to not in taken or place(taken[to][0], seen):
                    taken[to] = (d, m)
                    return True
            return False

        for d in range(128):
            place(d, set())
        perms.append([(d, to) for to, (d, _) in sorted(taken.items())])
        for to, (d, m) in taken.items():
            todo[d].remove(m)
            sent[k, d] = m
            filled[k, to] = left[d][m][1]
    return perms, sent, filled


def permute(value, pairs):
    return lax.ppermute(value, AXES, pairs)


def call(kernel, out_shape, scalars, arrays, scratch=(), flops=0, name=None, aliases=()):
    vmem, smem = pl.BlockSpec(memory_space=pltpu.VMEM), pl.BlockSpec(memory_space=pltpu.SMEM)
    size = 0
    return pl.pallas_call(
        kernel,
        out_shape=out_shape,
        in_specs=[smem] * len(scalars) + [vmem] * len(arrays),
        out_specs=[vmem] * len(out_shape),
        scratch_shapes=list(scratch),
        input_output_aliases=dict(aliases),
        compiler_params=pltpu.CompilerParams(vmem_limit_bytes=VMEM),
        cost_estimate=pl.CostEstimate(flops=flops, bytes_accessed=size, transcendentals=0),
        name=name,
    )(*scalars, *arrays)


def floats(*shape):
    return jax.ShapeDtypeStruct(shape, jnp.float32)


def product(lhs, rhs):
    return lax.dot_general(lhs, rhs, (((0,), (0,)), ((), ())), preferred_element_type=jnp.float32)


def scatter_blocks(place, total, outs, n):
    for d in range(4):
        for e in range(4):
            s1, s2 = (place[0] + d) & 3, (place[1] + e) & 3
            skew = (s1 + s2) & 3
            rows = pl.ds(pl.multiple_of(jnp.where(place[3] == 0, s1, skew) * T, T), T)
            columns = pl.ds(pl.multiple_of(jnp.where(place[3] == 0, skew, s2) * T, T), T)
            outs[d][e, n] = total[rows, columns].astype(outs[d].dtype)


def block_shapes(count):
    return [jax.ShapeDtypeStruct((4, count, T, T), jnp.float32 if d == 0 else jnp.bfloat16) for d in range(4)]


def own_kernel(place, frequencies, own, gaps, scaled, *rest):
    outs, total = rest[:4], rest[4]
    gap = jnp.broadcast_to(gaps[...], (8, gaps.shape[1]))
    weights = [(4.0 * gap / (gap * gap + frequencies[f] * frequencies[f])).T[:, 0:1] for f in range(FREQ)]
    for h in range(2):
        for f in range(FREQ):
            part = 2 * f + h
            scaled[part] = (own[:, 512 * h : 512 * (h + 1)].astype(jnp.float32) * weights[f]).astype(jnp.bfloat16)
            total[...] = product(own[:, :512], scaled[part])
            scatter_blocks(place, total, outs, f * 3 + h)
            if h == 1:
                total[...] = product(own[:, 512:], scaled[part])
                scatter_blocks(place, total, outs, f * 3 + 2)


def own_products(place, frequencies, own, gaps):
    rows = own.shape[0]
    return call(
        own_kernel,
        [jax.ShapeDtypeStruct((4, rows, 512), jnp.bfloat16)] + block_shapes(10),
        [place, frequencies],
        [own, gaps.reshape(1, rows)],
        [pltpu.VMEM((512, 512), jnp.float32)],
        flops=2 * 6 * 512 * 512 * rows,
        name="own_products",
    )


def mate_kernel(place, other, scaled, *rest):
    outs, total = rest[4:8], rest[8]

    def step(t, _):
        columns = pl.ds(pl.multiple_of(t // 2 * 512, 512), 512)
        total[...] = product(other[:, columns], scaled[2 * place[3] + t % 2])
        scatter_blocks(place, total, outs, 6 + t)
        return 0

    lax.fori_loop(0, 4, step, 0)


def mate_products(place, other, scaled, blocks):
    return call(
        mate_kernel,
        block_shapes(10),
        [place],
        [other, scaled, *blocks],
        [pltpu.VMEM((512, 512), jnp.float32)],
        flops=2 * 4 * 512 * 512 * other.shape[0],
        name="mate_products",
        aliases={3 + d: d for d in range(4)},
    )


def far_kernel(place, other, scaled, *rest):
    outs, total = rest[:4], rest[4]

    def step(t, _):
        total[...] = product(other[...], scaled[t])
        scatter_blocks(place, total, outs, t)
        return 0

    lax.fori_loop(0, 4, step, 0)


def far_products(place, other, scaled):
    return call(
        far_kernel,
        block_shapes(4),
        [place],
        [other, scaled],
        [pltpu.VMEM((512, 512), jnp.float32)],
        flops=2 * 4 * 512 * 512 * other.shape[0],
        name="far_products",
    )


def seal(outs, largest):
    divisor = jnp.clip(jnp.broadcast_to(largest, (16, T)) * 2.0**5, 2.0**-17, 2.0**15)
    divisor = divisor.astype(jnp.bfloat16).astype(jnp.float32)
    factor = (2.0**19 / divisor)[0:1]
    for out in outs:
        for row in range(0, out.shape[0] - 16, T):
            out[row : row + T] = out[row : row + T] * factor
        out[out.shape[0] - 16 :] = divisor


def sealed(count):
    return floats(count * T + 16, T)


def opened(value, start, count):
    end = start + count * T
    return value[start:end].astype(jnp.float32) * (value[end : end + 1].astype(jnp.float32) * 2.0**-19)


def halved(values):
    return [v.astype(jnp.float16) for v in values]


def largest_of(values):
    peak = functools.reduce(jnp.maximum, [jnp.abs(v) for v in values])
    return jnp.max(jnp.max(peak, axis=0, keepdims=True), axis=1, keepdims=True)


def first_sum_kernel(kept, a, b, c, *outs):
    peak = jnp.zeros((T, T), jnp.float32)
    for e in range(4):
        for n in range(kept.shape[1]):
            value = kept[e, n] + (a[e, n].astype(jnp.float32) + b[e, n].astype(jnp.float32)) + c[e, n].astype(jnp.float32)
            outs[e][n * T : (n + 1) * T] = value
            if e > 0:
                peak = jnp.maximum(peak, jnp.abs(value))
    seal(outs[1:], largest_of([peak]))


def first_sum(kept, a, b, c):
    count = kept.shape[1]
    kept, *send = call(
        first_sum_kernel,
        [floats(count * T, T)] + [sealed(count)] * 3,
        [],
        [kept, a, b, c],
        flops=20 * count * T * T,
        name="first_sum",
    )
    return kept, halved(send)


def seal_kernel(value, out):
    peak = jnp.zeros((T, T), jnp.float32)
    for row in range(0, value.shape[0], T):
        out[row : row + T] = value[row : row + T]
        peak = jnp.maximum(peak, jnp.abs(value[row : row + T]))
    seal([out], largest_of([peak]))


def across(value, at_home):
    pairs = [(s, d) for s, d in shift_perm(dy=1) if ((d >> 6) == (d & 3) >> 1) == at_home]
    count = value.shape[0] // T
    send = call(seal_kernel, [sealed(count)], [], [value], flops=2 * count * T * T, name="seal")
    return value + opened(permute(halved(send)[0], pairs), 0, count)


def pack_kernel(place, near, twin, far, *rest):
    outs, ready = rest[:4], rest[4]
    at_home = place[4] == 1
    block = lambda part, n: part[n * T : (n + 1) * T]

    @pl.when(at_home)
    def _():
        core = place[3]
        for f in range(FREQ):
            low, both, high = (block(near, 3 * f + j) for j in range(3))
            ready[0, f, 0] = low
            ready[0, f, 1] = both
            ready[1, f, 0] = both.T
            ready[1, f, 1] = high.T
        for k in range(2):
            for h in range(2):
                ready[2 + k, core, h] = block(near, 6 + 2 * h + k).T
                ready[2 + k, 1 - core, h] = block(twin, 2 * k + h)

    @pl.when(jnp.logical_not(at_home))
    def _():
        for half in range(2):
            for f in range(FREQ):
                for h in range(2):
                    value = block(far, 4 * half + 2 * f + h)
                    ready[half, f, h] = value
                    ready[2 + h, f, half] = value.T

    peak = jnp.zeros((T, T), jnp.float32)
    for k in range(4):
        for f in range(FREQ):
            for h in range(2):
                value = ready[place[5 + k], f, h]
                row = (2 * f + h) * T
                outs[k][row : row + T] = value
                peak = jnp.maximum(peak, jnp.abs(value))
    seal(outs, largest_of([peak]))


def pack(place, *arrays):
    return halved(
        call(
            pack_kernel,
            [sealed(2 * FREQ)] * 4,
            [place],
            arrays,
            [pltpu.VMEM((4, FREQ, 2, T, T), jnp.float32)],
            flops=2**20,
            name="pack",
        )
    )


def unpack_kernel(place, a, b, c, d, out):
    for k, arrived in enumerate((a, b, c, d)):
        for f in range(FREQ):
            for h in range(2):
                out[:, f, pl.ds(pl.multiple_of(512 * h + place[9 + k] * T, T), T)] = arrived[(2 * f + h) * T : (2 * f + h + 1) * T]


def unpack(place, arrived):
    arrived = [opened(v, 0, 2 * FREQ) for v in arrived]
    return call(unpack_kernel, [floats(T, FREQ, 1024)], [place], arrived, flops=2**18, name="unpack")[0]


def after(value, earlier):
    return value if earlier is None else lax.optimization_barrier((value, earlier))[0]


def send_first(send, earlier):
    return [permute(after(v, w), shift_perm(d1=d + 1)) for d, (v, w) in enumerate(zip(send, earlier))]


def send_second(send, earlier):
    return [permute(after(v, w), shift_perm(d2=e + 1)) for e, (v, w) in enumerate(zip(send, earlier))]


def on_device(own, energy_gaps, frequencies):
    blk, grp = lax.axis_index("blk"), lax.axis_index("grp")
    x, z, y_hi, core = blk & 3, (blk >> 2) & 3, blk >> 4, grp & 1
    perms, sent, filled = rounds()
    tables = lax.dynamic_index_in_dim(jnp.asarray(np.concatenate([sent, filled]).T), blk * 4 + grp, 0, keepdims=False)
    home = jnp.where(y_hi == grp >> 1, 1, 0)
    here = jnp.stack([jnp.where(core == 0, x, z), jnp.where(core == 0, z, x), y_hi, core, home]).astype(jnp.int32)
    place = jnp.concatenate([here, tables])

    swap, far_perm = group_perm(lambda g: g ^ 1), group_perm(lambda g: FAR[g])
    low = own[:, :512]
    own, low = lax.optimization_barrier((own, low))
    other = permute(own, swap)
    far0 = permute(low, far_perm)

    scaled, *blocks = own_products(here, frequencies, own, energy_gaps)
    near, *send = mate_products(place, other, scaled, blocks)
    high = after(own, near)[:, 512:]
    far1 = permute(after(high, far0), far_perm)
    near_sent = send_first(send, [None, None, None])
    sum0, *send = far_products(place, far0, scaled)
    sum0_sent = send_first(send, near_sent)
    near, send = first_sum(near, *near_sent)
    near_sent = send_second(send, [sum0_sent[0], sum0_sent[1], sum0_sent[2]])
    sum0, send0 = first_sum(sum0, *sum0_sent)
    sum1, *send = far_products(place, far1, scaled)
    sum1_sent = send_first(send, near_sent)
    sum1, send1 = first_sum(sum1, *sum1_sent)
    for v in near_sent:
        near = near + opened(v, 0, 10)
    near = across(after(near, sum1_sent[2]), True)
    twin = permute(near[6 * T :], swap)
    for v in send_second([jnp.concatenate(v) for v in zip(send0, send1)], [None]*3):
        sum0 = sum0 + opened(v, 0, 4)
        sum1 = sum1 + opened(v, 4 * T + 16, 4)
    far = across(jnp.concatenate([sum0, sum1]), False)
    packed = pack(place, near, twin, far)
    return unpack(place, [permute(v, p) for v, p in zip(packed, perms)])


def solution(mesh):
    in_specs = (P("blk", "grp"), P("blk"), P())
    out_specs = P("blk", None, "grp")
    return jax.shard_map(
        on_device, mesh=mesh, in_specs=in_specs, out_specs=out_specs, check_vma=False
    )
```

time: 163 us -> 149 us (0.914)
  the two profiles are of different devices: /device:TPU:19 before, /device:TPU:1 now
where the time goes in v3:
time: 149 us; the launch traced here: 147 us
  waiting for transfers between devices  63.3 us (42%)
  starting transfers between devices  48.1 us (32%)
  Pallas kernels  30.3 us (20%)
  local copies, waits for them, and re-layouts  3.87 us (3%)
    ppermute x25, waiting for transfers between devices, permute(): return lax.ppermute(value, AXES, pairs)  63.3 us
    ppermute x25, starting transfers between devices, permute(): return lax.ppermute(value, AXES, pairs)  48.1 us
    pallas_call x11, Pallas kernels, call(): pl.pallas_call(kernel, out_shape=out_shape, in_specs=[smem] * len(scalars...  30.3 us
  transfers between devices with their start and end apart: 25, of which 14 were waited for; matrix products, arithmetic and copies ran while one was open for 2% of the time, Pallas kernels for 18%

profile of v3, /device:TPU:1, one launch (start us, length us, event | category | flops | bytes accessed | tf_op | source)
XLA Modules:
  0.0 147.4 jit_solution(5880662855537122602)
XLA Ops:
  0.0 2.8 %slice.99 = bf16[1536,512]{1,0:T(8,128)(2,1)} slice(bf16[1536,1024]{1,0:T(8,128)(2,1)} %own), slice={[0:1536], [0:512]} | slice | bytes 3145728 | tf_op jit(solution)/shard_map/slice | solution.py:366
  2.8 1.4 collective-permute-start
  4.2 1.3 collective-permute-start.4
  5.6 0.7 dynamic-slice_bitcast_fusion
  6.4 7.5 %own_products.1 = (bf16[4,1536,512]{2,1,0:T(8,128)(2,1)S(1)}, f32[4,10,128,128]{3,2,1,0:T(8,128)S(1)}, bf16[4,10,128,128]{3,2,1,0:T(8,128)(2,1)S(1)}, bf16[4,10,...) custom-call(s32[5]{0:T(128)S(1)} %stack.23.place, f32[2]{0:T(128)S(1)} %copy-done.1, ...), custom_call_target="tpu_custom_call" | custom-call | flops 4831838208 | tf_op jit(solution)/shard_map/own_products/pallas_call | solution.py:101
  13.9 6.5 %mate_products.1 = (f32[4,10,128,128]{3,2,1,0:T(8,128)S(1)}, bf16[4,10,128,128]{3,2,1,0:T(8,128)(2,1)S(1)}, bf16[4,10,128,128]{3,2,1,0:T(8,128)(2,1)S(1)}, bf16[4,10,128,128]{3,2,1,0:T(8,128)(2,1)S(1)}) custom-call(s32[13]{0:T(128)S(1)} %concatenate.16.place, ...), custom_call_target="tpu_custom_call", output_to_operand_aliasing={{0}: (3, {}), {1}: (4, {}), {2}: (5, {}), {3}: (6, {})} | custom-call | flops 3221225472 | tf_op jit(solution)/shard_map/mate_products/pallas_call | solution.py:101
  20.4 3.8 %collective-permute-start.3 = (bf16[4,10,128,128]{3,2,1,0:T(8,128)(2,1)S(1)}, bf16[4,10,128,128]{3,2,1,0:T(8,128)(2,1)S(1)}, u32[]{:S(2)}, u32[]{:S(2)}) collective-permute-start(bf16[4,10,128,128]{3,2,1,0:T(8,128)(2,1)S(1)} %get-tuple-element.61), channel_id=1, source_target_pairs={{0,12},{1,49},{2,14},{3,51},{4,0},{5,53},{6,2},{7,55},{8,4},{9,57}... | collective-permute-start | bytes 3932168 | tf_op jit(solution)/shard_map/ppermute | solution.py:95
  24.2 0.7 collective-permute-start.1
  25.1 15.5 %collective-permute-done.4.other = bf16[1536,512]{1,0:T(8,128)(2,1)} collective-permute-done((bf16[1536,512]{1,0:T(8,128)(2,1)}, bf16[1536,512]{1,0:T(8,128)(2,1)}, u32[]{:S(2)}, u32[]{:S(2)}) %collective-permute-start.4) | collective-permute-done | bytes 1572896 | tf_op jit(solution)/shard_map/ppermute | solution.py:95
  40.6 1.3 collective-permute-start.11
  41.9 6.0 %far_products.2 = (f32[4,4,128,128]{3,2,1,0:T(8,128)S(1)}, bf16[4,4,128,128]{3,2,1,0:T(8,128)(2,1)S(1)}, bf16[4,4,128,128]{3,2,1,0:T(8,128)(2,1)S(1)}, bf16[4,4,128,128]{3,2,1,0:T(8,128)(2,1)S(1)}) custom-call(s32[13]{0:T(128)S(1)} %concatenate.16.place, bf16[1536,512]{1,0:T(8,128)(2,1)} %collective-permute-done.4.other, ...), custom_call_target="tpu_custom_call" | custom-call | flops 3221225472 | tf_op jit(solution)/shard_map/far_products/pallas_call | solution.py:101
  47.9 5.0 %collective-permute-done.3.c = bf16[4,10,128,128]{3,2,1,0:T(8,128)(2,1)S(1)} collective-permute-done((bf16[4,10,128,128]{3,2,1,0:T(8,128)(2,1)S(1)}, bf16[4,10,128,128]{3,2,1,0:T(8,128)(2,1)S(1)}, u32[]{:S(2)}, u32[]{:S(2)}) %collective-permute-start.3) | collective-permute-done | bytes 1310752 | tf_op jit(solution)/shard_map/ppermute | solution.py:95
  52.8 3.4 %collective-permute-start.9 = (bf16[4,4,128,128]{3,2,1,0:T(8,128)(2,1)S(1)}, bf16[4,4,128,128]{3,2,1,0:T(8,128)(2,1)S(1)}, u32[]{:S(2)}, u32[]{:S(2)}) collective-permute-start(bf16[4,4,128,128]{3,2,1,0:T(8,128)(2,1)S(1)} %get-tuple-element.74), channel_id=1, source_target_pairs={{0,12},{1,49},{2,14},{3,51},{4,0},{5,53},{6,2},{7,55},{8,4},{9,57}... | collective-permute-start | bytes 1572872 | tf_op jit(solution)/shard_map/ppermute | solution.py:95
  56.3 0.6 collective-permute-start.5
  56.8 0.9 first_sum.3
  57.8 10.2 %collective-permute-done.9.c = bf16[4,4,128,128]{3,2,1,0:T(8,128)(2,1)S(1)} collective-permute-done((bf16[4,4,128,128]{3,2,1,0:T(8,128)(2,1)S(1)}, bf16[4,4,128,128]{3,2,1,0:T(8,128)(2,1)S(1)}, u32[]{:S(2)}, u32[]{:S(2)}) %collective-permute-start.9) | collective-permute-done | bytes 524320 | tf_op jit(solution)/shard_map/ppermute | solution.py:95
  68.0 2.4 %collective-permute-start.10 = (f16[1296,128]{1,0:T(8,128)(2,1)S(1)}, f16[1296,128]{1,0:T(8,128)(2,1)S(1)}, u32[]{:S(2)}, u32[]{:S(2)}) collective-permute-start(f16[1296,128]{1,0:T(8,128)(2,1)S(1)} %convert_element_type.141), channel_id=1, source_target_pairs={{0,48},{1,13},{2,50},{3,15},{4,52},{5,1},{6,54},{7,3},{8,56},{9,5}... | collective-permute-start | bytes 995336 | tf_op jit(solution)/shard_map/ppermute | solution.py:95
  70.4 0.5 collective-permute-start.8
  70.9 0.7 collective-permute-done.5.a
  71.7 0.7 collective-permute-start.6
  72.4 3.5 %collective-permute-done.11.other = bf16[1536,512]{1,0:T(8,128)(2,1)S(1)} collective-permute-done((bf16[1536,512]{1,0:T(8,128)(2,1)S(1)}, bf16[1536,512]{1,0:T(8,128)(2,1)S(1)}, u32[]{:S(2)}, u32[]{:S(2)}) %collective-permute-start.11) | collective-permute-done | bytes 1572896 | tf_op jit(solution)/shard_map/ppermute | solution.py:95
  75.9 5.1 %far_products.3 = (f32[4,4,128,128]{3,2,1,0:T(8,128)S(1)}, bf16[4,4,128,128]{3,2,1,0:T(8,128)(2,1)S(1)}, bf16[4,4,128,128]{3,2,1,0:T(8,128)(2,1)S(1)}, bf16[4,4,128,128]{3,2,1,0:T(8,128)(2,1)S(1)}) custom-call(s32[13]{0:T(128)S(1)} %concatenate.16.place, bf16[1536,512]{1,0:T(8,128)(2,1)S(1)} %collective-permute-done.11.other, ...), custom_call_target="tpu_custom_call" | custom-call | flops 3221225472 | tf_op jit(solution)/shard_map/far_products/pallas_call | solution.py:101
  81.0 0.4 first_sum.4
  81.6 3.7 %collective-permute-start.12 = (bf16[4,4,128,128]{3,2,1,0:T(8,128)(2,1)S(1)}, bf16[4,4,128,128]{3,2,1,0:T(8,128)(2,1)S(1)}, u32[]{:S(2)}, u32[]{:S(2)}) collective-permute-start(bf16[4,4,128,128]{3,2,1,0:T(8,128)(2,1)S(1)} %get-tuple-element.79), channel_id=1, source_target_pairs={{0,12},{1,49},{2,14},{3,51},{4,0},{5,53},{6,2},{7,55},{8,4},{9,57}... | collective-permute-start | bytes 1572872 | tf_op jit(solution)/shard_map/ppermute | solution.py:95
  85.3 0.7 collective-permute-start.15
  86.0 0.2 multiply_add_fusion.1.value
  86.2 10.8 %collective-permute-done.12.c = bf16[4,4,128,128]{3,2,1,0:T(8,128)(2,1)S(1)} collective-permute-done((bf16[4,4,128,128]{3,2,1,0:T(8,128)(2,1)S(1)}, bf16[4,4,128,128]{3,2,1,0:T(8,128)(2,1)S(1)}, u32[]{:S(2)}, u32[]{:S(2)}) %collective-permute-start.12) | collective-permute-done | bytes 524320 | tf_op jit(solution)/shard_map/ppermute | solution.py:95
  97.0 3.5 %collective-permute-done.15.a = bf16[4,4,128,128]{3,2,1,0:T(8,128)(2,1)S(1)} collective-permute-done((bf16[4,4,128,128]{3,2,1,0:T(8,128)(2,1)S(1)}, bf16[4,4,128,128]{3,2,1,0:T(8,128)(2,1)S(1)}, u32[]{:S(2)}, u32[]{:S(2)}) %collective-permute-start.15) | collective-permute-done | bytes 524320 | tf_op jit(solution)/shard_map/ppermute | solution.py:95
  100.5 0.4 first_sum.5
  101.1 2.5 %collective-permute-start.19 = (f16[1056,128]{1,0:T(8,128)(2,1)S(1)}, f16[1056,128]{1,0:T(8,128)(2,1)S(1)}, u32[]{:S(2)}, u32[]{:S(2)}) collective-permute-start(f16[1056,128]{1,0:T(8,128)(2,1)S(1)} %pad_maximum_fusion.3), channel_id=1, source_target_pairs={{0,48},{1,13},{2,50},{3,15},{4,52},{5,1},{6,54},{7,3},{8,56},{9,5}... | collective-permute-start | bytes 811016 | tf_op jit(solution)/shard_map/ppermute | solution.py:95
  103.7 0.4 collective-permute-start.18
  104.2 0.5 collective-permute-start.17
  105.0 1.3 collective-permute-start.13
  106.3 3.6 %collective-permute-done.19 = f16[1056,128]{1,0:T(8,128)(2,1)S(1)} collective-permute-done((f16[1056,128]{1,0:T(8,128)(2,1)S(1)}, f16[1056,128]{1,0:T(8,128)(2,1)S(1)}, u32[]{:S(2)}, u32[]{:S(2)}) %collective-permute-start.19) | collective-permute-done | bytes 270368 | tf_op jit(solution)/shard_map/ppermute | solution.py:95
  109.9 0.8 collective-permute-done.18
  110.7 3.1 %collective-permute-done.17 = f16[1056,128]{1,0:T(8,128)(2,1)S(1)} collective-permute-done((f16[1056,128]{1,0:T(8,128)(2,1)S(1)}, f16[1056,128]{1,0:T(8,128)(2,1)S(1)}, u32[]{:S(2)}, u32[]{:S(2)}) %collective-permute-start.17) | collective-permute-done | bytes 270368 | tf_op jit(solution)/shard_map/ppermute | solution.py:95
  114.3 4.8 %collective-permute-start.20 = (f16[1040,128]{1,0:T(8,128)(2,1)S(1)}, f16[1040,128]{1,0:T(8,128)(2,1)S(1)}, u32[]{:S(2)}, u32[]{:S(2)}) collective-permute-start(f16[1040,128]{1,0:T(8,128)(2,1)S(1)} %convert_element_type.165), channel_id=1, source_target_pairs={{0,64},{1,65},{4,68},{5,69},{8,72},{9,73},{12,76},{13,77},{16,80},... | collective-permute-start | bytes 798728 | tf_op jit(solution)/shard_map/ppermute | solution.py:95
  119.2 4.9 %collective-permute-start.14 = (f32[512,128]{1,0:T(8,128)S(1)}, f32[512,128]{1,0:T(8,128)S(1)}, u32[]{:S(2)}, u32[]{:S(2)}) collective-permute-start(f32[512,128]{1,0:T(8,128)S(1)} %slice.140), channel_id=1, source_target_pairs={{1,0},{0,1},{3,2},{2,3},{5,4},{4,5},{7,6},{6,7},{9,8},{8,9},{11,10... | collective-permute-start | bytes 786440 | tf_op jit(solution)/shard_map/ppermute | solution.py:95
  124.1 1.1 collective-permute-done.14.twin
  125.2 1.0 pack.1
  126.3 4.4 %collective-permute-start.24 = (f16[528,128]{1,0:T(8,128)(2,1)S(1)}, f16[528,128]{1,0:T(8,128)(2,1)S(1)}, u32[]{:S(2)}, u32[]{:S(2)}) collective-permute-start(f16[528,128]{1,0:T(8,128)(2,1)S(1)} %convert_element_type.177), channel_id=1, source_target_pairs={{48,0},{0,1},{104,2},{31,3},{4,4},{44,5},{120,6},{59,7},{8,8},{20,... | collective-permute-start | bytes 405512 | tf_op jit(solution)/shard_map/ppermute | solution.py:95
  130.8 1.9 %collective-permute-start.23 = (f16[528,128]{1,0:T(8,128)(2,1)S(1)}, f16[528,128]{1,0:T(8,128)(2,1)S(1)}, u32[]{:S(2)}, u32[]{:S(2)}) collective-permute-start(f16[528,128]{1,0:T(8,128)(2,1)S(1)} %convert_element_type.174), channel_id=1, source_target_pairs={{32,0},{52,1},{116,2},{55,3},{36,4},{4,5},{108,6},{47,7},{40,8},{6... | collective-permute-start | bytes 405512 | tf_op jit(solution)/shard_map/ppermute | solution.py:95
  132.7 2.2 %collective-permute-start.22 = (f16[528,128]{1,0:T(8,128)(2,1)S(1)}, f16[528,128]{1,0:T(8,128)(2,1)S(1)}, u32[]{:S(2)}, u32[]{:S(2)}) collective-permute-start(f16[528,128]{1,0:T(8,128)(2,1)S(1)} %convert_element_type.171), channel_id=1, source_target_pairs={{0,0},{28,1},{64,2},{43,3},{20,4},{16,5},{68,6},{19,7},{56,8},{8,9... | collective-permute-start | bytes 405512 | tf_op jit(solution)/shard_map/ppermute | solution.py:95
  134.9 4.6 %collective-permute-start.21 = (f16[528,128]{1,0:T(8,128)(2,1)S(1)}, f16[528,128]{1,0:T(8,128)(2,1)S(1)}, u32[]{:S(2)}, u32[]{:S(2)}) collective-permute-start(f16[528,128]{1,0:T(8,128)(2,1)S(1)} %convert_element_type.168), channel_id=1, source_target_pairs={{16,0},{40,1},{92,2},{3,3},{52,4},{56,5},{80,6},{7,7},{24,8},{32,9... | collective-permute-start | bytes 405512 | tf_op jit(solution)/shard_map/ppermute | solution.py:95
  139.6 0.5 collective-permute-done.23
  140.1 1.1 collective-permute-done.22
  141.3 3.9 %collective-permute-done.21 = f16[528,128]{1,0:T(8,128)(2,1)S(1)} collective-permute-done((f16[528,128]{1,0:T(8,128)(2,1)S(1)}, f16[528,128]{1,0:T(8,128)(2,1)S(1)}, u32[]{:S(2)}, u32[]{:S(2)}) %collective-permute-start.21) | collective-permute-done | bytes 135200 | tf_op jit(solution)/shard_map/ppermute | solution.py:95
  145.2 2.2 %unpack.1 = f32[128,2,1024]{2,1,0:T(2,128)} custom-call(s32[13]{0:T(128)S(1)} %concatenate.16.place, f32[512,128]{1,0:T(8,128)S(1)} %convert_multiply_fusion.3.a, f32[512,128]{1,0:T(8,128)S(1)} %convert_multiply_fusion.2.b, f32[512,128]{1,0:T(8,128)S(1)} %convert_multiply_fusion.1.c, f32[512,128]{1,0:T(8,128)S(1)} %convert_multiply_fusion.d), custom_call_target="tpu_custom_call" | custom-call | flops 262144 | tf_op jit(solution)/shard_map/unpack/pallas_call | solution.py:101
  (65 shorter events, 1.9 us)
Async XLA Ops:
  0.0 2.8 %copy-start = (bf16[1536,1024]{1,0:T(8,128)(2,1)S(1)}, bf16[1536,1024]{1,0:T(8,128)(2,1)}, u32[]{:S(2)}) copy-start(bf16[1536,1024]{1,0:T(8,128)(2,1)} %own) | copy-start | bytes 9437188
  0.0 6.4 %copy-start.2 = (f32[1536]{0:T(1024)S(1)}, f32[1536]{0:T(1024)}, u32[]{:S(2)}) copy-start(f32[1536]{0:T(1024)} %param.5) | copy-start | bytes 18436
  0.0 6.4 %copy-start.1 = (f32[2]{0:T(128)S(1)}, f32[2]{0:T(128)}, u32[]{:S(2)}) copy-start(f32[2]{0:T(128)} %frequencies.1) | copy-start | bytes 28
  2.8 11.0 %collective-permute-start = (bf16[1536,1024]{1,0:T(8,128)(2,1)S(1)}, bf16[1536,1024]{1,0:T(8,128)(2,1)}, u32[]{:S(2)}, u32[]{:S(2)}) collective-permute-start(bf16[1536,1024]{1,0:T(8,128)(2,1)S(1)} %copy-done), channel_id=1, source_target_pairs={{1,0},{0,1},{3,2},{2,3},{5,4},{4,5},{7,6},{6,7},{9,8},{8,9},{11,10... | collective-permute-start | bytes 9437192 | tf_op jit(solution)/shard_map/ppermute | solution.py:95
  4.2 36.3 %collective-permute-start.4 = (bf16[1536,512]{1,0:T(8,128)(2,1)}, bf16[1536,512]{1,0:T(8,128)(2,1)}, u32[]{:S(2)}, u32[]{:S(2)}) collective-permute-start(bf16[1536,512]{1,0:T(8,128)(2,1)} %slice.99), channel_id=1, source_target_pairs={{2,0},{3,1},{1,2},{0,3},{6,4},{7,5},{5,6},{4,7},{10,8},{11,9},{9,1... | collective-permute-start | bytes 4718600 | tf_op jit(solution)/shard_map/ppermute | solution.py:95
  20.4 32.4 %collective-permute-start.3 = (bf16[4,10,128,128]{3,2,1,0:T(8,128)(2,1)S(1)}, bf16[4,10,128,128]{3,2,1,0:T(8,128)(2,1)S(1)}, u32[]{:S(2)}, u32[]{:S(2)}) collective-permute-start(bf16[4,10,128,128]{3,2,1,0:T(8,128)(2,1)S(1)} %get-tuple-element.61), channel_id=1, source_target_pairs={{0,12},{1,49},{2,14},{3,51},{4,0},{5,53},{6,2},{7,55},{8,4},{9,57}... | collective-permute-start | bytes 3932168 | tf_op jit(solution)/shard_map/ppermute | solution.py:95
  24.2 32.0 %collective-permute-start.2 = (bf16[4,10,128,128]{3,2,1,0:T(8,128)(2,1)S(1)}, bf16[4,10,128,128]{3,2,1,0:T(8,128)(2,1)S(1)}, u32[]{:S(2)}, u32[]{:S(2)}) collective-permute-start(bf16[4,10,128,128]{3,2,1,0:T(8,128)(2,1)S(1)} %get-tuple-element.60), channel_id=1, source_target_pairs={{0,8},{1,33},{2,10},{3,35},{4,12},{5,37},{6,14},{7,39},{8,0},{9,41... | collective-permute-start | bytes 3932168 | tf_op jit(solution)/shard_map/ppermute | solution.py:95
  24.2 32.0 %collective-permute-start.1 = (bf16[4,10,128,128]{3,2,1,0:T(8,128)(2,1)S(1)}, bf16[4,10,128,128]{3,2,1,0:T(8,128)(2,1)S(1)}, u32[]{:S(2)}, u32[]{:S(2)}) collective-permute-start(bf16[4,10,128,128]{3,2,1,0:T(8,128)(2,1)S(1)} %get-tuple-element.59), channel_id=1, source_target_pairs={{0,4},{1,17},{2,6},{3,19},{4,8},{5,21},{6,10},{7,23},{8,12},{9,25}... | collective-permute-start | bytes 3932168 | tf_op jit(solution)/shard_map/ppermute | solution.py:95
  40.6 35.3 %collective-permute-start.11 = (bf16[1536,512]{1,0:T(8,128)(2,1)S(1)}, bf16[1536,512]{1,0:T(8,128)(2,1)S(1)}, u32[]{:S(2)}, u32[]{:S(2)}) collective-permute-start(bf16[1536,512]{1,0:T(8,128)(2,1)S(1)} %slice.106), channel_id=1, source_target_pairs={{2,0},{3,1},{1,2},{0,3},{6,4},{7,5},{5,6},{4,7},{10,8},{11,9},{9,1... | collective-permute-start | bytes 4718600 | tf_op jit(solution)/shard_map/ppermute | solution.py:95
  52.8 15.2 %collective-permute-start.9 = (bf16[4,4,128,128]{3,2,1,0:T(8,128)(2,1)S(1)}, bf16[4,4,128,128]{3,2,1,0:T(8,128)(2,1)S(1)}, u32[]{:S(2)}, u32[]{:S(2)}) collective-permute-start(bf16[4,4,128,128]{3,2,1,0:T(8,128)(2,1)S(1)} %get-tuple-element.74), channel_id=1, source_target_pairs={{0,12},{1,49},{2,14},{3,51},{4,0},{5,53},{6,2},{7,55},{8,4},{9,57}... | collective-permute-start | bytes 1572872 | tf_op jit(solution)/shard_map/ppermute | solution.py:95
  56.3 14.2 %collective-permute-start.7 = (bf16[4,4,128,128]{3,2,1,0:T(8,128)(2,1)S(1)}, bf16[4,4,128,128]{3,2,1,0:T(8,128)(2,1)S(1)}, u32[]{:S(2)}, u32[]{:S(2)}) collective-permute-start(bf16[4,4,128,128]{3,2,1,0:T(8,128)(2,1)S(1)} %get-tuple-element.70), channel_id=1, source_target_pairs={{0,8},{1,33},{2,10},{3,35},{4,12},{5,37},{6,14},{7,39},{8,0},{9,41... | collective-permute-start | bytes 1572872 | tf_op jit(solution)/shard_map/ppermute | solution.py:95
  56.3 15.4 %collective-permute-start.5 = (bf16[4,4,128,128]{3,2,1,0:T(8,128)(2,1)S(1)}, bf16[4,4,128,128]{3,2,1,0:T(8,128)(2,1)S(1)}, u32[]{:S(2)}, u32[]{:S(2)}) collective-permute-start(bf16[4,4,128,128]{3,2,1,0:T(8,128)(2,1)S(1)} %get-tuple-element.66), channel_id=1, source_target_pairs={{0,4},{1,17},{2,6},{3,19},{4,8},{5,21},{6,10},{7,23},{8,12},{9,25}... | collective-permute-start | bytes 1572872 | tf_op jit(solution)/shard_map/ppermute | solution.py:95
  68.0 13.6 %collective-permute-start.10 = (f16[1296,128]{1,0:T(8,128)(2,1)S(1)}, f16[1296,128]{1,0:T(8,128)(2,1)S(1)}, u32[]{:S(2)}, u32[]{:S(2)}) collective-permute-start(f16[1296,128]{1,0:T(8,128)(2,1)S(1)} %convert_element_type.141), channel_id=1, source_target_pairs={{0,48},{1,13},{2,50},{3,15},{4,52},{5,1},{6,54},{7,3},{8,56},{9,5}... | collective-permute-start | bytes 995336 | tf_op jit(solution)/shard_map/ppermute | solution.py:95
  70.4 14.8 %collective-permute-start.8 = (f16[1296,128]{1,0:T(8,128)(2,1)S(1)}, f16[1296,128]{1,0:T(8,128)(2,1)S(1)}, u32[]{:S(2)}, u32[]{:S(2)}) collective-permute-start(f16[1296,128]{1,0:T(8,128)(2,1)S(1)} %convert_element_type.138), channel_id=1, source_target_pairs={{0,32},{1,9},{2,34},{3,11},{4,36},{5,13},{6,38},{7,15},{8,40},{9,1... | collective-permute-start | bytes 995336 | tf_op jit(solution)/shard_map/ppermute | solution.py:95
  71.7 13.6 %collective-permute-start.6 = (f16[1296,128]{1,0:T(8,128)(2,1)S(1)}, f16[1296,128]{1,0:T(8,128)(2,1)S(1)}, u32[]{:S(2)}, u32[]{:S(2)}) collective-permute-start(f16[1296,128]{1,0:T(8,128)(2,1)S(1)} %convert_element_type.135), channel_id=1, source_target_pairs={{0,16},{1,5},{2,18},{3,7},{4,20},{5,9},{6,22},{7,11},{8,24},{9,13}... | collective-permute-start | bytes 995336 | tf_op jit(solution)/shard_map/ppermute | solution.py:95
  81.6 15.5 %collective-permute-start.12 = (bf16[4,4,128,128]{3,2,1,0:T(8,128)(2,1)S(1)}, bf16[4,4,128,128]{3,2,1,0:T(8,128)(2,1)S(1)}, u32[]{:S(2)}, u32[]{:S(2)}) collective-permute-start(bf16[4,4,128,128]{3,2,1,0:T(8,128)(2,1)S(1)} %get-tuple-element.79), channel_id=1, source_target_pairs={{0,12},{1,49},{2,14},{3,51},{4,0},{5,53},{6,2},{7,55},{8,4},{9,57}... | collective-permute-start | bytes 1572872 | tf_op jit(solution)/shard_map/ppermute | solution.py:95
  85.3 11.7 %collective-permute-start.16 = (bf16[4,4,128,128]{3,2,1,0:T(8,128)(2,1)S(1)}, bf16[4,4,128,128]{3,2,1,0:T(8,128)(2,1)S(1)}, u32[]{:S(2)}, u32[]{:S(2)}) collective-permute-start(bf16[4,4,128,128]{3,2,1,0:T(8,128)(2,1)S(1)} %get-tuple-element.88), channel_id=1, source_target_pairs={{0,8},{1,33},{2,10},{3,35},{4,12},{5,37},{6,14},{7,39},{8,0},{9,41... | collective-permute-start | bytes 1572872 | tf_op jit(solution)/shard_map/ppermute | solution.py:95
  85.3 15.2 %collective-permute-start.15 = (bf16[4,4,128,128]{3,2,1,0:T(8,128)(2,1)S(1)}, bf16[4,4,128,128]{3,2,1,0:T(8,128)(2,1)S(1)}, u32[]{:S(2)}, u32[]{:S(2)}) collective-permute-start(bf16[4,4,128,128]{3,2,1,0:T(8,128)(2,1)S(1)} %get-tuple-element.86), channel_id=1, source_target_pairs={{0,4},{1,17},{2,6},{3,19},{4,8},{5,21},{6,10},{7,23},{8,12},{9,25}... | collective-permute-start | bytes 1572872 | tf_op jit(solution)/shard_map/ppermute | solution.py:95
  101.1 8.8 %collective-permute-start.19 = (f16[1056,128]{1,0:T(8,128)(2,1)S(1)}, f16[1056,128]{1,0:T(8,128)(2,1)S(1)}, u32[]{:S(2)}, u32[]{:S(2)}) collective-permute-start(f16[1056,128]{1,0:T(8,128)(2,1)S(1)} %pad_maximum_fusion.3), channel_id=1, source_target_pairs={{0,48},{1,13},{2,50},{3,15},{4,52},{5,1},{6,54},{7,3},{8,56},{9,5}... | collective-permute-start | bytes 811016 | tf_op jit(solution)/shard_map/ppermute | solution.py:95
  103.7 7.0 %collective-permute-start.18 = (f16[1056,128]{1,0:T(8,128)(2,1)S(1)}, f16[1056,128]{1,0:T(8,128)(2,1)S(1)}, u32[]{:S(2)}, u32[]{:S(2)}) collective-permute-start(f16[1056,128]{1,0:T(8,128)(2,1)S(1)} %pad_maximum_fusion.2), channel_id=1, source_target_pairs={{0,32},{1,9},{2,34},{3,11},{4,36},{5,13},{6,38},{7,15},{8,40},{9,1... | collective-permute-start | bytes 811016 | tf_op jit(solution)/shard_map/ppermute | solution.py:95
  104.2 9.6 %collective-permute-start.17 = (f16[1056,128]{1,0:T(8,128)(2,1)S(1)}, f16[1056,128]{1,0:T(8,128)(2,1)S(1)}, u32[]{:S(2)}, u32[]{:S(2)}) collective-permute-start(f16[1056,128]{1,0:T(8,128)(2,1)S(1)} %pad_maximum_fusion.1), channel_id=1, source_target_pairs={{0,16},{1,5},{2,18},{3,7},{4,20},{5,9},{6,22},{7,11},{8,24},{9,13}... | collective-permute-start | bytes 811016 | tf_op jit(solution)/shard_map/ppermute | solution.py:95
  105.0 14.1 %collective-permute-start.13 = (f16[1296,128]{1,0:T(8,128)(2,1)S(1)}, f16[1296,128]{1,0:T(8,128)(2,1)S(1)}, u32[]{:S(2)}, u32[]{:S(2)}) collective-permute-start(f16[1296,128]{1,0:T(8,128)(2,1)S(1)} %convert_element_type.144), channel_id=1, source_target_pairs={{2,66},{3,67},{6,70},{7,71},{10,74},{11,75},{14,78},{15,79},{18,82... | collective-permute-start | bytes 995336 | tf_op jit(solution)/shard_map/ppermute | solution.py:95
  114.3 9.8 %collective-permute-start.20 = (f16[1040,128]{1,0:T(8,128)(2,1)S(1)}, f16[1040,128]{1,0:T(8,128)(2,1)S(1)}, u32[]{:S(2)}, u32[]{:S(2)}) collective-permute-start(f16[1040,128]{1,0:T(8,128)(2,1)S(1)} %convert_element_type.165), channel_id=1, source_target_pairs={{0,64},{1,65},{4,68},{5,69},{8,72},{9,73},{12,76},{13,77},{16,80},... | collective-permute-start | bytes 798728 | tf_op jit(solution)/shard_map/ppermute | solution.py:95
  119.2 6.0 %collective-permute-start.14 = (f32[512,128]{1,0:T(8,128)S(1)}, f32[512,128]{1,0:T(8,128)S(1)}, u32[]{:S(2)}, u32[]{:S(2)}) collective-permute-start(f32[512,128]{1,0:T(8,128)S(1)} %slice.140), channel_id=1, source_target_pairs={{1,0},{0,1},{3,2},{2,3},{5,4},{4,5},{7,6},{6,7},{9,8},{8,9},{11,10... | collective-permute-start | bytes 786440 | tf_op jit(solution)/shard_map/ppermute | solution.py:95
  126.3 13.2 %collective-permute-start.24 = (f16[528,128]{1,0:T(8,128)(2,1)S(1)}, f16[528,128]{1,0:T(8,128)(2,1)S(1)}, u32[]{:S(2)}, u32[]{:S(2)}) collective-permute-start(f16[528,128]{1,0:T(8,128)(2,1)S(1)} %convert_element_type.177), channel_id=1, source_target_pairs={{48,0},{0,1},{104,2},{31,3},{4,4},{44,5},{120,6},{59,7},{8,8},{20,... | collective-permute-start | bytes 405512 | tf_op jit(solution)/shard_map/ppermute | solution.py:95
  130.8 9.3 %collective-permute-start.23 = (f16[528,128]{1,0:T(8,128)(2,1)S(1)}, f16[528,128]{1,0:T(8,128)(2,1)S(1)}, u32[]{:S(2)}, u32[]{:S(2)}) collective-permute-start(f16[528,128]{1,0:T(8,128)(2,1)S(1)} %convert_element_type.174), channel_id=1, source_target_pairs={{32,0},{52,1},{116,2},{55,3},{36,4},{4,5},{108,6},{47,7},{40,8},{6... | collective-permute-start | bytes 405512 | tf_op jit(solution)/shard_map/ppermute | solution.py:95
  132.7 8.5 %collective-permute-start.22 = (f16[528,128]{1,0:T(8,128)(2,1)S(1)}, f16[528,128]{1,0:T(8,128)(2,1)S(1)}, u32[]{:S(2)}, u32[]{:S(2)}) collective-permute-start(f16[528,128]{1,0:T(8,128)(2,1)S(1)} %convert_element_type.171), channel_id=1, source_target_pairs={{0,0},{28,1},{64,2},{43,3},{20,4},{16,5},{68,6},{19,7},{56,8},{8,9... | collective-permute-start | bytes 405512 | tf_op jit(solution)/shard_map/ppermute | solution.py:95
  134.9 10.2 %collective-permute-start.21 = (f16[528,128]{1,0:T(8,128)(2,1)S(1)}, f16[528,128]{1,0:T(8,128)(2,1)S(1)}, u32[]{:S(2)}, u32[]{:S(2)}) collective-permute-start(f16[528,128]{1,0:T(8,128)(2,1)S(1)} %convert_element_type.168), channel_id=1, source_target_pairs={{16,0},{40,1},{92,2},{3,3},{52,4},{56,5},{80,6},{7,7},{24,8},{32,9... | collective-permute-start | bytes 405512 | tf_op jit(solution)/shard_map/ppermute | solution.py:95

commit v4 on v3

--- a/solution.py
+++ b/solution.py
@@ -64,30 +64,15 @@
 
 @functools.cache
 def rounds():
-    left = [messages(d) for d in range(128)]
-    todo = [set(range(4)) for _ in range(128)]
     perms, sent, filled = [], np.zeros((4, 128), np.int32), np.zeros((4, 128), np.int32)
     for k in range(4):
-        taken = {}
-
-        def place(d, seen):
-            for m in sorted(todo[d]):
-                to = left[d][m][0]
-                if to in seen:
-                    continue
-                seen.add(to)
-                if to not in taken or place(taken[to][0], seen):
-                    taken[to] = (d, m)
-                    return True
-            return False
-
+        pairs = []
         for d in range(128):
-            place(d, set())
-        perms.append([(d, to) for to, (d, _) in sorted(taken.items())])
-        for to, (d, m) in taken.items():
-            todo[d].remove(m)
-            sent[k, d] = m
-            filled[k, to] = left[d][m][1]
+            sent[k, d] = ((d >> 4) & 3) ^ k
+            to, slot = messages(d)[sent[k, d]]
+            filled[k, to] = slot
+            pairs.append((d, to))
+        perms.append(pairs)
     return perms, sent, filled
 
 
@@ -164,13 +149,10 @@
 def mate_kernel(place, other, scaled, *rest):
     outs, total = rest[4:8], rest[8]
 
-    def step(t, _):
-        columns = pl.ds(pl.multiple_of(t // 2 * 512, 512), 512)
-        total[...] = product(other[:, columns], scaled[2 * place[3] + t % 2])
+    for t in range(4):
+        half = slice(t // 2 * 512, t // 2 * 512 + 512)
+        total[...] = product(other[:, half], scaled[2 * place[3] + t % 2])
         scatter_blocks(place, total, outs, 6 + t)
-        return 0
-
-    lax.fori_loop(0, 4, step, 0)
 
 
 def mate_products(place, other, scaled, blocks):

time: 149 us -> 146 us (0.980)
  starting transfers between devices: 48.1 us -> 46.2 us
    ppermute x25, starting transfers between devices: 48.1 us -> 46.2 us  [permute(): return lax.ppermute(value, AXES, pairs)]
  transfers between devices with their start and end apart: 25 -> 25, of which waited for: 14 -> 13; matrix products, arithmetic and copies ran while one was open for 2% -> 2% of each run, Pallas kernels for 18% -> 18%
where the time goes in v4:
time: 146 us; the launch traced here: 145 us
  waiting for transfers between devices  63.8 us (44%)
  starting transfers between devices  46.2 us (32%)
  Pallas kernels  29.6 us (20%)
  local copies, waits for them, and re-layouts  3.87 us (3%)
    ppermute x25, waiting for transfers between devices, permute(): return lax.ppermute(value, AXES, pairs)  63.8 us
    ppermute x25, starting transfers between devices, permute(): return lax.ppermute(value, AXES, pairs)  46.2 us
    pallas_call x11, Pallas kernels, call(): pl.pallas_call(kernel, out_shape=out_shape, in_specs=[smem] * len(scalars...  29.6 us
  transfers between devices with their start and end apart: 25, of which 13 were waited for; matrix products, arithmetic and copies ran while one was open for 2% of the time, Pallas kernels for 18%

profile of v4, /device:TPU:1, one launch (start us, length us, event | category | flops | bytes accessed | tf_op | source)
XLA Modules:
  0.0 145.3 jit_solution(15433617539552555443)
XLA Ops:
  0.0 2.8 %slice.99 = bf16[1536,512]{1,0:T(8,128)(2,1)} slice(bf16[1536,1024]{1,0:T(8,128)(2,1)} %own), slice={[0:1536], [0:512]} | slice | bytes 3145728 | tf_op jit(solution)/shard_map/slice | solution.py:348
  2.8 1.4 collective-permute-start
  4.2 1.3 collective-permute-start.4
  5.6 0.7 dynamic-slice_bitcast_fusion
  6.4 7.5 %own_products.1 = (bf16[4,1536,512]{2,1,0:T(8,128)(2,1)S(1)}, f32[4,10,128,128]{3,2,1,0:T(8,128)S(1)}, bf16[4,10,128,128]{3,2,1,0:T(8,128)(2,1)S(1)}, bf16[4,10,...) custom-call(s32[5]{0:T(128)S(1)} %stack.23.place, f32[2]{0:T(128)S(1)} %copy-done.1, ...), custom_call_target="tpu_custom_call" | custom-call | flops 4831838208 | tf_op jit(solution)/shard_map/own_products/pallas_call | solution.py:86
  13.9 5.8 %mate_products.1 = (f32[4,10,128,128]{3,2,1,0:T(8,128)S(1)}, bf16[4,10,128,128]{3,2,1,0:T(8,128)(2,1)S(1)}, bf16[4,10,128,128]{3,2,1,0:T(8,128)(2,1)S(1)}, bf16[4,10,128,128]{3,2,1,0:T(8,128)(2,1)S(1)}) custom-call(s32[13]{0:T(128)S(1)} %concatenate.16.place, ...), custom_call_target="tpu_custom_call", output_to_operand_aliasing={{0}: (3, {}), {1}: (4, {}), {2}: (5, {}), {3}: (6, {})} | custom-call | flops 3221225472 | tf_op jit(solution)/shard_map/mate_products/pallas_call | solution.py:86
  19.7 3.8 %collective-permute-start.3 = (bf16[4,10,128,128]{3,2,1,0:T(8,128)(2,1)S(1)}, bf16[4,10,128,128]{3,2,1,0:T(8,128)(2,1)S(1)}, u32[]{:S(2)}, u32[]{:S(2)}) collective-permute-start(bf16[4,10,128,128]{3,2,1,0:T(8,128)(2,1)S(1)} %get-tuple-element.61), channel_id=1, source_target_pairs={{0,12},{1,49},{2,14},{3,51},{4,0},{5,53},{6,2},{7,55},{8,4},{9,57}... | collective-permute-start | bytes 3932168 | tf_op jit(solution)/shard_map/ppermute | solution.py:80
  23.5 0.7 collective-permute-start.1
  24.4 16.2 %collective-permute-done.4.other = bf16[1536,512]{1,0:T(8,128)(2,1)} collective-permute-done((bf16[1536,512]{1,0:T(8,128)(2,1)}, bf16[1536,512]{1,0:T(8,128)(2,1)}, u32[]{:S(2)}, u32[]{:S(2)}) %collective-permute-start.4) | collective-permute-done | bytes 1572896 | tf_op jit(solution)/shard_map/ppermute | solution.py:80
  40.6 1.3 collective-permute-start.11
  41.9 6.0 %far_products.2 = (f32[4,4,128,128]{3,2,1,0:T(8,128)S(1)}, bf16[4,4,128,128]{3,2,1,0:T(8,128)(2,1)S(1)}, bf16[4,4,128,128]{3,2,1,0:T(8,128)(2,1)S(1)}, bf16[4,4,128,128]{3,2,1,0:T(8,128)(2,1)S(1)}) custom-call(s32[13]{0:T(128)S(1)} %concatenate.16.place, bf16[1536,512]{1,0:T(8,128)(2,1)} %collective-permute-done.4.other, ...), custom_call_target="tpu_custom_call" | custom-call | flops 3221225472 | tf_op jit(solution)/shard_map/far_products/pallas_call | solution.py:86
  47.9 4.2 %collective-permute-done.3.c = bf16[4,10,128,128]{3,2,1,0:T(8,128)(2,1)S(1)} collective-permute-done((bf16[4,10,128,128]{3,2,1,0:T(8,128)(2,1)S(1)}, bf16[4,10,128,128]{3,2,1,0:T(8,128)(2,1)S(1)}, u32[]{:S(2)}, u32[]{:S(2)}) %collective-permute-start.3) | collective-permute-done | bytes 1310752 | tf_op jit(solution)/shard_map/ppermute | solution.py:80
  52.1 3.4 %collective-permute-start.9 = (bf16[4,4,128,128]{3,2,1,0:T(8,128)(2,1)S(1)}, bf16[4,4,128,128]{3,2,1,0:T(8,128)(2,1)S(1)}, u32[]{:S(2)}, u32[]{:S(2)}) collective-permute-start(bf16[4,4,128,128]{3,2,1,0:T(8,128)(2,1)S(1)} %get-tuple-element.74), channel_id=1, source_target_pairs={{0,12},{1,49},{2,14},{3,51},{4,0},{5,53},{6,2},{7,55},{8,4},{9,57}... | collective-permute-start | bytes 1572872 | tf_op jit(solution)/shard_map/ppermute | solution.py:80
  55.5 0.6 collective-permute-start.5
  56.1 0.9 first_sum.3
  57.1 10.2 %collective-permute-done.9.c = bf16[4,4,128,128]{3,2,1,0:T(8,128)(2,1)S(1)} collective-permute-done((bf16[4,4,128,128]{3,2,1,0:T(8,128)(2,1)S(1)}, bf16[4,4,128,128]{3,2,1,0:T(8,128)(2,1)S(1)}, u32[]{:S(2)}, u32[]{:S(2)}) %collective-permute-start.9) | collective-permute-done | bytes 524320 | tf_op jit(solution)/shard_map/ppermute | solution.py:80
  67.3 2.4 %collective-permute-start.10 = (f16[1296,128]{1,0:T(8,128)(2,1)S(1)}, f16[1296,128]{1,0:T(8,128)(2,1)S(1)}, u32[]{:S(2)}, u32[]{:S(2)}) collective-permute-start(f16[1296,128]{1,0:T(8,128)(2,1)S(1)} %convert_element_type.141), channel_id=1, source_target_pairs={{0,48},{1,13},{2,50},{3,15},{4,52},{5,1},{6,54},{7,3},{8,56},{9,5}... | collective-permute-start | bytes 995336 | tf_op jit(solution)/shard_map/ppermute | solution.py:80
  69.7 0.5 collective-permute-start.8
  70.2 0.5 collective-permute-done.5.a
  70.7 0.7 collective-permute-start.6
  71.5 4.4 %collective-permute-done.11.other = bf16[1536,512]{1,0:T(8,128)(2,1)S(1)} collective-permute-done((bf16[1536,512]{1,0:T(8,128)(2,1)S(1)}, bf16[1536,512]{1,0:T(8,128)(2,1)S(1)}, u32[]{:S(2)}, u32[]{:S(2)}) %collective-permute-start.11) | collective-permute-done | bytes 1572896 | tf_op jit(solution)/shard_map/ppermute | solution.py:80
  75.9 5.1 %far_products.3 = (f32[4,4,128,128]{3,2,1,0:T(8,128)S(1)}, bf16[4,4,128,128]{3,2,1,0:T(8,128)(2,1)S(1)}, bf16[4,4,128,128]{3,2,1,0:T(8,128)(2,1)S(1)}, bf16[4,4,128,128]{3,2,1,0:T(8,128)(2,1)S(1)}) custom-call(s32[13]{0:T(128)S(1)} %concatenate.16.place, bf16[1536,512]{1,0:T(8,128)(2,1)S(1)} %collective-permute-done.11.other, ...), custom_call_target="tpu_custom_call" | custom-call | flops 3221225472 | tf_op jit(solution)/shard_map/far_products/pallas_call | solution.py:86
  81.0 0.4 first_sum.4
  81.6 3.7 %collective-permute-start.12 = (bf16[4,4,128,128]{3,2,1,0:T(8,128)(2,1)S(1)}, bf16[4,4,128,128]{3,2,1,0:T(8,128)(2,1)S(1)}, u32[]{:S(2)}, u32[]{:S(2)}) collective-permute-start(bf16[4,4,128,128]{3,2,1,0:T(8,128)(2,1)S(1)} %get-tuple-element.79), channel_id=1, source_target_pairs={{0,12},{1,49},{2,14},{3,51},{4,0},{5,53},{6,2},{7,55},{8,4},{9,57}... | collective-permute-start | bytes 1572872 | tf_op jit(solution)/shard_map/ppermute | solution.py:80
  85.3 0.7 collective-permute-start.15
  86.0 0.2 multiply_add_fusion.1.value
  86.2 10.8 %collective-permute-done.12.c = bf16[4,4,128,128]{3,2,1,0:T(8,128)(2,1)S(1)} collective-permute-done((bf16[4,4,128,128]{3,2,1,0:T(8,128)(2,1)S(1)}, bf16[4,4,128,128]{3,2,1,0:T(8,128)(2,1)S(1)}, u32[]{:S(2)}, u32[]{:S(2)}) %collective-permute-start.12) | collective-permute-done | bytes 524320 | tf_op jit(solution)/shard_map/ppermute | solution.py:80
  97.0 3.5 %collective-permute-done.15.a = bf16[4,4,128,128]{3,2,1,0:T(8,128)(2,1)S(1)} collective-permute-done((bf16[4,4,128,128]{3,2,1,0:T(8,128)(2,1)S(1)}, bf16[4,4,128,128]{3,2,1,0:T(8,128)(2,1)S(1)}, u32[]{:S(2)}, u32[]{:S(2)}) %collective-permute-start.15) | collective-permute-done | bytes 524320 | tf_op jit(solution)/shard_map/ppermute | solution.py:80
  100.5 0.4 first_sum.5
  101.1 2.5 %collective-permute-start.19 = (f16[1056,128]{1,0:T(8,128)(2,1)S(1)}, f16[1056,128]{1,0:T(8,128)(2,1)S(1)}, u32[]{:S(2)}, u32[]{:S(2)}) collective-permute-start(f16[1056,128]{1,0:T(8,128)(2,1)S(1)} %pad_maximum_fusion.3), channel_id=1, source_target_pairs={{0,48},{1,13},{2,50},{3,15},{4,52},{5,1},{6,54},{7,3},{8,56},{9,5}... | collective-permute-start | bytes 811016 | tf_op jit(solution)/shard_map/ppermute | solution.py:80
  103.7 0.3 collective-permute-start.18
  104.1 0.7 collective-permute-start.17
  104.8 0.2 seal.2
  105.0 1.3 collective-permute-start.13
  106.3 3.6 %collective-permute-done.19 = f16[1056,128]{1,0:T(8,128)(2,1)S(1)} collective-permute-done((f16[1056,128]{1,0:T(8,128)(2,1)S(1)}, f16[1056,128]{1,0:T(8,128)(2,1)S(1)}, u32[]{:S(2)}, u32[]{:S(2)}) %collective-permute-start.19) | collective-permute-done | bytes 270368 | tf_op jit(solution)/shard_map/ppermute | solution.py:80
  109.9 0.8 collective-permute-done.18
  110.7 3.1 %collective-permute-done.17 = f16[1056,128]{1,0:T(8,128)(2,1)S(1)} collective-permute-done((f16[1056,128]{1,0:T(8,128)(2,1)S(1)}, f16[1056,128]{1,0:T(8,128)(2,1)S(1)}, u32[]{:S(2)}, u32[]{:S(2)}) %collective-permute-start.17) | collective-permute-done | bytes 270368 | tf_op jit(solution)/shard_map/ppermute | solution.py:80
  113.8 0.2 multiply_add_fusion.4
  114.0 0.2 seal.3
  114.3 4.8 %collective-permute-start.20 = (f16[1040,128]{1,0:T(8,128)(2,1)S(1)}, f16[1040,128]{1,0:T(8,128)(2,1)S(1)}, u32[]{:S(2)}, u32[]{:S(2)}) collective-permute-start(f16[1040,128]{1,0:T(8,128)(2,1)S(1)} %convert_element_type.165), channel_id=1, source_target_pairs={{0,64},{1,65},{4,68},{5,69},{8,72},{9,73},{12,76},{13,77},{16,80},... | collective-permute-start | bytes 798728 | tf_op jit(solution)/shard_map/ppermute | solution.py:80
  119.2 4.4 %collective-permute-start.14 = (f32[512,128]{1,0:T(8,128)S(1)}, f32[512,128]{1,0:T(8,128)S(1)}, u32[]{:S(2)}, u32[]{:S(2)}) collective-permute-start(f32[512,128]{1,0:T(8,128)S(1)} %slice.140), channel_id=1, source_target_pairs={{1,0},{0,1},{3,2},{2,3},{5,4},{4,5},{7,6},{6,7},{9,8},{8,9},{11,10... | collective-permute-start | bytes 786440 | tf_op jit(solution)/shard_map/ppermute | solution.py:80
  123.7 1.1 collective-permute-done.14.twin
  124.8 1.0 pack.1
  125.8 3.0 %collective-permute-start.24 = (f16[528,128]{1,0:T(8,128)(2,1)S(1)}, f16[528,128]{1,0:T(8,128)(2,1)S(1)}, u32[]{:S(2)}, u32[]{:S(2)}) collective-permute-start(f16[528,128]{1,0:T(8,128)(2,1)S(1)} %convert_element_type.177), channel_id=1, source_target_pairs={{0,17},{1,48},{2,81},{3,112},{4,21},{5,52},{6,85},{7,116},{8,25},{... | collective-permute-start | bytes 405512 | tf_op jit(solution)/shard_map/ppermute | solution.py:80
  128.9 2.1 %collective-permute-start.23 = (f16[528,128]{1,0:T(8,128)(2,1)S(1)}, f16[528,128]{1,0:T(8,128)(2,1)S(1)}, u32[]{:S(2)}, u32[]{:S(2)}) collective-permute-start(f16[528,128]{1,0:T(8,128)(2,1)S(1)} %convert_element_type.174), channel_id=1, source_target_pairs={{0,1},{1,32},{2,65},{3,96},{4,5},{5,36},{6,69},{7,100},{8,9},{9,40... | collective-permute-start | bytes 405512 | tf_op jit(solution)/shard_map/ppermute | solution.py:80
  131.1 6.4 %collective-permute-start.21 = (f16[528,128]{1,0:T(8,128)(2,1)S(1)}, f16[528,128]{1,0:T(8,128)(2,1)S(1)}, u32[]{:S(2)}, u32[]{:S(2)}) collective-permute-start(f16[528,128]{1,0:T(8,128)(2,1)S(1)} %convert_element_type.168), channel_id=1, source_target_pairs={{0,0},{1,33},{2,34},{3,3},{4,4},{5,37},{6,38},{7,7},{8,8},{9,41},{... | collective-permute-start | bytes 405512 | tf_op jit(solution)/shard_map/ppermute | solution.py:80
  137.8 5.2 %collective-permute-done.21 = f16[528,128]{1,0:T(8,128)(2,1)S(1)} collective-permute-done((f16[528,128]{1,0:T(8,128)(2,1)S(1)}, f16[528,128]{1,0:T(8,128)(2,1)S(1)}, u32[]{:S(2)}, u32[]{:S(2)}) %collective-permute-start.21) | collective-permute-done | bytes 135200 | tf_op jit(solution)/shard_map/ppermute | solution.py:80
  143.1 2.2 %unpack.1 = f32[128,2,1024]{2,1,0:T(2,128)} custom-call(s32[13]{0:T(128)S(1)} %concatenate.16.place, f32[512,128]{1,0:T(8,128)S(1)} %convert_multiply_fusion.3.a, f32[512,128]{1,0:T(8,128)S(1)} %convert_multiply_fusion.2.b, f32[512,128]{1,0:T(8,128)S(1)} %convert_multiply_fusion.1.c, f32[512,128]{1,0:T(8,128)S(1)} %convert_multiply_fusion.d), custom_call_target="tpu_custom_call" | custom-call | flops 262144 | tf_op jit(solution)/shard_map/unpack/pallas_call | solution.py:86
  (65 shorter events, 1.6 us)
Async XLA Ops:
  0.0 2.8 %copy-start = (bf16[1536,1024]{1,0:T(8,128)(2,1)S(1)}, bf16[1536,1024]{1,0:T(8,128)(2,1)}, u32[]{:S(2)}) copy-start(bf16[1536,1024]{1,0:T(8,128)(2,1)} %own) | copy-start | bytes 9437188
  0.0 6.4 %copy-start.2 = (f32[1536]{0:T(1024)S(1)}, f32[1536]{0:T(1024)}, u32[]{:S(2)}) copy-start(f32[1536]{0:T(1024)} %param.5) | copy-start | bytes 18436
  0.0 6.4 %copy-start.1 = (f32[2]{0:T(128)S(1)}, f32[2]{0:T(128)}, u32[]{:S(2)}) copy-start(f32[2]{0:T(128)} %frequencies.1) | copy-start | bytes 28
  2.8 11.0 %collective-permute-start = (bf16[1536,1024]{1,0:T(8,128)(2,1)S(1)}, bf16[1536,1024]{1,0:T(8,128)(2,1)}, u32[]{:S(2)}, u32[]{:S(2)}) collective-permute-start(bf16[1536,1024]{1,0:T(8,128)(2,1)S(1)} %copy-done), channel_id=1, source_target_pairs={{1,0},{0,1},{3,2},{2,3},{5,4},{4,5},{7,6},{6,7},{9,8},{8,9},{11,10... | collective-permute-start | bytes 9437192 | tf_op jit(solution)/shard_map/ppermute | solution.py:80
  4.2 36.3 %collective-permute-start.4 = (bf16[1536,512]{1,0:T(8,128)(2,1)}, bf16[1536,512]{1,0:T(8,128)(2,1)}, u32[]{:S(2)}, u32[]{:S(2)}) collective-permute-start(bf16[1536,512]{1,0:T(8,128)(2,1)} %slice.99), channel_id=1, source_target_pairs={{2,0},{3,1},{1,2},{0,3},{6,4},{7,5},{5,6},{4,7},{10,8},{11,9},{9,1... | collective-permute-start | bytes 4718600 | tf_op jit(solution)/shard_map/ppermute | solution.py:80
  19.7 32.4 %collective-permute-start.3 = (bf16[4,10,128,128]{3,2,1,0:T(8,128)(2,1)S(1)}, bf16[4,10,128,128]{3,2,1,0:T(8,128)(2,1)S(1)}, u32[]{:S(2)}, u32[]{:S(2)}) collective-permute-start(bf16[4,10,128,128]{3,2,1,0:T(8,128)(2,1)S(1)} %get-tuple-element.61), channel_id=1, source_target_pairs={{0,12},{1,49},{2,14},{3,51},{4,0},{5,53},{6,2},{7,55},{8,4},{9,57}... | collective-permute-start | bytes 3932168 | tf_op jit(solution)/shard_map/ppermute | solution.py:80
  23.5 32.0 %collective-permute-start.2 = (bf16[4,10,128,128]{3,2,1,0:T(8,128)(2,1)S(1)}, bf16[4,10,128,128]{3,2,1,0:T(8,128)(2,1)S(1)}, u32[]{:S(2)}, u32[]{:S(2)}) collective-permute-start(bf16[4,10,128,128]{3,2,1,0:T(8,128)(2,1)S(1)} %get-tuple-element.60), channel_id=1, source_target_pairs={{0,8},{1,33},{2,10},{3,35},{4,12},{5,37},{6,14},{7,39},{8,0},{9,41... | collective-permute-start | bytes 3932168 | tf_op jit(solution)/shard_map/ppermute | solution.py:80
  23.5 32.0 %collective-permute-start.1 = (bf16[4,10,128,128]{3,2,1,0:T(8,128)(2,1)S(1)}, bf16[4,10,128,128]{3,2,1,0:T(8,128)(2,1)S(1)}, u32[]{:S(2)}, u32[]{:S(2)}) collective-permute-start(bf16[4,10,128,128]{3,2,1,0:T(8,128)(2,1)S(1)} %get-tuple-element.59), channel_id=1, source_target_pairs={{0,4},{1,17},{2,6},{3,19},{4,8},{5,21},{6,10},{7,23},{8,12},{9,25}... | collective-permute-start | bytes 3932168 | tf_op jit(solution)/shard_map/ppermute | solution.py:80
  40.6 35.3 %collective-permute-start.11 = (bf16[1536,512]{1,0:T(8,128)(2,1)S(1)}, bf16[1536,512]{1,0:T(8,128)(2,1)S(1)}, u32[]{:S(2)}, u32[]{:S(2)}) collective-permute-start(bf16[1536,512]{1,0:T(8,128)(2,1)S(1)} %slice.106), channel_id=1, source_target_pairs={{2,0},{3,1},{1,2},{0,3},{6,4},{7,5},{5,6},{4,7},{10,8},{11,9},{9,1... | collective-permute-start | bytes 4718600 | tf_op jit(solution)/shard_map/ppermute | solution.py:80
  52.1 15.2 %collective-permute-start.9 = (bf16[4,4,128,128]{3,2,1,0:T(8,128)(2,1)S(1)}, bf16[4,4,128,128]{3,2,1,0:T(8,128)(2,1)S(1)}, u32[]{:S(2)}, u32[]{:S(2)}) collective-permute-start(bf16[4,4,128,128]{3,2,1,0:T(8,128)(2,1)S(1)} %get-tuple-element.74), channel_id=1, source_target_pairs={{0,12},{1,49},{2,14},{3,51},{4,0},{5,53},{6,2},{7,55},{8,4},{9,57}... | collective-permute-start | bytes 1572872 | tf_op jit(solution)/shard_map/ppermute | solution.py:80
  55.5 14.2 %collective-permute-start.7 = (bf16[4,4,128,128]{3,2,1,0:T(8,128)(2,1)S(1)}, bf16[4,4,128,128]{3,2,1,0:T(8,128)(2,1)S(1)}, u32[]{:S(2)}, u32[]{:S(2)}) collective-permute-start(bf16[4,4,128,128]{3,2,1,0:T(8,128)(2,1)S(1)} %get-tuple-element.70), channel_id=1, source_target_pairs={{0,8},{1,33},{2,10},{3,35},{4,12},{5,37},{6,14},{7,39},{8,0},{9,41... | collective-permute-start | bytes 1572872 | tf_op jit(solution)/shard_map/ppermute | solution.py:80
  55.5 15.2 %collective-permute-start.5 = (bf16[4,4,128,128]{3,2,1,0:T(8,128)(2,1)S(1)}, bf16[4,4,128,128]{3,2,1,0:T(8,128)(2,1)S(1)}, u32[]{:S(2)}, u32[]{:S(2)}) collective-permute-start(bf16[4,4,128,128]{3,2,1,0:T(8,128)(2,1)S(1)} %get-tuple-element.66), channel_id=1, source_target_pairs={{0,4},{1,17},{2,6},{3,19},{4,8},{5,21},{6,10},{7,23},{8,12},{9,25}... | collective-permute-start | bytes 1572872 | tf_op jit(solution)/shard_map/ppermute | solution.py:80
  67.3 14.3 %collective-permute-start.10 = (f16[1296,128]{1,0:T(8,128)(2,1)S(1)}, f16[1296,128]{1,0:T(8,128)(2,1)S(1)}, u32[]{:S(2)}, u32[]{:S(2)}) collective-permute-start(f16[1296,128]{1,0:T(8,128)(2,1)S(1)} %convert_element_type.141), channel_id=1, source_target_pairs={{0,48},{1,13},{2,50},{3,15},{4,52},{5,1},{6,54},{7,3},{8,56},{9,5}... | collective-permute-start | bytes 995336 | tf_op jit(solution)/shard_map/ppermute | solution.py:80
  69.7 15.6 %collective-permute-start.8 = (f16[1296,128]{1,0:T(8,128)(2,1)S(1)}, f16[1296,128]{1,0:T(8,128)(2,1)S(1)}, u32[]{:S(2)}, u32[]{:S(2)}) collective-permute-start(f16[1296,128]{1,0:T(8,128)(2,1)S(1)} %convert_element_type.138), channel_id=1, source_target_pairs={{0,32},{1,9},{2,34},{3,11},{4,36},{5,13},{6,38},{7,15},{8,40},{9,1... | collective-permute-start | bytes 995336 | tf_op jit(solution)/shard_map/ppermute | solution.py:80
  70.7 14.5 %collective-permute-start.6 = (f16[1296,128]{1,0:T(8,128)(2,1)S(1)}, f16[1296,128]{1,0:T(8,128)(2,1)S(1)}, u32[]{:S(2)}, u32[]{:S(2)}) collective-permute-start(f16[1296,128]{1,0:T(8,128)(2,1)S(1)} %convert_element_type.135), channel_id=1, source_target_pairs={{0,16},{1,5},{2,18},{3,7},{4,20},{5,9},{6,22},{7,11},{8,24},{9,13}... | collective-permute-start | bytes 995336 | tf_op jit(solution)/shard_map/ppermute | solution.py:80
  81.6 15.5 %collective-permute-start.12 = (bf16[4,4,128,128]{3,2,1,0:T(8,128)(2,1)S(1)}, bf16[4,4,128,128]{3,2,1,0:T(8,128)(2,1)S(1)}, u32[]{:S(2)}, u32[]{:S(2)}) collective-permute-start(bf16[4,4,128,128]{3,2,1,0:T(8,128)(2,1)S(1)} %get-tuple-element.79), channel_id=1, source_target_pairs={{0,12},{1,49},{2,14},{3,51},{4,0},{5,53},{6,2},{7,55},{8,4},{9,57}... | collective-permute-start | bytes 1572872 | tf_op jit(solution)/shard_map/ppermute | solution.py:80
  85.3 11.7 %collective-permute-start.16 = (bf16[4,4,128,128]{3,2,1,0:T(8,128)(2,1)S(1)}, bf16[4,4,128,128]{3,2,1,0:T(8,128)(2,1)S(1)}, u32[]{:S(2)}, u32[]{:S(2)}) collective-permute-start(bf16[4,4,128,128]{3,2,1,0:T(8,128)(2,1)S(1)} %get-tuple-element.88), channel_id=1, source_target_pairs={{0,8},{1,33},{2,10},{3,35},{4,12},{5,37},{6,14},{7,39},{8,0},{9,41... | collective-permute-start | bytes 1572872 | tf_op jit(solution)/shard_map/ppermute | solution.py:80
  85.3 15.2 %collective-permute-start.15 = (bf16[4,4,128,128]{3,2,1,0:T(8,128)(2,1)S(1)}, bf16[4,4,128,128]{3,2,1,0:T(8,128)(2,1)S(1)}, u32[]{:S(2)}, u32[]{:S(2)}) collective-permute-start(bf16[4,4,128,128]{3,2,1,0:T(8,128)(2,1)S(1)} %get-tuple-element.86), channel_id=1, source_target_pairs={{0,4},{1,17},{2,6},{3,19},{4,8},{5,21},{6,10},{7,23},{8,12},{9,25}... | collective-permute-start | bytes 1572872 | tf_op jit(solution)/shard_map/ppermute | solution.py:80
  101.1 8.8 %collective-permute-start.19 = (f16[1056,128]{1,0:T(8,128)(2,1)S(1)}, f16[1056,128]{1,0:T(8,128)(2,1)S(1)}, u32[]{:S(2)}, u32[]{:S(2)}) collective-permute-start(f16[1056,128]{1,0:T(8,128)(2,1)S(1)} %pad_maximum_fusion.3), channel_id=1, source_target_pairs={{0,48},{1,13},{2,50},{3,15},{4,52},{5,1},{6,54},{7,3},{8,56},{9,5}... | collective-permute-start | bytes 811016 | tf_op jit(solution)/shard_map/ppermute | solution.py:80
  103.7 7.0 %collective-permute-start.18 = (f16[1056,128]{1,0:T(8,128)(2,1)S(1)}, f16[1056,128]{1,0:T(8,128)(2,1)S(1)}, u32[]{:S(2)}, u32[]{:S(2)}) collective-permute-start(f16[1056,128]{1,0:T(8,128)(2,1)S(1)} %pad_maximum_fusion.2), channel_id=1, source_target_pairs={{0,32},{1,9},{2,34},{3,11},{4,36},{5,13},{6,38},{7,15},{8,40},{9,1... | collective-permute-start | bytes 811016 | tf_op jit(solution)/shard_map/ppermute | solution.py:80
  104.1 9.7 %collective-permute-start.17 = (f16[1056,128]{1,0:T(8,128)(2,1)S(1)}, f16[1056,128]{1,0:T(8,128)(2,1)S(1)}, u32[]{:S(2)}, u32[]{:S(2)}) collective-permute-start(f16[1056,128]{1,0:T(8,128)(2,1)S(1)} %pad_maximum_fusion.1), channel_id=1, source_target_pairs={{0,16},{1,5},{2,18},{3,7},{4,20},{5,9},{6,22},{7,11},{8,24},{9,13}... | collective-permute-start | bytes 811016 | tf_op jit(solution)/shard_map/ppermute | solution.py:80
  105.0 14.1 %collective-permute-start.13 = (f16[1296,128]{1,0:T(8,128)(2,1)S(1)}, f16[1296,128]{1,0:T(8,128)(2,1)S(1)}, u32[]{:S(2)}, u32[]{:S(2)}) collective-permute-start(f16[1296,128]{1,0:T(8,128)(2,1)S(1)} %convert_element_type.144), channel_id=1, source_target_pairs={{2,66},{3,67},{6,70},{7,71},{10,74},{11,75},{14,78},{15,79},{18,82... | collective-permute-start | bytes 995336 | tf_op jit(solution)/shard_map/ppermute | solution.py:80
  114.3 9.3 %collective-permute-start.20 = (f16[1040,128]{1,0:T(8,128)(2,1)S(1)}, f16[1040,128]{1,0:T(8,128)(2,1)S(1)}, u32[]{:S(2)}, u32[]{:S(2)}) collective-permute-start(f16[1040,128]{1,0:T(8,128)(2,1)S(1)} %convert_element_type.165), channel_id=1, source_target_pairs={{0,64},{1,65},{4,68},{5,69},{8,72},{9,73},{12,76},{13,77},{16,80},... | collective-permute-start | bytes 798728 | tf_op jit(solution)/shard_map/ppermute | solution.py:80
  119.2 5.6 %collective-permute-start.14 = (f32[512,128]{1,0:T(8,128)S(1)}, f32[512,128]{1,0:T(8,128)S(1)}, u32[]{:S(2)}, u32[]{:S(2)}) collective-permute-start(f32[512,128]{1,0:T(8,128)S(1)} %slice.140), channel_id=1, source_target_pairs={{1,0},{0,1},{3,2},{2,3},{5,4},{4,5},{7,6},{6,7},{9,8},{8,9},{11,10... | collective-permute-start | bytes 786440 | tf_op jit(solution)/shard_map/ppermute | solution.py:80
  125.8 11.8 %collective-permute-start.24 = (f16[528,128]{1,0:T(8,128)(2,1)S(1)}, f16[528,128]{1,0:T(8,128)(2,1)S(1)}, u32[]{:S(2)}, u32[]{:S(2)}) collective-permute-start(f16[528,128]{1,0:T(8,128)(2,1)S(1)} %convert_element_type.177), channel_id=1, source_target_pairs={{0,17},{1,48},{2,81},{3,112},{4,21},{5,52},{6,85},{7,116},{8,25},{... | collective-permute-start | bytes 405512 | tf_op jit(solution)/shard_map/ppermute | solution.py:80
  128.9 8.7 %collective-permute-start.23 = (f16[528,128]{1,0:T(8,128)(2,1)S(1)}, f16[528,128]{1,0:T(8,128)(2,1)S(1)}, u32[]{:S(2)}, u32[]{:S(2)}) collective-permute-start(f16[528,128]{1,0:T(8,128)(2,1)S(1)} %convert_element_type.174), channel_id=1, source_target_pairs={{0,1},{1,32},{2,65},{3,96},{4,5},{5,36},{6,69},{7,100},{8,9},{9,40... | collective-permute-start | bytes 405512 | tf_op jit(solution)/shard_map/ppermute | solution.py:80
  131.1 6.7 %collective-permute-start.22 = (f16[528,128]{1,0:T(8,128)(2,1)S(1)}, f16[528,128]{1,0:T(8,128)(2,1)S(1)}, u32[]{:S(2)}, u32[]{:S(2)}) collective-permute-start(f16[528,128]{1,0:T(8,128)(2,1)S(1)} %convert_element_type.171), channel_id=1, source_target_pairs={{0,16},{1,49},{2,50},{3,19},{4,20},{5,53},{6,54},{7,23},{8,24},{9,... | collective-permute-start | bytes 405512 | tf_op jit(solution)/shard_map/ppermute | solution.py:80
  131.1 11.9 %collective-permute-start.21 = (f16[528,128]{1,0:T(8,128)(2,1)S(1)}, f16[528,128]{1,0:T(8,128)(2,1)S(1)}, u32[]{:S(2)}, u32[]{:S(2)}) collective-permute-start(f16[528,128]{1,0:T(8,128)(2,1)S(1)} %convert_element_type.168), channel_id=1, source_target_pairs={{0,0},{1,33},{2,34},{3,3},{4,4},{5,37},{6,38},{7,7},{8,8},{9,41},{... | collective-permute-start | bytes 405512 | tf_op jit(solution)/shard_map/ppermute | solution.py:80

commit v5 on v4

--- a/solution.py
+++ b/solution.py
@@ -25,11 +25,11 @@
     return (((y_hi * 4 + z) * 4 + x) << 2) + grp
 
 
-def shift_perm(d1=0, d2=0, dy=0):
+def swap_perm(d1=0, d2=0, dy=0):
     pairs = []
     for d in range(128):
         y_hi, s1, s2, grp = parts_of(d)
-        pairs.append((d, device(y_hi ^ dy, (s1 + d1) & 3, (s2 + d2) & 3, grp)))
+        pairs.append((d, device(y_hi ^ dy, s1 ^ d1, s2 ^ d2, grp)))
     return pairs
 
 
@@ -107,7 +107,7 @@
 def scatter_blocks(place, total, outs, n):
     for d in range(4):
         for e in range(4):
-            s1, s2 = (place[0] + d) & 3, (place[1] + e) & 3
+            s1, s2 = place[0] ^ d, place[1] ^ e
             skew = (s1 + s2) & 3
             rows = pl.ds(pl.multiple_of(jnp.where(place[3] == 0, s1, skew) * T, T), T)
             columns = pl.ds(pl.multiple_of(jnp.where(place[3] == 0, skew, s2) * T, T), T)
@@ -252,7 +252,7 @@
 
 
 def across(value, at_home):
-    pairs = [(s, d) for s, d in shift_perm(dy=1) if ((d >> 6) == (d & 3) >> 1) == at_home]
+    pairs = [(s, d) for s, d in swap_perm(dy=1) if ((d >> 6) == (d & 3) >> 1) == at_home]
     count = value.shape[0] // T
     send = call(seal_kernel, [sealed(count)], [], [value], flops=2 * count * T * T, name="seal")
     return value + opened(permute(halved(send)[0], pairs), 0, count)
@@ -328,11 +328,11 @@
 
 
 def send_first(send, earlier):
-    return [permute(after(v, w), shift_perm(d1=d + 1)) for d, (v, w) in enumerate(zip(send, earlier))]
+    return [permute(after(v, w), swap_perm(d1=d + 1)) for d, (v, w) in enumerate(zip(send, earlier))]
 
 
 def send_second(send, earlier):
-    return [permute(after(v, w), shift_perm(d2=e + 1)) for e, (v, w) in enumerate(zip(send, earlier))]
+    return [permute(after(v, w), swap_perm(d2=e + 1)) for e, (v, w) in enumerate(zip(send, earlier))]
 
 
 def on_device(own, energy_gaps, frequencies):

time: 146 us -> 144 us (0.986)
  waiting for transfers between devices: 63.8 us -> 61.9 us
    ppermute x25, waiting for transfers between devices: 63.8 us -> 61.9 us  [permute(): return lax.ppermute(value, AXES, pairs)]
  transfers between devices with their start and end apart: 25 -> 25, of which waited for: 13 -> 12; matrix products, arithmetic and copies ran while one was open for 2% -> 2% of each run, Pallas kernels for 18% -> 18%
where the time goes in v5:
time: 144 us
  waiting for transfers between devices  61.9 us (43%)
  starting transfers between devices  46.6 us (32%)
  Pallas kernels  29.6 us (21%)
  local copies, waits for them, and re-layouts  3.87 us (3%)
    ppermute x25, waiting for transfers between devices, permute(): return lax.ppermute(value, AXES, pairs)  61.9 us
    ppermute x25, starting transfers between devices, permute(): return lax.ppermute(value, AXES, pairs)  46.6 us
    pallas_call x11, Pallas kernels, call(): pl.pallas_call(kernel, out_shape=out_shape, in_specs=[smem] * len(scalars...  29.6 us
  transfers between devices with their start and end apart: 25, of which 12 were waited for; matrix products, arithmetic and copies ran while one was open for 2% of the time, Pallas kernels for 18%

profile of v5, /device:TPU:1, one launch (start us, length us, event | category | flops | bytes accessed | tf_op | source)
XLA Modules:
  0.0 143.7 jit_solution(4787254419115224757)
XLA Ops:
  0.0 2.8 %slice.99 = bf16[1536,512]{1,0:T(8,128)(2,1)} slice(bf16[1536,1024]{1,0:T(8,128)(2,1)} %own), slice={[0:1536], [0:512]} | slice | bytes 3145728 | tf_op jit(solution)/shard_map/slice | solution.py:348
  2.8 1.4 collective-permute-start
  4.2 1.3 collective-permute-start.4
  5.6 0.7 dynamic-slice_bitcast_fusion
  6.4 7.5 %own_products.1 = (bf16[4,1536,512]{2,1,0:T(8,128)(2,1)S(1)}, f32[4,10,128,128]{3,2,1,0:T(8,128)S(1)}, bf16[4,10,128,128]{3,2,1,0:T(8,128)(2,1)S(1)}, bf16[4,10,...) custom-call(s32[5]{0:T(128)S(1)} %stack.23.place, f32[2]{0:T(128)S(1)} %copy-done.1, ...), custom_call_target="tpu_custom_call" | custom-call | flops 4831838208 | tf_op jit(solution)/shard_map/own_products/pallas_call | solution.py:86
  13.9 5.8 %mate_products.1 = (f32[4,10,128,128]{3,2,1,0:T(8,128)S(1)}, bf16[4,10,128,128]{3,2,1,0:T(8,128)(2,1)S(1)}, bf16[4,10,128,128]{3,2,1,0:T(8,128)(2,1)S(1)}, bf16[4,10,128,128]{3,2,1,0:T(8,128)(2,1)S(1)}) custom-call(s32[13]{0:T(128)S(1)} %concatenate.16.place, ...), custom_call_target="tpu_custom_call", output_to_operand_aliasing={{0}: (3, {}), {1}: (4, {}), {2}: (5, {}), {3}: (6, {})} | custom-call | flops 3221225472 | tf_op jit(solution)/shard_map/mate_products/pallas_call | solution.py:86
  19.7 3.8 %collective-permute-start.3 = (bf16[4,10,128,128]{3,2,1,0:T(8,128)(2,1)S(1)}, bf16[4,10,128,128]{3,2,1,0:T(8,128)(2,1)S(1)}, u32[]{:S(2)}, u32[]{:S(2)}) collective-permute-start(bf16[4,10,128,128]{3,2,1,0:T(8,128)(2,1)S(1)} %get-tuple-element.61), channel_id=1, source_target_pairs={{0,12},{1,49},{2,14},{3,51},{4,8},{5,53},{6,10},{7,55},{8,4},{9,57... | collective-permute-start | bytes 3932168 | tf_op jit(solution)/shard_map/ppermute | solution.py:80
  23.5 0.7 collective-permute-start.1
  24.2 0.2 slice.106
  24.4 16.2 %collective-permute-done.4.other = bf16[1536,512]{1,0:T(8,128)(2,1)} collective-permute-done((bf16[1536,512]{1,0:T(8,128)(2,1)}, bf16[1536,512]{1,0:T(8,128)(2,1)}, u32[]{:S(2)}, u32[]{:S(2)}) %collective-permute-start.4) | collective-permute-done | bytes 1572896 | tf_op jit(solution)/shard_map/ppermute | solution.py:80
  40.6 1.3 collective-permute-start.11
  41.9 6.0 %far_products.2 = (f32[4,4,128,128]{3,2,1,0:T(8,128)S(1)}, bf16[4,4,128,128]{3,2,1,0:T(8,128)(2,1)S(1)}, bf16[4,4,128,128]{3,2,1,0:T(8,128)(2,1)S(1)}, bf16[4,4,128,128]{3,2,1,0:T(8,128)(2,1)S(1)}) custom-call(s32[13]{0:T(128)S(1)} %concatenate.16.place, bf16[1536,512]{1,0:T(8,128)(2,1)} %collective-permute-done.4.other, ...), custom_call_target="tpu_custom_call" | custom-call | flops 3221225472 | tf_op jit(solution)/shard_map/far_products/pallas_call | solution.py:86
  47.9 4.8 %collective-permute-done.3.c = bf16[4,10,128,128]{3,2,1,0:T(8,128)(2,1)S(1)} collective-permute-done((bf16[4,10,128,128]{3,2,1,0:T(8,128)(2,1)S(1)}, bf16[4,10,128,128]{3,2,1,0:T(8,128)(2,1)S(1)}, u32[]{:S(2)}, u32[]{:S(2)}) %collective-permute-start.3) | collective-permute-done | bytes 1310752 | tf_op jit(solution)/shard_map/ppermute | solution.py:80
  52.7 2.8 %collective-permute-start.9 = (bf16[4,4,128,128]{3,2,1,0:T(8,128)(2,1)S(1)}, bf16[4,4,128,128]{3,2,1,0:T(8,128)(2,1)S(1)}, u32[]{:S(2)}, u32[]{:S(2)}) collective-permute-start(bf16[4,4,128,128]{3,2,1,0:T(8,128)(2,1)S(1)} %get-tuple-element.74), channel_id=1, source_target_pairs={{0,12},{1,49},{2,14},{3,51},{4,8},{5,53},{6,10},{7,55},{8,4},{9,57... | collective-permute-start | bytes 1572872 | tf_op jit(solution)/shard_map/ppermute | solution.py:80
  55.5 0.6 collective-permute-start.5
  56.1 0.9 first_sum.3
  57.1 10.9 %collective-permute-done.9.c = bf16[4,4,128,128]{3,2,1,0:T(8,128)(2,1)S(1)} collective-permute-done((bf16[4,4,128,128]{3,2,1,0:T(8,128)(2,1)S(1)}, bf16[4,4,128,128]{3,2,1,0:T(8,128)(2,1)S(1)}, u32[]{:S(2)}, u32[]{:S(2)}) %collective-permute-start.9) | collective-permute-done | bytes 524320 | tf_op jit(solution)/shard_map/ppermute | solution.py:80
  68.0 2.4 %collective-permute-start.10 = (f16[1296,128]{1,0:T(8,128)(2,1)S(1)}, f16[1296,128]{1,0:T(8,128)(2,1)S(1)}, u32[]{:S(2)}, u32[]{:S(2)}) collective-permute-start(f16[1296,128]{1,0:T(8,128)(2,1)S(1)} %convert_element_type.141), channel_id=1, source_target_pairs={{0,48},{1,13},{2,50},{3,15},{4,52},{5,9},{6,54},{7,11},{8,56},{9,5... | collective-permute-start | bytes 995336 | tf_op jit(solution)/shard_map/ppermute | solution.py:80
  70.5 0.9 collective-permute-start.6
  71.4 4.5 %collective-permute-done.11.other = bf16[1536,512]{1,0:T(8,128)(2,1)S(1)} collective-permute-done((bf16[1536,512]{1,0:T(8,128)(2,1)S(1)}, bf16[1536,512]{1,0:T(8,128)(2,1)S(1)}, u32[]{:S(2)}, u32[]{:S(2)}) %collective-permute-start.11) | collective-permute-done | bytes 1572896 | tf_op jit(solution)/shard_map/ppermute | solution.py:80
  75.9 5.1 %far_products.3 = (f32[4,4,128,128]{3,2,1,0:T(8,128)S(1)}, bf16[4,4,128,128]{3,2,1,0:T(8,128)(2,1)S(1)}, bf16[4,4,128,128]{3,2,1,0:T(8,128)(2,1)S(1)}, bf16[4,4,128,128]{3,2,1,0:T(8,128)(2,1)S(1)}) custom-call(s32[13]{0:T(128)S(1)} %concatenate.16.place, bf16[1536,512]{1,0:T(8,128)(2,1)S(1)} %collective-permute-done.11.other, ...), custom_call_target="tpu_custom_call" | custom-call | flops 3221225472 | tf_op jit(solution)/shard_map/far_products/pallas_call | solution.py:86
  81.0 0.4 first_sum.4
  81.6 3.7 %collective-permute-start.12 = (bf16[4,4,128,128]{3,2,1,0:T(8,128)(2,1)S(1)}, bf16[4,4,128,128]{3,2,1,0:T(8,128)(2,1)S(1)}, u32[]{:S(2)}, u32[]{:S(2)}) collective-permute-start(bf16[4,4,128,128]{3,2,1,0:T(8,128)(2,1)S(1)} %get-tuple-element.79), channel_id=1, source_target_pairs={{0,12},{1,49},{2,14},{3,51},{4,8},{5,53},{6,10},{7,55},{8,4},{9,57... | collective-permute-start | bytes 1572872 | tf_op jit(solution)/shard_map/ppermute | solution.py:80
  85.3 0.7 collective-permute-start.15
  86.0 0.2 multiply_add_fusion.1.value
  86.2 11.6 %collective-permute-done.12.c = bf16[4,4,128,128]{3,2,1,0:T(8,128)(2,1)S(1)} collective-permute-done((bf16[4,4,128,128]{3,2,1,0:T(8,128)(2,1)S(1)}, bf16[4,4,128,128]{3,2,1,0:T(8,128)(2,1)S(1)}, u32[]{:S(2)}, u32[]{:S(2)}) %collective-permute-start.12) | collective-permute-done | bytes 524320 | tf_op jit(solution)/shard_map/ppermute | solution.py:80
  97.8 0.7 collective-permute-done.15.a
  98.5 0.4 first_sum.5
  99.1 2.6 %collective-permute-start.19 = (f16[1056,128]{1,0:T(8,128)(2,1)S(1)}, f16[1056,128]{1,0:T(8,128)(2,1)S(1)}, u32[]{:S(2)}, u32[]{:S(2)}) collective-permute-start(f16[1056,128]{1,0:T(8,128)(2,1)S(1)} %pad_maximum_fusion.3), channel_id=1, source_target_pairs={{0,48},{1,13},{2,50},{3,15},{4,52},{5,9},{6,54},{7,11},{8,56},{9,5... | collective-permute-start | bytes 811016 | tf_op jit(solution)/shard_map/ppermute | solution.py:80
  101.7 0.6 collective-permute-start.18
  102.4 0.3 collective-permute-start.17
  102.7 0.2 seal.2
  103.0 1.3 collective-permute-start.13
  104.3 3.6 %collective-permute-done.19 = f16[1056,128]{1,0:T(8,128)(2,1)S(1)} collective-permute-done((f16[1056,128]{1,0:T(8,128)(2,1)S(1)}, f16[1056,128]{1,0:T(8,128)(2,1)S(1)}, u32[]{:S(2)}, u32[]{:S(2)}) %collective-permute-start.19) | collective-permute-done | bytes 270368 | tf_op jit(solution)/shard_map/ppermute | solution.py:80
  107.9 0.7 collective-permute-done.18
  108.6 1.0 collective-permute-done.17
  109.7 0.2 multiply_add_fusion.4
  109.9 0.2 seal.3
  110.1 4.5 %collective-permute-start.20 = (f16[1040,128]{1,0:T(8,128)(2,1)S(1)}, f16[1040,128]{1,0:T(8,128)(2,1)S(1)}, u32[]{:S(2)}, u32[]{:S(2)}) collective-permute-start(f16[1040,128]{1,0:T(8,128)(2,1)S(1)} %convert_element_type.165), channel_id=1, source_target_pairs={{0,64},{1,65},{4,68},{5,69},{8,72},{9,73},{12,76},{13,77},{16,80},... | collective-permute-start | bytes 798728 | tf_op jit(solution)/shard_map/ppermute | solution.py:80
  114.8 4.2 %collective-permute-start.14 = (f32[512,128]{1,0:T(8,128)S(1)}, f32[512,128]{1,0:T(8,128)S(1)}, u32[]{:S(2)}, u32[]{:S(2)}) collective-permute-start(f32[512,128]{1,0:T(8,128)S(1)} %slice.140), channel_id=1, source_target_pairs={{1,0},{0,1},{3,2},{2,3},{5,4},{4,5},{7,6},{6,7},{9,8},{8,9},{11,10... | collective-permute-start | bytes 786440 | tf_op jit(solution)/shard_map/ppermute | solution.py:80
  119.1 1.1 collective-permute-done.14.twin
  120.2 1.0 pack.1
  121.2 5.5 %collective-permute-start.24 = (f16[528,128]{1,0:T(8,128)(2,1)S(1)}, f16[528,128]{1,0:T(8,128)(2,1)S(1)}, u32[]{:S(2)}, u32[]{:S(2)}) collective-permute-start(f16[528,128]{1,0:T(8,128)(2,1)S(1)} %convert_element_type.177), channel_id=1, source_target_pairs={{0,17},{1,48},{2,81},{3,112},{4,21},{5,52},{6,85},{7,116},{8,25},{... | collective-permute-start | bytes 405512 | tf_op jit(solution)/shard_map/ppermute | solution.py:80
  126.8 4.4 %collective-permute-start.23 = (f16[528,128]{1,0:T(8,128)(2,1)S(1)}, f16[528,128]{1,0:T(8,128)(2,1)S(1)}, u32[]{:S(2)}, u32[]{:S(2)}) collective-permute-start(f16[528,128]{1,0:T(8,128)(2,1)S(1)} %convert_element_type.174), channel_id=1, source_target_pairs={{0,1},{1,32},{2,65},{3,96},{4,5},{5,36},{6,69},{7,100},{8,9},{9,40... | collective-permute-start | bytes 405512 | tf_op jit(solution)/shard_map/ppermute | solution.py:80
  131.3 3.4 %collective-permute-start.21 = (f16[528,128]{1,0:T(8,128)(2,1)S(1)}, f16[528,128]{1,0:T(8,128)(2,1)S(1)}, u32[]{:S(2)}, u32[]{:S(2)}) collective-permute-start(f16[528,128]{1,0:T(8,128)(2,1)S(1)} %convert_element_type.168), channel_id=1, source_target_pairs={{0,0},{1,33},{2,34},{3,3},{4,4},{5,37},{6,38},{7,7},{8,8},{9,41},{... | collective-permute-start | bytes 405512 | tf_op jit(solution)/shard_map/ppermute | solution.py:80
  134.8 3.0 %collective-permute-done.22 = f16[528,128]{1,0:T(8,128)(2,1)S(1)} collective-permute-done((f16[528,128]{1,0:T(8,128)(2,1)S(1)}, f16[528,128]{1,0:T(8,128)(2,1)S(1)}, u32[]{:S(2)}, u32[]{:S(2)}) %collective-permute-start.22) | collective-permute-done | bytes 135200 | tf_op jit(solution)/shard_map/ppermute | solution.py:80
  137.9 3.7 %collective-permute-done.21 = f16[528,128]{1,0:T(8,128)(2,1)S(1)} collective-permute-done((f16[528,128]{1,0:T(8,128)(2,1)S(1)}, f16[528,128]{1,0:T(8,128)(2,1)S(1)}, u32[]{:S(2)}, u32[]{:S(2)}) %collective-permute-start.21) | collective-permute-done | bytes 135200 | tf_op jit(solution)/shard_map/ppermute | solution.py:80
  141.6 2.2 %unpack.1 = f32[128,2,1024]{2,1,0:T(2,128)} custom-call(s32[13]{0:T(128)S(1)} %concatenate.16.place, f32[512,128]{1,0:T(8,128)S(1)} %convert_multiply_fusion.3.a, f32[512,128]{1,0:T(8,128)S(1)} %convert_multiply_fusion.2.b, f32[512,128]{1,0:T(8,128)S(1)} %convert_multiply_fusion.1.c, f32[512,128]{1,0:T(8,128)S(1)} %convert_multiply_fusion.d), custom_call_target="tpu_custom_call" | custom-call | flops 262144 | tf_op jit(solution)/shard_map/unpack/pallas_call | solution.py:86
  (65 shorter events, 1.3 us)
Async XLA Ops:
  0.0 2.8 %copy-start = (bf16[1536,1024]{1,0:T(8,128)(2,1)S(1)}, bf16[1536,1024]{1,0:T(8,128)(2,1)}, u32[]{:S(2)}) copy-start(bf16[1536,1024]{1,0:T(8,128)(2,1)} %own) | copy-start | bytes 9437188
  0.0 6.4 %copy-start.2 = (f32[1536]{0:T(1024)S(1)}, f32[1536]{0:T(1024)}, u32[]{:S(2)}) copy-start(f32[1536]{0:T(1024)} %param.5) | copy-start | bytes 18436
  0.0 6.4 %copy-start.1 = (f32[2]{0:T(128)S(1)}, f32[2]{0:T(128)}, u32[]{:S(2)}) copy-start(f32[2]{0:T(128)} %frequencies.1) | copy-start | bytes 28
  2.8 11.0 %collective-permute-start = (bf16[1536,1024]{1,0:T(8,128)(2,1)S(1)}, bf16[1536,1024]{1,0:T(8,128)(2,1)}, u32[]{:S(2)}, u32[]{:S(2)}) collective-permute-start(bf16[1536,1024]{1,0:T(8,128)(2,1)S(1)} %copy-done), channel_id=1, source_target_pairs={{1,0},{0,1},{3,2},{2,3},{5,4},{4,5},{7,6},{6,7},{9,8},{8,9},{11,10... | collective-permute-start | bytes 9437192 | tf_op jit(solution)/shard_map/ppermute | solution.py:80
  4.2 36.3 %collective-permute-start.4 = (bf16[1536,512]{1,0:T(8,128)(2,1)}, bf16[1536,512]{1,0:T(8,128)(2,1)}, u32[]{:S(2)}, u32[]{:S(2)}) collective-permute-start(bf16[1536,512]{1,0:T(8,128)(2,1)} %slice.99), channel_id=1, source_target_pairs={{2,0},{3,1},{1,2},{0,3},{6,4},{7,5},{5,6},{4,7},{10,8},{11,9},{9,1... | collective-permute-start | bytes 4718600 | tf_op jit(solution)/shard_map/ppermute | solution.py:80
  19.7 33.0 %collective-permute-start.3 = (bf16[4,10,128,128]{3,2,1,0:T(8,128)(2,1)S(1)}, bf16[4,10,128,128]{3,2,1,0:T(8,128)(2,1)S(1)}, u32[]{:S(2)}, u32[]{:S(2)}) collective-permute-start(bf16[4,10,128,128]{3,2,1,0:T(8,128)(2,1)S(1)} %get-tuple-element.61), channel_id=1, source_target_pairs={{0,12},{1,49},{2,14},{3,51},{4,8},{5,53},{6,10},{7,55},{8,4},{9,57... | collective-permute-start | bytes 3932168 | tf_op jit(solution)/shard_map/ppermute | solution.py:80
  23.5 32.0 %collective-permute-start.2 = (bf16[4,10,128,128]{3,2,1,0:T(8,128)(2,1)S(1)}, bf16[4,10,128,128]{3,2,1,0:T(8,128)(2,1)S(1)}, u32[]{:S(2)}, u32[]{:S(2)}) collective-permute-start(bf16[4,10,128,128]{3,2,1,0:T(8,128)(2,1)S(1)} %get-tuple-element.60), channel_id=1, source_target_pairs={{0,8},{1,33},{2,10},{3,35},{4,12},{5,37},{6,14},{7,39},{8,0},{9,41... | collective-permute-start | bytes 3932168 | tf_op jit(solution)/shard_map/ppermute | solution.py:80
  23.5 32.0 %collective-permute-start.1 = (bf16[4,10,128,128]{3,2,1,0:T(8,128)(2,1)S(1)}, bf16[4,10,128,128]{3,2,1,0:T(8,128)(2,1)S(1)}, u32[]{:S(2)}, u32[]{:S(2)}) collective-permute-start(bf16[4,10,128,128]{3,2,1,0:T(8,128)(2,1)S(1)} %get-tuple-element.59), channel_id=1, source_target_pairs={{0,4},{1,17},{2,6},{3,19},{4,0},{5,21},{6,2},{7,23},{8,12},{9,25},... | collective-permute-start | bytes 3932168 | tf_op jit(solution)/shard_map/ppermute | solution.py:80
  40.6 35.3 %collective-permute-start.11 = (bf16[1536,512]{1,0:T(8,128)(2,1)S(1)}, bf16[1536,512]{1,0:T(8,128)(2,1)S(1)}, u32[]{:S(2)}, u32[]{:S(2)}) collective-permute-start(bf16[1536,512]{1,0:T(8,128)(2,1)S(1)} %slice.106), channel_id=1, source_target_pairs={{2,0},{3,1},{1,2},{0,3},{6,4},{7,5},{5,6},{4,7},{10,8},{11,9},{9,1... | collective-permute-start | bytes 4718600 | tf_op jit(solution)/shard_map/ppermute | solution.py:80
  52.7 15.3 %collective-permute-start.9 = (bf16[4,4,128,128]{3,2,1,0:T(8,128)(2,1)S(1)}, bf16[4,4,128,128]{3,2,1,0:T(8,128)(2,1)S(1)}, u32[]{:S(2)}, u32[]{:S(2)}) collective-permute-start(bf16[4,4,128,128]{3,2,1,0:T(8,128)(2,1)S(1)} %get-tuple-element.74), channel_id=1, source_target_pairs={{0,12},{1,49},{2,14},{3,51},{4,8},{5,53},{6,10},{7,55},{8,4},{9,57... | collective-permute-start | bytes 1572872 | tf_op jit(solution)/shard_map/ppermute | solution.py:80
  55.5 14.9 %collective-permute-start.7 = (bf16[4,4,128,128]{3,2,1,0:T(8,128)(2,1)S(1)}, bf16[4,4,128,128]{3,2,1,0:T(8,128)(2,1)S(1)}, u32[]{:S(2)}, u32[]{:S(2)}) collective-permute-start(bf16[4,4,128,128]{3,2,1,0:T(8,128)(2,1)S(1)} %get-tuple-element.70), channel_id=1, source_target_pairs={{0,8},{1,33},{2,10},{3,35},{4,12},{5,37},{6,14},{7,39},{8,0},{9,41... | collective-permute-start | bytes 1572872 | tf_op jit(solution)/shard_map/ppermute | solution.py:80
  55.5 15.0 %collective-permute-start.5 = (bf16[4,4,128,128]{3,2,1,0:T(8,128)(2,1)S(1)}, bf16[4,4,128,128]{3,2,1,0:T(8,128)(2,1)S(1)}, u32[]{:S(2)}, u32[]{:S(2)}) collective-permute-start(bf16[4,4,128,128]{3,2,1,0:T(8,128)(2,1)S(1)} %get-tuple-element.66), channel_id=1, source_target_pairs={{0,4},{1,17},{2,6},{3,19},{4,0},{5,21},{6,2},{7,23},{8,12},{9,25},... | collective-permute-start | bytes 1572872 | tf_op jit(solution)/shard_map/ppermute | solution.py:80
  68.0 13.5 %collective-permute-start.10 = (f16[1296,128]{1,0:T(8,128)(2,1)S(1)}, f16[1296,128]{1,0:T(8,128)(2,1)S(1)}, u32[]{:S(2)}, u32[]{:S(2)}) collective-permute-start(f16[1296,128]{1,0:T(8,128)(2,1)S(1)} %convert_element_type.141), channel_id=1, source_target_pairs={{0,48},{1,13},{2,50},{3,15},{4,52},{5,9},{6,54},{7,11},{8,56},{9,5... | collective-permute-start | bytes 995336 | tf_op jit(solution)/shard_map/ppermute | solution.py:80
  70.5 14.8 %collective-permute-start.8 = (f16[1296,128]{1,0:T(8,128)(2,1)S(1)}, f16[1296,128]{1,0:T(8,128)(2,1)S(1)}, u32[]{:S(2)}, u32[]{:S(2)}) collective-permute-start(f16[1296,128]{1,0:T(8,128)(2,1)S(1)} %convert_element_type.138), channel_id=1, source_target_pairs={{0,32},{1,9},{2,34},{3,11},{4,36},{5,13},{6,38},{7,15},{8,40},{9,1... | collective-permute-start | bytes 995336 | tf_op jit(solution)/shard_map/ppermute | solution.py:80
  70.5 14.8 %collective-permute-start.6 = (f16[1296,128]{1,0:T(8,128)(2,1)S(1)}, f16[1296,128]{1,0:T(8,128)(2,1)S(1)}, u32[]{:S(2)}, u32[]{:S(2)}) collective-permute-start(f16[1296,128]{1,0:T(8,128)(2,1)S(1)} %convert_element_type.135), channel_id=1, source_target_pairs={{0,16},{1,5},{2,18},{3,7},{4,20},{5,1},{6,22},{7,3},{8,24},{9,13},... | collective-permute-start | bytes 995336 | tf_op jit(solution)/shard_map/ppermute | solution.py:80
  81.6 16.2 %collective-permute-start.12 = (bf16[4,4,128,128]{3,2,1,0:T(8,128)(2,1)S(1)}, bf16[4,4,128,128]{3,2,1,0:T(8,128)(2,1)S(1)}, u32[]{:S(2)}, u32[]{:S(2)}) collective-permute-start(bf16[4,4,128,128]{3,2,1,0:T(8,128)(2,1)S(1)} %get-tuple-element.79), channel_id=1, source_target_pairs={{0,12},{1,49},{2,14},{3,51},{4,8},{5,53},{6,10},{7,55},{8,4},{9,57... | collective-permute-start | bytes 1572872 | tf_op jit(solution)/shard_map/ppermute | solution.py:80
  85.3 12.5 %collective-permute-start.16 = (bf16[4,4,128,128]{3,2,1,0:T(8,128)(2,1)S(1)}, bf16[4,4,128,128]{3,2,1,0:T(8,128)(2,1)S(1)}, u32[]{:S(2)}, u32[]{:S(2)}) collective-permute-start(bf16[4,4,128,128]{3,2,1,0:T(8,128)(2,1)S(1)} %get-tuple-element.88), channel_id=1, source_target_pairs={{0,8},{1,33},{2,10},{3,35},{4,12},{5,37},{6,14},{7,39},{8,0},{9,41... | collective-permute-start | bytes 1572872 | tf_op jit(solution)/shard_map/ppermute | solution.py:80
  85.3 13.2 %collective-permute-start.15 = (bf16[4,4,128,128]{3,2,1,0:T(8,128)(2,1)S(1)}, bf16[4,4,128,128]{3,2,1,0:T(8,128)(2,1)S(1)}, u32[]{:S(2)}, u32[]{:S(2)}) collective-permute-start(bf16[4,4,128,128]{3,2,1,0:T(8,128)(2,1)S(1)} %get-tuple-element.86), channel_id=1, source_target_pairs={{0,4},{1,17},{2,6},{3,19},{4,0},{5,21},{6,2},{7,23},{8,12},{9,25},... | collective-permute-start | bytes 1572872 | tf_op jit(solution)/shard_map/ppermute | solution.py:80
  99.1 8.9 %collective-permute-start.19 = (f16[1056,128]{1,0:T(8,128)(2,1)S(1)}, f16[1056,128]{1,0:T(8,128)(2,1)S(1)}, u32[]{:S(2)}, u32[]{:S(2)}) collective-permute-start(f16[1056,128]{1,0:T(8,128)(2,1)S(1)} %pad_maximum_fusion.3), channel_id=1, source_target_pairs={{0,48},{1,13},{2,50},{3,15},{4,52},{5,9},{6,54},{7,11},{8,56},{9,5... | collective-permute-start | bytes 811016 | tf_op jit(solution)/shard_map/ppermute | solution.py:80
  101.7 6.9 %collective-permute-start.18 = (f16[1056,128]{1,0:T(8,128)(2,1)S(1)}, f16[1056,128]{1,0:T(8,128)(2,1)S(1)}, u32[]{:S(2)}, u32[]{:S(2)}) collective-permute-start(f16[1056,128]{1,0:T(8,128)(2,1)S(1)} %pad_maximum_fusion.2), channel_id=1, source_target_pairs={{0,32},{1,9},{2,34},{3,11},{4,36},{5,13},{6,38},{7,15},{8,40},{9,1... | collective-permute-start | bytes 811016 | tf_op jit(solution)/shard_map/ppermute | solution.py:80
  102.4 7.3 %collective-permute-start.17 = (f16[1056,128]{1,0:T(8,128)(2,1)S(1)}, f16[1056,128]{1,0:T(8,128)(2,1)S(1)}, u32[]{:S(2)}, u32[]{:S(2)}) collective-permute-start(f16[1056,128]{1,0:T(8,128)(2,1)S(1)} %pad_maximum_fusion.1), channel_id=1, source_target_pairs={{0,16},{1,5},{2,18},{3,7},{4,20},{5,1},{6,22},{7,3},{8,24},{9,13},... | collective-permute-start | bytes 811016 | tf_op jit(solution)/shard_map/ppermute | solution.py:80
  103.0 11.7 %collective-permute-start.13 = (f16[1296,128]{1,0:T(8,128)(2,1)S(1)}, f16[1296,128]{1,0:T(8,128)(2,1)S(1)}, u32[]{:S(2)}, u32[]{:S(2)}) collective-permute-start(f16[1296,128]{1,0:T(8,128)(2,1)S(1)} %convert_element_type.144), channel_id=1, source_target_pairs={{2,66},{3,67},{6,70},{7,71},{10,74},{11,75},{14,78},{15,79},{18,82... | collective-permute-start | bytes 995336 | tf_op jit(solution)/shard_map/ppermute | solution.py:80
  110.1 8.9 %collective-permute-start.20 = (f16[1040,128]{1,0:T(8,128)(2,1)S(1)}, f16[1040,128]{1,0:T(8,128)(2,1)S(1)}, u32[]{:S(2)}, u32[]{:S(2)}) collective-permute-start(f16[1040,128]{1,0:T(8,128)(2,1)S(1)} %convert_element_type.165), channel_id=1, source_target_pairs={{0,64},{1,65},{4,68},{5,69},{8,72},{9,73},{12,76},{13,77},{16,80},... | collective-permute-start | bytes 798728 | tf_op jit(solution)/shard_map/ppermute | solution.py:80
  114.8 5.4 %collective-permute-start.14 = (f32[512,128]{1,0:T(8,128)S(1)}, f32[512,128]{1,0:T(8,128)S(1)}, u32[]{:S(2)}, u32[]{:S(2)}) collective-permute-start(f32[512,128]{1,0:T(8,128)S(1)} %slice.140), channel_id=1, source_target_pairs={{1,0},{0,1},{3,2},{2,3},{5,4},{4,5},{7,6},{6,7},{9,8},{8,9},{11,10... | collective-permute-start | bytes 786440 | tf_op jit(solution)/shard_map/ppermute | solution.py:80
  121.2 13.5 %collective-permute-start.24 = (f16[528,128]{1,0:T(8,128)(2,1)S(1)}, f16[528,128]{1,0:T(8,128)(2,1)S(1)}, u32[]{:S(2)}, u32[]{:S(2)}) collective-permute-start(f16[528,128]{1,0:T(8,128)(2,1)S(1)} %convert_element_type.177), channel_id=1, source_target_pairs={{0,17},{1,48},{2,81},{3,112},{4,21},{5,52},{6,85},{7,116},{8,25},{... | collective-permute-start | bytes 405512 | tf_op jit(solution)/shard_map/ppermute | solution.py:80
  126.8 8.0 %collective-permute-start.23 = (f16[528,128]{1,0:T(8,128)(2,1)S(1)}, f16[528,128]{1,0:T(8,128)(2,1)S(1)}, u32[]{:S(2)}, u32[]{:S(2)}) collective-permute-start(f16[528,128]{1,0:T(8,128)(2,1)S(1)} %convert_element_type.174), channel_id=1, source_target_pairs={{0,1},{1,32},{2,65},{3,96},{4,5},{5,36},{6,69},{7,100},{8,9},{9,40... | collective-permute-start | bytes 405512 | tf_op jit(solution)/shard_map/ppermute | solution.py:80
  131.2 6.6 %collective-permute-start.22 = (f16[528,128]{1,0:T(8,128)(2,1)S(1)}, f16[528,128]{1,0:T(8,128)(2,1)S(1)}, u32[]{:S(2)}, u32[]{:S(2)}) collective-permute-start(f16[528,128]{1,0:T(8,128)(2,1)S(1)} %convert_element_type.171), channel_id=1, source_target_pairs={{0,16},{1,49},{2,50},{3,19},{4,20},{5,53},{6,54},{7,23},{8,24},{9,... | collective-permute-start | bytes 405512 | tf_op jit(solution)/shard_map/ppermute | solution.py:80
  131.3 10.2 %collective-permute-start.21 = (f16[528,128]{1,0:T(8,128)(2,1)S(1)}, f16[528,128]{1,0:T(8,128)(2,1)S(1)}, u32[]{:S(2)}, u32[]{:S(2)}) collective-permute-start(f16[528,128]{1,0:T(8,128)(2,1)S(1)} %convert_element_type.168), channel_id=1, source_target_pairs={{0,0},{1,33},{2,34},{3,3},{4,4},{5,37},{6,38},{7,7},{8,8},{9,41},{... | collective-permute-start | bytes 405512 | tf_op jit(solution)/shard_map/ppermute | solution.py:80

commit v6 on v5

--- a/solution.py
+++ b/solution.py
@@ -179,6 +179,38 @@
     lax.fori_loop(0, 4, step, 0)
 
 
+def early_kernel(other, scaled, out):
+    for t in range(4):
+        out[t] = product(other[...], scaled[t])
+
+
+def early_products(other, scaled):
+    columns = other.shape[1]
+    flops = 2 * 4 * columns * 512 * other.shape[0]
+    return call(early_kernel, [floats(4, columns, 512)], [], [other, scaled], flops=flops, name="early_products")[0]
+
+
+def late_kernel(place, other, scaled, early, *rest):
+    outs, total = rest[:4], rest[4]
+    rows = early.shape[1]
+    for t in range(4):
+        total[:rows] = early[t]
+        total[rows:] = product(other[...], scaled[t])
+        scatter_blocks(place, total, outs, t)
+
+
+def late_products(place, other, scaled, early):
+    return call(
+        late_kernel,
+        block_shapes(4),
+        [place],
+        [other, scaled, early],
+        [pltpu.VMEM((512, 512), jnp.float32)],
+        flops=2 * 4 * 256 * 512 * other.shape[0],
+        name="late_products",
+    )
+
+
 def far_products(place, other, scaled):
     return call(
         far_kernel,
@@ -352,15 +384,17 @@
 
     scaled, *blocks = own_products(here, frequencies, own, energy_gaps)
     near, *send = mate_products(place, other, scaled, blocks)
-    high = after(own, near)[:, 512:]
-    far1 = permute(after(high, far0), far_perm)
+    rest = after(own, near)
+    far1 = permute(after(rest[:, 512:768], far0), far_perm)
     near_sent = send_first(send, [None, None, None])
     sum0, *send = far_products(place, far0, scaled)
+    far2 = permute(after(rest[:, 768:], sum0), far_perm)
     sum0_sent = send_first(send, near_sent)
     near, send = first_sum(near, *near_sent)
     near_sent = send_second(send, [sum0_sent[0], sum0_sent[1], sum0_sent[2]])
     sum0, send0 = first_sum(sum0, *sum0_sent)
-    sum1, *send = far_products(place, far1, scaled)
+    early = early_products(far1, scaled)
+    sum1, *send = late_products(place, far2, scaled, early)
     sum1_sent = send_first(send, near_sent)
     sum1, send1 = first_sum(sum1, *sum1_sent)
     for v in near_sent:

time: 144 us -> 141 us (0.979)
  waiting for transfers between devices: 61.9 us -> 53.3 us
  starting transfers between devices: 46.6 us -> 52.9 us
    ppermute x25 -> x26, waiting for transfers between devices: 61.9 us -> 53.3 us  [permute(): return lax.ppermute(value, AXES, pairs)]
    ppermute x25 -> x26, starting transfers between devices: 46.6 us -> 52.9 us  [permute(): return lax.ppermute(value, AXES, pairs)]
    pallas_call x11 -> x12, Pallas kernels: 29.6 us -> 29.4 us  [call(): pl.pallas_call(kernel, out_shape=out_shape, in_specs=[smem] * len(scalars...]
  transfers between devices with their start and end apart: 25 -> 26, of which waited for: 12 -> 13; matrix products, arithmetic and copies ran while one was open for 2% -> 2% of each run, Pallas kernels for 18% -> 18%
where the time goes in v6:
time: 141 us
  waiting for transfers between devices  53.3 us (38%)
  starting transfers between devices  52.9 us (38%)
  Pallas kernels  29.4 us (21%)
  local copies, waits for them, and re-layouts  3.79 us (3%)
    ppermute x26, waiting for transfers between devices, permute(): return lax.ppermute(value, AXES, pairs)  53.3 us
    ppermute x26, starting transfers between devices, permute(): return lax.ppermute(value, AXES, pairs)  52.9 us
    pallas_call x12, Pallas kernels, call(): pl.pallas_call(kernel, out_shape=out_shape, in_specs=[smem] * len(scalars...  29.4 us
  transfers between devices with their start and end apart: 26, of which 13 were waited for; matrix products, arithmetic and copies ran while one was open for 2% of the time, Pallas kernels for 18%

profile of v6, /device:TPU:1, one launch (start us, length us, event | category | flops | bytes accessed | tf_op | source)
XLA Modules:
  0.0 141.1 jit_solution(4463059603773430057)
XLA Ops:
  0.0 2.8 %slice.102 = bf16[1536,512]{1,0:T(8,128)(2,1)} slice(bf16[1536,1024]{1,0:T(8,128)(2,1)} %own), slice={[0:1536], [0:512]} | slice | bytes 3145728 | tf_op jit(solution)/shard_map/slice | solution.py:380
  2.8 1.4 %collective-permute-start = (bf16[1536,1024]{1,0:T(8,128)(2,1)S(1)}, bf16[1536,1024]{1,0:T(8,128)(2,1)}, u32[]{:S(2)}, u32[]{:S(2)}) collective-permute-start(bf16[1536,1024]{1,0:T(8,128)(2,1)S(1)} %copy-done), channel_id=1, source_target_pairs={{1,0},{0,1},{3,2},{2,3},{5,4},{4,5},{7,6},{6,7},{9,8},{8,9},{11,10... | collective-permute-start | bytes 9437192 | tf_op jit(solution)/shard_map/ppermute | solution.py:80
  4.2 1.3 collective-permute-start.4
  5.6 0.7 dynamic-slice_bitcast_fusion
  6.4 7.5 %own_products.1 = (bf16[4,1536,512]{2,1,0:T(8,128)(2,1)S(1)}, f32[4,10,128,128]{3,2,1,0:T(8,128)S(1)}, bf16[4,10,128,128]{3,2,1,0:T(8,128)(2,1)S(1)}, bf16[4,10,...) custom-call(s32[5]{0:T(128)S(1)} %stack.23.place, f32[2]{0:T(128)S(1)} %copy-done.1, ...), custom_call_target="tpu_custom_call" | custom-call | flops 4831838208 | tf_op jit(solution)/shard_map/own_products/pallas_call | solution.py:86
  13.9 5.8 %mate_products.1 = (f32[4,10,128,128]{3,2,1,0:T(8,128)S(1)}, bf16[4,10,128,128]{3,2,1,0:T(8,128)(2,1)S(1)}, bf16[4,10,128,128]{3,2,1,0:T(8,128)(2,1)S(1)}, bf16[4,10,128,128]{3,2,1,0:T(8,128)(2,1)S(1)}) custom-call(s32[13]{0:T(128)S(1)} %concatenate.16.place, ...), custom_call_target="tpu_custom_call", output_to_operand_aliasing={{0}: (3, {}), {1}: (4, {}), {2}: (5, {}), {3}: (6, {})} | custom-call | flops 3221225472 | tf_op jit(solution)/shard_map/mate_products/pallas_call | solution.py:86
  19.7 3.8 %collective-permute-start.3 = (bf16[4,10,128,128]{3,2,1,0:T(8,128)(2,1)S(1)}, bf16[4,10,128,128]{3,2,1,0:T(8,128)(2,1)S(1)}, u32[]{:S(2)}, u32[]{:S(2)}) collective-permute-start(bf16[4,10,128,128]{3,2,1,0:T(8,128)(2,1)S(1)} %get-tuple-element.62), channel_id=1, source_target_pairs={{0,12},{1,49},{2,14},{3,51},{4,8},{5,53},{6,10},{7,55},{8,4},{9,57... | collective-permute-start | bytes 3932168 | tf_op jit(solution)/shard_map/ppermute | solution.py:80
  23.5 1.3 collective-permute-start.2
  24.9 15.7 %collective-permute-done.4.other = bf16[1536,512]{1,0:T(8,128)(2,1)} collective-permute-done((bf16[1536,512]{1,0:T(8,128)(2,1)}, bf16[1536,512]{1,0:T(8,128)(2,1)}, u32[]{:S(2)}, u32[]{:S(2)}) %collective-permute-start.4) | collective-permute-done | bytes 1572896 | tf_op jit(solution)/shard_map/ppermute | solution.py:80
  40.6 1.3 collective-permute-start.12
  41.9 6.0 %far_products.1 = (f32[4,4,128,128]{3,2,1,0:T(8,128)S(1)}, bf16[4,4,128,128]{3,2,1,0:T(8,128)(2,1)S(1)}, bf16[4,4,128,128]{3,2,1,0:T(8,128)(2,1)S(1)}, bf16[4,4,128,128]{3,2,1,0:T(8,128)(2,1)S(1)}) custom-call(s32[13]{0:T(128)S(1)} %concatenate.16.place, bf16[1536,512]{1,0:T(8,128)(2,1)} %collective-permute-done.4.other, ...), custom_call_target="tpu_custom_call" | custom-call | flops 3221225472 | tf_op jit(solution)/shard_map/far_products/pallas_call | solution.py:86
  47.9 1.2 collective-permute-start.11
  49.1 3.8 %collective-permute-start.9 = (bf16[4,4,128,128]{3,2,1,0:T(8,128)(2,1)S(1)}, bf16[4,4,128,128]{3,2,1,0:T(8,128)(2,1)S(1)}, u32[]{:S(2)}, u32[]{:S(2)}) collective-permute-start(bf16[4,4,128,128]{3,2,1,0:T(8,128)(2,1)S(1)} %get-tuple-element.75), channel_id=1, source_target_pairs={{0,12},{1,49},{2,14},{3,51},{4,8},{5,53},{6,10},{7,55},{8,4},{9,57... | collective-permute-start | bytes 1572872 | tf_op jit(solution)/shard_map/ppermute | solution.py:80
  52.9 1.2 collective-permute-done.2.b
  54.1 1.7 %collective-permute-start.7 = (bf16[4,4,128,128]{3,2,1,0:T(8,128)(2,1)S(1)}, bf16[4,4,128,128]{3,2,1,0:T(8,128)(2,1)S(1)}, u32[]{:S(2)}, u32[]{:S(2)}) collective-permute-start(bf16[4,4,128,128]{3,2,1,0:T(8,128)(2,1)S(1)} %get-tuple-element.71), channel_id=1, source_target_pairs={{0,8},{1,33},{2,10},{3,35},{4,12},{5,37},{6,14},{7,39},{8,0},{9,41... | collective-permute-start | bytes 1572872 | tf_op jit(solution)/shard_map/ppermute | solution.py:80
  55.8 0.9 first_sum.3
  56.8 2.9 %collective-permute-done.9.c = bf16[4,4,128,128]{3,2,1,0:T(8,128)(2,1)S(1)} collective-permute-done((bf16[4,4,128,128]{3,2,1,0:T(8,128)(2,1)S(1)}, bf16[4,4,128,128]{3,2,1,0:T(8,128)(2,1)S(1)}, u32[]{:S(2)}, u32[]{:S(2)}) %collective-permute-start.9) | collective-permute-done | bytes 524320 | tf_op jit(solution)/shard_map/ppermute | solution.py:80
  59.8 2.5 %collective-permute-start.10 = (f16[1296,128]{1,0:T(8,128)(2,1)S(1)}, f16[1296,128]{1,0:T(8,128)(2,1)S(1)}, u32[]{:S(2)}, u32[]{:S(2)}) collective-permute-start(f16[1296,128]{1,0:T(8,128)(2,1)S(1)} %convert_element_type.141), channel_id=1, source_target_pairs={{0,48},{1,13},{2,50},{3,15},{4,52},{5,9},{6,54},{7,11},{8,56},{9,5... | collective-permute-start | bytes 995336 | tf_op jit(solution)/shard_map/ppermute | solution.py:80
  62.4 4.0 %collective-permute-done.7.b = bf16[4,4,128,128]{3,2,1,0:T(8,128)(2,1)S(1)} collective-permute-done((bf16[4,4,128,128]{3,2,1,0:T(8,128)(2,1)S(1)}, bf16[4,4,128,128]{3,2,1,0:T(8,128)(2,1)S(1)}, u32[]{:S(2)}, u32[]{:S(2)}) %collective-permute-start.7) | collective-permute-done | bytes 524320 | tf_op jit(solution)/shard_map/ppermute | solution.py:80
  66.5 3.6 %collective-permute-start.8 = (f16[1296,128]{1,0:T(8,128)(2,1)S(1)}, f16[1296,128]{1,0:T(8,128)(2,1)S(1)}, u32[]{:S(2)}, u32[]{:S(2)}) collective-permute-start(f16[1296,128]{1,0:T(8,128)(2,1)S(1)} %convert_element_type.138), channel_id=1, source_target_pairs={{0,32},{1,9},{2,34},{3,11},{4,36},{5,13},{6,38},{7,15},{8,40},{9,1... | collective-permute-start | bytes 995336 | tf_op jit(solution)/shard_map/ppermute | solution.py:80
  70.0 1.8 %early_products.1.early = f32[4,256,512]{2,1,0:T(8,128)S(1)} custom-call(bf16[1536,256]{1,0:T(8,128)(2,1)S(1)} %collective-permute-done.12.other, bf16[4,1536,512]{2,1,0:T(8,128)(2,1)S(1)} %get-tuple-element.54.scaled), custom_call_target="tpu_custom_call" | custom-call | flops 1610612736 | tf_op jit(solution)/shard_map/early_products/pallas_call | solution.py:86
  71.9 4.0 %collective-permute-done.11.other = bf16[1536,256]{1,0:T(8,128)(2,1)S(1)} collective-permute-done((bf16[1536,256]{1,0:T(8,128)(2,1)S(1)}, bf16[1536,256]{1,0:T(8,128)(2,1)S(1)}, u32[]{:S(2)}, u32[]{:S(2)}) %collective-permute-start.11) | collective-permute-done | bytes 786464 | tf_op jit(solution)/shard_map/ppermute | solution.py:80
  75.9 3.1 %late_products.1 = (f32[4,4,128,128]{3,2,1,0:T(8,128)S(1)}, bf16[4,4,128,128]{3,2,1,0:T(8,128)(2,1)S(1)}, bf16[4,4,128,128]{3,2,1,0:T(8,128)(2,1)S(1)}, bf16[4,4,128,128]{3,2,1,0:T(8,128)(2,1)S(1)}) custom-call(s32[13]{0:T(128)S(1)} %concatenate.16.place, bf16[1536,256]{1,0:T(8,128)(2,1)S(1)} %collective-permute-done.11.other, ...), custom_call_target="tpu_custom_call" | custom-call | flops 1610612736 | tf_op jit(solution)/shard_map/late_products/pallas_call | solution.py:86
  79.0 0.4 first_sum.4
  79.5 3.6 %collective-permute-start.17 = (bf16[4,4,128,128]{3,2,1,0:T(8,128)(2,1)S(1)}, bf16[4,4,128,128]{3,2,1,0:T(8,128)(2,1)S(1)}, u32[]{:S(2)}, u32[]{:S(2)}) collective-permute-start(bf16[4,4,128,128]{3,2,1,0:T(8,128)(2,1)S(1)} %get-tuple-element.90), channel_id=1, source_target_pairs={{0,8},{1,33},{2,10},{3,35},{4,12},{5,37},{6,14},{7,39},{8,0},{9,41... | collective-permute-start | bytes 1572872 | tf_op jit(solution)/shard_map/ppermute | solution.py:80
  83.1 0.7 collective-permute-start.16
  83.8 0.2 multiply_add_fusion.1.value
  84.0 6.0 %collective-permute-done.17.b = bf16[4,4,128,128]{3,2,1,0:T(8,128)(2,1)S(1)} collective-permute-done((bf16[4,4,128,128]{3,2,1,0:T(8,128)(2,1)S(1)}, bf16[4,4,128,128]{3,2,1,0:T(8,128)(2,1)S(1)}, u32[]{:S(2)}, u32[]{:S(2)}) %collective-permute-start.17) | collective-permute-done | bytes 524320 | tf_op jit(solution)/shard_map/ppermute | solution.py:80
  90.0 6.3 %collective-permute-done.16.a = bf16[4,4,128,128]{3,2,1,0:T(8,128)(2,1)S(1)} collective-permute-done((bf16[4,4,128,128]{3,2,1,0:T(8,128)(2,1)S(1)}, bf16[4,4,128,128]{3,2,1,0:T(8,128)(2,1)S(1)}, u32[]{:S(2)}, u32[]{:S(2)}) %collective-permute-start.16) | collective-permute-done | bytes 524320 | tf_op jit(solution)/shard_map/ppermute | solution.py:80
  96.3 0.4 first_sum.5
  96.9 2.6 %collective-permute-start.20 = (f16[1056,128]{1,0:T(8,128)(2,1)S(1)}, f16[1056,128]{1,0:T(8,128)(2,1)S(1)}, u32[]{:S(2)}, u32[]{:S(2)}) collective-permute-start(f16[1056,128]{1,0:T(8,128)(2,1)S(1)} %pad_maximum_fusion.3), channel_id=1, source_target_pairs={{0,48},{1,13},{2,50},{3,15},{4,52},{5,9},{6,54},{7,11},{8,56},{9,5... | collective-permute-start | bytes 811016 | tf_op jit(solution)/shard_map/ppermute | solution.py:80
  99.6 0.6 collective-permute-start.19
  100.2 0.3 collective-permute-start.18
  100.6 0.2 seal.2
  100.8 1.3 collective-permute-start.14
  102.1 3.6 %collective-permute-done.20 = f16[1056,128]{1,0:T(8,128)(2,1)S(1)} collective-permute-done((f16[1056,128]{1,0:T(8,128)(2,1)S(1)}, f16[1056,128]{1,0:T(8,128)(2,1)S(1)}, u32[]{:S(2)}, u32[]{:S(2)}) %collective-permute-start.20) | collective-permute-done | bytes 270368 | tf_op jit(solution)/shard_map/ppermute | solution.py:80
  105.8 0.7 collective-permute-done.19
  106.5 1.0 collective-permute-done.18
  108.0 4.8 %collective-permute-start.21 = (f16[1040,128]{1,0:T(8,128)(2,1)S(1)}, f16[1040,128]{1,0:T(8,128)(2,1)S(1)}, u32[]{:S(2)}, u32[]{:S(2)}) collective-permute-start(f16[1040,128]{1,0:T(8,128)(2,1)S(1)} %convert_element_type.165), channel_id=1, source_target_pairs={{0,64},{1,65},{4,68},{5,69},{8,72},{9,73},{12,76},{13,77},{16,80},... | collective-permute-start | bytes 798728 | tf_op jit(solution)/shard_map/ppermute | solution.py:80
  112.9 3.6 %collective-permute-start.15 = (f32[512,128]{1,0:T(8,128)S(1)}, f32[512,128]{1,0:T(8,128)S(1)}, u32[]{:S(2)}, u32[]{:S(2)}) collective-permute-start(f32[512,128]{1,0:T(8,128)S(1)} %slice.144), channel_id=1, source_target_pairs={{1,0},{0,1},{3,2},{2,3},{5,4},{4,5},{7,6},{6,7},{9,8},{8,9},{11,10... | collective-permute-start | bytes 786440 | tf_op jit(solution)/shard_map/ppermute | solution.py:80
  116.6 1.1 collective-permute-done.15.twin
  117.7 1.0 pack.1
  118.7 5.5 %collective-permute-start.25 = (f16[528,128]{1,0:T(8,128)(2,1)S(1)}, f16[528,128]{1,0:T(8,128)(2,1)S(1)}, u32[]{:S(2)}, u32[]{:S(2)}) collective-permute-start(f16[528,128]{1,0:T(8,128)(2,1)S(1)} %convert_element_type.177), channel_id=1, source_target_pairs={{0,17},{1,48},{2,81},{3,112},{4,21},{5,52},{6,85},{7,116},{8,25},{... | collective-permute-start | bytes 405512 | tf_op jit(solution)/shard_map/ppermute | solution.py:80
  124.3 4.3 %collective-permute-start.24 = (f16[528,128]{1,0:T(8,128)(2,1)S(1)}, f16[528,128]{1,0:T(8,128)(2,1)S(1)}, u32[]{:S(2)}, u32[]{:S(2)}) collective-permute-start(f16[528,128]{1,0:T(8,128)(2,1)S(1)} %convert_element_type.174), channel_id=1, source_target_pairs={{0,1},{1,32},{2,65},{3,96},{4,5},{5,36},{6,69},{7,100},{8,9},{9,40... | collective-permute-start | bytes 405512 | tf_op jit(solution)/shard_map/ppermute | solution.py:80
  128.7 3.4 %collective-permute-start.22 = (f16[528,128]{1,0:T(8,128)(2,1)S(1)}, f16[528,128]{1,0:T(8,128)(2,1)S(1)}, u32[]{:S(2)}, u32[]{:S(2)}) collective-permute-start(f16[528,128]{1,0:T(8,128)(2,1)S(1)} %convert_element_type.168), channel_id=1, source_target_pairs={{0,0},{1,33},{2,34},{3,3},{4,4},{5,37},{6,38},{7,7},{8,8},{9,41},{... | collective-permute-start | bytes 405512 | tf_op jit(solution)/shard_map/ppermute | solution.py:80
  132.2 3.0 %collective-permute-done.23 = f16[528,128]{1,0:T(8,128)(2,1)S(1)} collective-permute-done((f16[528,128]{1,0:T(8,128)(2,1)S(1)}, f16[528,128]{1,0:T(8,128)(2,1)S(1)}, u32[]{:S(2)}, u32[]{:S(2)}) %collective-permute-start.23) | collective-permute-done | bytes 135200 | tf_op jit(solution)/shard_map/ppermute | solution.py:80
  135.2 3.7 %collective-permute-done.22 = f16[528,128]{1,0:T(8,128)(2,1)S(1)} collective-permute-done((f16[528,128]{1,0:T(8,128)(2,1)S(1)}, f16[528,128]{1,0:T(8,128)(2,1)S(1)}, u32[]{:S(2)}, u32[]{:S(2)}) %collective-permute-start.22) | collective-permute-done | bytes 135200 | tf_op jit(solution)/shard_map/ppermute | solution.py:80
  138.9 2.2 %unpack.1 = f32[128,2,1024]{2,1,0:T(2,128)} custom-call(s32[13]{0:T(128)S(1)} %concatenate.16.place, f32[512,128]{1,0:T(8,128)S(1)} %convert_multiply_fusion.3.a, f32[512,128]{1,0:T(8,128)S(1)} %convert_multiply_fusion.2.b, f32[512,128]{1,0:T(8,128)S(1)} %convert_multiply_fusion.1.c, f32[512,128]{1,0:T(8,128)S(1)} %convert_multiply_fusion.d), custom_call_target="tpu_custom_call" | custom-call | flops 262144 | tf_op jit(solution)/shard_map/unpack/pallas_call | solution.py:86
  (68 shorter events, 2.0 us)
Async XLA Ops:
  0.0 2.8 %copy-start = (bf16[1536,1024]{1,0:T(8,128)(2,1)S(1)}, bf16[1536,1024]{1,0:T(8,128)(2,1)}, u32[]{:S(2)}) copy-start(bf16[1536,1024]{1,0:T(8,128)(2,1)} %own) | copy-start | bytes 9437188
  0.0 6.4 %copy-start.2 = (f32[1536]{0:T(1024)S(1)}, f32[1536]{0:T(1024)}, u32[]{:S(2)}) copy-start(f32[1536]{0:T(1024)} %param.5) | copy-start | bytes 18436
  0.0 6.4 %copy-start.1 = (f32[2]{0:T(128)S(1)}, f32[2]{0:T(128)}, u32[]{:S(2)}) copy-start(f32[2]{0:T(128)} %frequencies.1) | copy-start | bytes 28
  2.8 11.0 %collective-permute-start = (bf16[1536,1024]{1,0:T(8,128)(2,1)S(1)}, bf16[1536,1024]{1,0:T(8,128)(2,1)}, u32[]{:S(2)}, u32[]{:S(2)}) collective-permute-start(bf16[1536,1024]{1,0:T(8,128)(2,1)S(1)} %copy-done), channel_id=1, source_target_pairs={{1,0},{0,1},{3,2},{2,3},{5,4},{4,5},{7,6},{6,7},{9,8},{8,9},{11,10... | collective-permute-start | bytes 9437192 | tf_op jit(solution)/shard_map/ppermute | solution.py:80
  4.2 36.3 %collective-permute-start.4 = (bf16[1536,512]{1,0:T(8,128)(2,1)}, bf16[1536,512]{1,0:T(8,128)(2,1)}, u32[]{:S(2)}, u32[]{:S(2)}) collective-permute-start(bf16[1536,512]{1,0:T(8,128)(2,1)} %slice.102), channel_id=1, source_target_pairs={{2,0},{3,1},{1,2},{0,3},{6,4},{7,5},{5,6},{4,7},{10,8},{11,9},{9,1... | collective-permute-start | bytes 4718600 | tf_op jit(solution)/shard_map/ppermute | solution.py:80
  19.7 29.4 %collective-permute-start.3 = (bf16[4,10,128,128]{3,2,1,0:T(8,128)(2,1)S(1)}, bf16[4,10,128,128]{3,2,1,0:T(8,128)(2,1)S(1)}, u32[]{:S(2)}, u32[]{:S(2)}) collective-permute-start(bf16[4,10,128,128]{3,2,1,0:T(8,128)(2,1)S(1)} %get-tuple-element.62), channel_id=1, source_target_pairs={{0,12},{1,49},{2,14},{3,51},{4,8},{5,53},{6,10},{7,55},{8,4},{9,57... | collective-permute-start | bytes 3932168 | tf_op jit(solution)/shard_map/ppermute | solution.py:80
  23.5 29.4 %collective-permute-start.1 = (bf16[4,10,128,128]{3,2,1,0:T(8,128)(2,1)S(1)}, bf16[4,10,128,128]{3,2,1,0:T(8,128)(2,1)S(1)}, u32[]{:S(2)}, u32[]{:S(2)}) collective-permute-start(bf16[4,10,128,128]{3,2,1,0:T(8,128)(2,1)S(1)} %get-tuple-element.60), channel_id=1, source_target_pairs={{0,4},{1,17},{2,6},{3,19},{4,0},{5,21},{6,2},{7,23},{8,12},{9,25},... | collective-permute-start | bytes 3932168 | tf_op jit(solution)/shard_map/ppermute | solution.py:80
  23.5 30.6 %collective-permute-start.2 = (bf16[4,10,128,128]{3,2,1,0:T(8,128)(2,1)S(1)}, bf16[4,10,128,128]{3,2,1,0:T(8,128)(2,1)S(1)}, u32[]{:S(2)}, u32[]{:S(2)}) collective-permute-start(bf16[4,10,128,128]{3,2,1,0:T(8,128)(2,1)S(1)} %get-tuple-element.61), channel_id=1, source_target_pairs={{0,8},{1,33},{2,10},{3,35},{4,12},{5,37},{6,14},{7,39},{8,0},{9,41... | collective-permute-start | bytes 3932168 | tf_op jit(solution)/shard_map/ppermute | solution.py:80
  40.6 29.5 %collective-permute-start.12 = (bf16[1536,256]{1,0:T(8,128)(2,1)S(1)}, bf16[1536,256]{1,0:T(8,128)(2,1)S(1)}, u32[]{:S(2)}, u32[]{:S(2)}) collective-permute-start(bf16[1536,256]{1,0:T(8,128)(2,1)S(1)} %get-tuple-element.80), channel_id=1, source_target_pairs={{2,0},{3,1},{1,2},{0,3},{6,4},{7,5},{5,6},{4,7},{10,8},{11,9},{9,1... | collective-permute-start | bytes 2359304 | tf_op jit(solution)/shard_map/ppermute | solution.py:80
  47.9 28.1 %collective-permute-start.11 = (bf16[1536,256]{1,0:T(8,128)(2,1)S(1)}, bf16[1536,256]{1,0:T(8,128)(2,1)S(1)}, u32[]{:S(2)}, u32[]{:S(2)}) collective-permute-start(bf16[1536,256]{1,0:T(8,128)(2,1)S(1)} %get-tuple-element.79), channel_id=1, source_target_pairs={{2,0},{3,1},{1,2},{0,3},{6,4},{7,5},{5,6},{4,7},{10,8},{11,9},{9,1... | collective-permute-start | bytes 2359304 | tf_op jit(solution)/shard_map/ppermute | solution.py:80
  49.1 10.7 %collective-permute-start.9 = (bf16[4,4,128,128]{3,2,1,0:T(8,128)(2,1)S(1)}, bf16[4,4,128,128]{3,2,1,0:T(8,128)(2,1)S(1)}, u32[]{:S(2)}, u32[]{:S(2)}) collective-permute-start(bf16[4,4,128,128]{3,2,1,0:T(8,128)(2,1)S(1)} %get-tuple-element.75), channel_id=1, source_target_pairs={{0,12},{1,49},{2,14},{3,51},{4,8},{5,53},{6,10},{7,55},{8,4},{9,57... | collective-permute-start | bytes 1572872 | tf_op jit(solution)/shard_map/ppermute | solution.py:80
  52.9 9.3 %collective-permute-start.5 = (bf16[4,4,128,128]{3,2,1,0:T(8,128)(2,1)S(1)}, bf16[4,4,128,128]{3,2,1,0:T(8,128)(2,1)S(1)}, u32[]{:S(2)}, u32[]{:S(2)}) collective-permute-start(bf16[4,4,128,128]{3,2,1,0:T(8,128)(2,1)S(1)} %get-tuple-element.67), channel_id=1, source_target_pairs={{0,4},{1,17},{2,6},{3,19},{4,0},{5,21},{6,2},{7,23},{8,12},{9,25},... | collective-permute-start | bytes 1572872 | tf_op jit(solution)/shard_map/ppermute | solution.py:80
  54.1 12.3 %collective-permute-start.7 = (bf16[4,4,128,128]{3,2,1,0:T(8,128)(2,1)S(1)}, bf16[4,4,128,128]{3,2,1,0:T(8,128)(2,1)S(1)}, u32[]{:S(2)}, u32[]{:S(2)}) collective-permute-start(bf16[4,4,128,128]{3,2,1,0:T(8,128)(2,1)S(1)} %get-tuple-element.71), channel_id=1, source_target_pairs={{0,8},{1,33},{2,10},{3,35},{4,12},{5,37},{6,14},{7,39},{8,0},{9,41... | collective-permute-start | bytes 1572872 | tf_op jit(solution)/shard_map/ppermute | solution.py:80
  59.8 19.7 %collective-permute-start.10 = (f16[1296,128]{1,0:T(8,128)(2,1)S(1)}, f16[1296,128]{1,0:T(8,128)(2,1)S(1)}, u32[]{:S(2)}, u32[]{:S(2)}) collective-permute-start(f16[1296,128]{1,0:T(8,128)(2,1)S(1)} %convert_element_type.141), channel_id=1, source_target_pairs={{0,48},{1,13},{2,50},{3,15},{4,52},{5,9},{6,54},{7,11},{8,56},{9,5... | collective-permute-start | bytes 995336 | tf_op jit(solution)/shard_map/ppermute | solution.py:80
  62.3 17.2 %collective-permute-start.6 = (f16[1296,128]{1,0:T(8,128)(2,1)S(1)}, f16[1296,128]{1,0:T(8,128)(2,1)S(1)}, u32[]{:S(2)}, u32[]{:S(2)}) collective-permute-start(f16[1296,128]{1,0:T(8,128)(2,1)S(1)} %convert_element_type.135), channel_id=1, source_target_pairs={{0,16},{1,5},{2,18},{3,7},{4,20},{5,1},{6,22},{7,3},{8,24},{9,13},... | collective-permute-start | bytes 995336 | tf_op jit(solution)/shard_map/ppermute | solution.py:80
  66.5 13.0 %collective-permute-start.8 = (f16[1296,128]{1,0:T(8,128)(2,1)S(1)}, f16[1296,128]{1,0:T(8,128)(2,1)S(1)}, u32[]{:S(2)}, u32[]{:S(2)}) collective-permute-start(f16[1296,128]{1,0:T(8,128)(2,1)S(1)} %convert_element_type.138), channel_id=1, source_target_pairs={{0,32},{1,9},{2,34},{3,11},{4,36},{5,13},{6,38},{7,15},{8,40},{9,1... | collective-permute-start | bytes 995336 | tf_op jit(solution)/shard_map/ppermute | solution.py:80
  79.5 10.5 %collective-permute-start.17 = (bf16[4,4,128,128]{3,2,1,0:T(8,128)(2,1)S(1)}, bf16[4,4,128,128]{3,2,1,0:T(8,128)(2,1)S(1)}, u32[]{:S(2)}, u32[]{:S(2)}) collective-permute-start(bf16[4,4,128,128]{3,2,1,0:T(8,128)(2,1)S(1)} %get-tuple-element.90), channel_id=1, source_target_pairs={{0,8},{1,33},{2,10},{3,35},{4,12},{5,37},{6,14},{7,39},{8,0},{9,41... | collective-permute-start | bytes 1572872 | tf_op jit(solution)/shard_map/ppermute | solution.py:80
  83.1 13.2 %collective-permute-start.16 = (bf16[4,4,128,128]{3,2,1,0:T(8,128)(2,1)S(1)}, bf16[4,4,128,128]{3,2,1,0:T(8,128)(2,1)S(1)}, u32[]{:S(2)}, u32[]{:S(2)}) collective-permute-start(bf16[4,4,128,128]{3,2,1,0:T(8,128)(2,1)S(1)} %get-tuple-element.88), channel_id=1, source_target_pairs={{0,4},{1,17},{2,6},{3,19},{4,0},{5,21},{6,2},{7,23},{8,12},{9,25},... | collective-permute-start | bytes 1572872 | tf_op jit(solution)/shard_map/ppermute | solution.py:80
  83.8 12.5 %collective-permute-start.13 = (bf16[4,4,128,128]{3,2,1,0:T(8,128)(2,1)S(1)}, bf16[4,4,128,128]{3,2,1,0:T(8,128)(2,1)S(1)}, u32[]{:S(2)}, u32[]{:S(2)}) collective-permute-start(bf16[4,4,128,128]{3,2,1,0:T(8,128)(2,1)S(1)} %get-tuple-element.82), channel_id=1, source_target_pairs={{0,12},{1,49},{2,14},{3,51},{4,8},{5,53},{6,10},{7,55},{8,4},{9,57... | collective-permute-start | bytes 1572872 | tf_op jit(solution)/shard_map/ppermute | solution.py:80
  96.9 8.9 %collective-permute-start.20 = (f16[1056,128]{1,0:T(8,128)(2,1)S(1)}, f16[1056,128]{1,0:T(8,128)(2,1)S(1)}, u32[]{:S(2)}, u32[]{:S(2)}) collective-permute-start(f16[1056,128]{1,0:T(8,128)(2,1)S(1)} %pad_maximum_fusion.3), channel_id=1, source_target_pairs={{0,48},{1,13},{2,50},{3,15},{4,52},{5,9},{6,54},{7,11},{8,56},{9,5... | collective-permute-start | bytes 811016 | tf_op jit(solution)/shard_map/ppermute | solution.py:80
  99.6 6.9 %collective-permute-start.19 = (f16[1056,128]{1,0:T(8,128)(2,1)S(1)}, f16[1056,128]{1,0:T(8,128)(2,1)S(1)}, u32[]{:S(2)}, u32[]{:S(2)}) collective-permute-start(f16[1056,128]{1,0:T(8,128)(2,1)S(1)} %pad_maximum_fusion.2), channel_id=1, source_target_pairs={{0,32},{1,9},{2,34},{3,11},{4,36},{5,13},{6,38},{7,15},{8,40},{9,1... | collective-permute-start | bytes 811016 | tf_op jit(solution)/shard_map/ppermute | solution.py:80
  100.2 7.3 %collective-permute-start.18 = (f16[1056,128]{1,0:T(8,128)(2,1)S(1)}, f16[1056,128]{1,0:T(8,128)(2,1)S(1)}, u32[]{:S(2)}, u32[]{:S(2)}) collective-permute-start(f16[1056,128]{1,0:T(8,128)(2,1)S(1)} %pad_maximum_fusion.1), channel_id=1, source_target_pairs={{0,16},{1,5},{2,18},{3,7},{4,20},{5,1},{6,22},{7,3},{8,24},{9,13},... | collective-permute-start | bytes 811016 | tf_op jit(solution)/shard_map/ppermute | solution.py:80
  100.8 12.0 %collective-permute-start.14 = (f16[1296,128]{1,0:T(8,128)(2,1)S(1)}, f16[1296,128]{1,0:T(8,128)(2,1)S(1)}, u32[]{:S(2)}, u32[]{:S(2)}) collective-permute-start(f16[1296,128]{1,0:T(8,128)(2,1)S(1)} %convert_element_type.144), channel_id=1, source_target_pairs={{2,66},{3,67},{6,70},{7,71},{10,74},{11,75},{14,78},{15,79},{18,82... | collective-permute-start | bytes 995336 | tf_op jit(solution)/shard_map/ppermute | solution.py:80
  108.0 8.5 %collective-permute-start.21 = (f16[1040,128]{1,0:T(8,128)(2,1)S(1)}, f16[1040,128]{1,0:T(8,128)(2,1)S(1)}, u32[]{:S(2)}, u32[]{:S(2)}) collective-permute-start(f16[1040,128]{1,0:T(8,128)(2,1)S(1)} %convert_element_type.165), channel_id=1, source_target_pairs={{0,64},{1,65},{4,68},{5,69},{8,72},{9,73},{12,76},{13,77},{16,80},... | collective-permute-start | bytes 798728 | tf_op jit(solution)/shard_map/ppermute | solution.py:80
  112.9 4.7 %collective-permute-start.15 = (f32[512,128]{1,0:T(8,128)S(1)}, f32[512,128]{1,0:T(8,128)S(1)}, u32[]{:S(2)}, u32[]{:S(2)}) collective-permute-start(f32[512,128]{1,0:T(8,128)S(1)} %slice.144), channel_id=1, source_target_pairs={{1,0},{0,1},{3,2},{2,3},{5,4},{4,5},{7,6},{6,7},{9,8},{8,9},{11,10... | collective-permute-start | bytes 786440 | tf_op jit(solution)/shard_map/ppermute | solution.py:80
  118.7 13.4 %collective-permute-start.25 = (f16[528,128]{1,0:T(8,128)(2,1)S(1)}, f16[528,128]{1,0:T(8,128)(2,1)S(1)}, u32[]{:S(2)}, u32[]{:S(2)}) collective-permute-start(f16[528,128]{1,0:T(8,128)(2,1)S(1)} %convert_element_type.177), channel_id=1, source_target_pairs={{0,17},{1,48},{2,81},{3,112},{4,21},{5,52},{6,85},{7,116},{8,25},{... | collective-permute-start | bytes 405512 | tf_op jit(solution)/shard_map/ppermute | solution.py:80
  124.3 7.9 %collective-permute-start.24 = (f16[528,128]{1,0:T(8,128)(2,1)S(1)}, f16[528,128]{1,0:T(8,128)(2,1)S(1)}, u32[]{:S(2)}, u32[]{:S(2)}) collective-permute-start(f16[528,128]{1,0:T(8,128)(2,1)S(1)} %convert_element_type.174), channel_id=1, source_target_pairs={{0,1},{1,32},{2,65},{3,96},{4,5},{5,36},{6,69},{7,100},{8,9},{9,40... | collective-permute-start | bytes 405512 | tf_op jit(solution)/shard_map/ppermute | solution.py:80
  128.6 6.6 %collective-permute-start.23 = (f16[528,128]{1,0:T(8,128)(2,1)S(1)}, f16[528,128]{1,0:T(8,128)(2,1)S(1)}, u32[]{:S(2)}, u32[]{:S(2)}) collective-permute-start(f16[528,128]{1,0:T(8,128)(2,1)S(1)} %convert_element_type.171), channel_id=1, source_target_pairs={{0,16},{1,49},{2,50},{3,19},{4,20},{5,53},{6,54},{7,23},{8,24},{9,... | collective-permute-start | bytes 405512 | tf_op jit(solution)/shard_map/ppermute | solution.py:80
  128.7 10.2 %collective-permute-start.22 = (f16[528,128]{1,0:T(8,128)(2,1)S(1)}, f16[528,128]{1,0:T(8,128)(2,1)S(1)}, u32[]{:S(2)}, u32[]{:S(2)}) collective-permute-start(f16[528,128]{1,0:T(8,128)(2,1)S(1)} %convert_element_type.168), channel_id=1, source_target_pairs={{0,0},{1,33},{2,34},{3,3},{4,4},{5,37},{6,38},{7,7},{8,8},{9,41},{... | collective-permute-start | bytes 405512 | tf_op jit(solution)/shard_map/ppermute | solution.py:80

commit v7 on v6

--- a/solution.py
+++ b/solution.py
@@ -68,7 +68,7 @@
     for k in range(4):
         pairs = []
         for d in range(128):
-            sent[k, d] = ((d >> 4) & 3) ^ k
+            sent[k, d] = (0, 1, 3, 2)[((d >> 4) & 3) ^ k]
             to, slot = messages(d)[sent[k, d]]
             filled[k, to] = slot
             pairs.append((d, to))

time: 141 us -> 141 us (level); the launches traced: 141 us -> 139 us
  starting transfers between devices: 52.9 us -> 51.4 us
    ppermute x26, starting transfers between devices: 52.9 us -> 51.4 us  [permute(): return lax.ppermute(value, AXES, pairs)]
  transfers between devices with their start and end apart: 26 -> 26, of which waited for: 13 -> 14; matrix products, arithmetic and copies ran while one was open for 2% -> 2% of each run, Pallas kernels for 18% -> 19%
where the time goes in v7:
time: 141 us; the launch traced here: 139 us
  waiting for transfers between devices  52.3 us (37%)
  starting transfers between devices  51.4 us (36%)
  Pallas kernels  29.4 us (21%)
  local copies, waits for them, and re-layouts  3.79 us (3%)
    ppermute x26, waiting for transfers between devices, permute(): return lax.ppermute(value, AXES, pairs)  52.3 us
    ppermute x26, starting transfers between devices, permute(): return lax.ppermute(value, AXES, pairs)  51.4 us
    pallas_call x12, Pallas kernels, call(): pl.pallas_call(kernel, out_shape=out_shape, in_specs=[smem] * len(scalars...  29.4 us
  transfers between devices with their start and end apart: 26, of which 14 were waited for; matrix products, arithmetic and copies ran while one was open for 2% of the time, Pallas kernels for 19%

profile of v7, /device:TPU:1, one launch (start us, length us, event | category | flops | bytes accessed | tf_op | source)
XLA Modules:
  0.0 138.7 jit_solution(8791594486538157463)
XLA Ops:
  0.0 2.8 %slice.102 = bf16[1536,512]{1,0:T(8,128)(2,1)} slice(bf16[1536,1024]{1,0:T(8,128)(2,1)} %own), slice={[0:1536], [0:512]} | slice | bytes 3145728 | tf_op jit(solution)/shard_map/slice | solution.py:380
  2.8 1.4 %collective-permute-start = (bf16[1536,1024]{1,0:T(8,128)(2,1)S(1)}, bf16[1536,1024]{1,0:T(8,128)(2,1)}, u32[]{:S(2)}, u32[]{:S(2)}) collective-permute-start(bf16[1536,1024]{1,0:T(8,128)(2,1)S(1)} %copy-done), channel_id=1, source_target_pairs={{1,0},{0,1},{3,2},{2,3},{5,4},{4,5},{7,6},{6,7},{9,8},{8,9},{11,10... | collective-permute-start | bytes 9437192 | tf_op jit(solution)/shard_map/ppermute | solution.py:80
  4.2 1.3 collective-permute-start.4
  5.6 0.7 dynamic-slice_bitcast_fusion
  6.4 7.5 %own_products.1 = (bf16[4,1536,512]{2,1,0:T(8,128)(2,1)S(1)}, f32[4,10,128,128]{3,2,1,0:T(8,128)S(1)}, bf16[4,10,128,128]{3,2,1,0:T(8,128)(2,1)S(1)}, bf16[4,10,...) custom-call(s32[5]{0:T(128)S(1)} %stack.23.place, f32[2]{0:T(128)S(1)} %copy-done.1, ...), custom_call_target="tpu_custom_call" | custom-call | flops 4831838208 | tf_op jit(solution)/shard_map/own_products/pallas_call | solution.py:86
  13.9 5.8 %mate_products.1 = (f32[4,10,128,128]{3,2,1,0:T(8,128)S(1)}, bf16[4,10,128,128]{3,2,1,0:T(8,128)(2,1)S(1)}, bf16[4,10,128,128]{3,2,1,0:T(8,128)(2,1)S(1)}, bf16[4,10,128,128]{3,2,1,0:T(8,128)(2,1)S(1)}) custom-call(s32[13]{0:T(128)S(1)} %concatenate.16.place, ...), custom_call_target="tpu_custom_call", output_to_operand_aliasing={{0}: (3, {}), {1}: (4, {}), {2}: (5, {}), {3}: (6, {})} | custom-call | flops 3221225472 | tf_op jit(solution)/shard_map/mate_products/pallas_call | solution.py:86
  19.7 3.8 %collective-permute-start.3 = (bf16[4,10,128,128]{3,2,1,0:T(8,128)(2,1)S(1)}, bf16[4,10,128,128]{3,2,1,0:T(8,128)(2,1)S(1)}, u32[]{:S(2)}, u32[]{:S(2)}) collective-permute-start(bf16[4,10,128,128]{3,2,1,0:T(8,128)(2,1)S(1)} %get-tuple-element.62), channel_id=1, source_target_pairs={{0,12},{1,49},{2,14},{3,51},{4,8},{5,53},{6,10},{7,55},{8,4},{9,57... | collective-permute-start | bytes 3932168 | tf_op jit(solution)/shard_map/ppermute | solution.py:80
  23.5 1.3 collective-permute-start.2
  24.9 15.7 %collective-permute-done.4.other = bf16[1536,512]{1,0:T(8,128)(2,1)} collective-permute-done((bf16[1536,512]{1,0:T(8,128)(2,1)}, bf16[1536,512]{1,0:T(8,128)(2,1)}, u32[]{:S(2)}, u32[]{:S(2)}) %collective-permute-start.4) | collective-permute-done | bytes 1572896 | tf_op jit(solution)/shard_map/ppermute | solution.py:80
  40.6 1.3 collective-permute-start.12
  41.9 6.0 %far_products.1 = (f32[4,4,128,128]{3,2,1,0:T(8,128)S(1)}, bf16[4,4,128,128]{3,2,1,0:T(8,128)(2,1)S(1)}, bf16[4,4,128,128]{3,2,1,0:T(8,128)(2,1)S(1)}, bf16[4,4,128,128]{3,2,1,0:T(8,128)(2,1)S(1)}) custom-call(s32[13]{0:T(128)S(1)} %concatenate.16.place, bf16[1536,512]{1,0:T(8,128)(2,1)} %collective-permute-done.4.other, ...), custom_call_target="tpu_custom_call" | custom-call | flops 3221225472 | tf_op jit(solution)/shard_map/far_products/pallas_call | solution.py:86
  47.9 1.2 collective-permute-start.11
  49.1 3.8 %collective-permute-start.9 = (bf16[4,4,128,128]{3,2,1,0:T(8,128)(2,1)S(1)}, bf16[4,4,128,128]{3,2,1,0:T(8,128)(2,1)S(1)}, u32[]{:S(2)}, u32[]{:S(2)}) collective-permute-start(bf16[4,4,128,128]{3,2,1,0:T(8,128)(2,1)S(1)} %get-tuple-element.75), channel_id=1, source_target_pairs={{0,12},{1,49},{2,14},{3,51},{4,8},{5,53},{6,10},{7,55},{8,4},{9,57... | collective-permute-start | bytes 1572872 | tf_op jit(solution)/shard_map/ppermute | solution.py:80
  52.9 1.2 collective-permute-done.2.b
  54.1 1.7 %collective-permute-start.7 = (bf16[4,4,128,128]{3,2,1,0:T(8,128)(2,1)S(1)}, bf16[4,4,128,128]{3,2,1,0:T(8,128)(2,1)S(1)}, u32[]{:S(2)}, u32[]{:S(2)}) collective-permute-start(bf16[4,4,128,128]{3,2,1,0:T(8,128)(2,1)S(1)} %get-tuple-element.71), channel_id=1, source_target_pairs={{0,8},{1,33},{2,10},{3,35},{4,12},{5,37},{6,14},{7,39},{8,0},{9,41... | collective-permute-start | bytes 1572872 | tf_op jit(solution)/shard_map/ppermute | solution.py:80
  55.8 0.9 first_sum.3
  56.8 2.9 %collective-permute-done.9.c = bf16[4,4,128,128]{3,2,1,0:T(8,128)(2,1)S(1)} collective-permute-done((bf16[4,4,128,128]{3,2,1,0:T(8,128)(2,1)S(1)}, bf16[4,4,128,128]{3,2,1,0:T(8,128)(2,1)S(1)}, u32[]{:S(2)}, u32[]{:S(2)}) %collective-permute-start.9) | collective-permute-done | bytes 524320 | tf_op jit(solution)/shard_map/ppermute | solution.py:80
  59.8 2.5 %collective-permute-start.10 = (f16[1296,128]{1,0:T(8,128)(2,1)S(1)}, f16[1296,128]{1,0:T(8,128)(2,1)S(1)}, u32[]{:S(2)}, u32[]{:S(2)}) collective-permute-start(f16[1296,128]{1,0:T(8,128)(2,1)S(1)} %convert_element_type.141), channel_id=1, source_target_pairs={{0,48},{1,13},{2,50},{3,15},{4,52},{5,9},{6,54},{7,11},{8,56},{9,5... | collective-permute-start | bytes 995336 | tf_op jit(solution)/shard_map/ppermute | solution.py:80
  62.4 4.0 %collective-permute-done.7.b = bf16[4,4,128,128]{3,2,1,0:T(8,128)(2,1)S(1)} collective-permute-done((bf16[4,4,128,128]{3,2,1,0:T(8,128)(2,1)S(1)}, bf16[4,4,128,128]{3,2,1,0:T(8,128)(2,1)S(1)}, u32[]{:S(2)}, u32[]{:S(2)}) %collective-permute-start.7) | collective-permute-done | bytes 524320 | tf_op jit(solution)/shard_map/ppermute | solution.py:80
  66.5 3.6 %collective-permute-start.8 = (f16[1296,128]{1,0:T(8,128)(2,1)S(1)}, f16[1296,128]{1,0:T(8,128)(2,1)S(1)}, u32[]{:S(2)}, u32[]{:S(2)}) collective-permute-start(f16[1296,128]{1,0:T(8,128)(2,1)S(1)} %convert_element_type.138), channel_id=1, source_target_pairs={{0,32},{1,9},{2,34},{3,11},{4,36},{5,13},{6,38},{7,15},{8,40},{9,1... | collective-permute-start | bytes 995336 | tf_op jit(solution)/shard_map/ppermute | solution.py:80
  70.0 1.8 %early_products.1.early = f32[4,256,512]{2,1,0:T(8,128)S(1)} custom-call(bf16[1536,256]{1,0:T(8,128)(2,1)S(1)} %collective-permute-done.12.other, bf16[4,1536,512]{2,1,0:T(8,128)(2,1)S(1)} %get-tuple-element.54.scaled), custom_call_target="tpu_custom_call" | custom-call | flops 1610612736 | tf_op jit(solution)/shard_map/early_products/pallas_call | solution.py:86
  71.9 4.0 %collective-permute-done.11.other = bf16[1536,256]{1,0:T(8,128)(2,1)S(1)} collective-permute-done((bf16[1536,256]{1,0:T(8,128)(2,1)S(1)}, bf16[1536,256]{1,0:T(8,128)(2,1)S(1)}, u32[]{:S(2)}, u32[]{:S(2)}) %collective-permute-start.11) | collective-permute-done | bytes 786464 | tf_op jit(solution)/shard_map/ppermute | solution.py:80
  75.9 3.1 %late_products.1 = (f32[4,4,128,128]{3,2,1,0:T(8,128)S(1)}, bf16[4,4,128,128]{3,2,1,0:T(8,128)(2,1)S(1)}, bf16[4,4,128,128]{3,2,1,0:T(8,128)(2,1)S(1)}, bf16[4,4,128,128]{3,2,1,0:T(8,128)(2,1)S(1)}) custom-call(s32[13]{0:T(128)S(1)} %concatenate.16.place, bf16[1536,256]{1,0:T(8,128)(2,1)S(1)} %collective-permute-done.11.other, ...), custom_call_target="tpu_custom_call" | custom-call | flops 1610612736 | tf_op jit(solution)/shard_map/late_products/pallas_call | solution.py:86
  79.0 0.4 first_sum.4
  79.5 3.6 %collective-permute-start.17 = (bf16[4,4,128,128]{3,2,1,0:T(8,128)(2,1)S(1)}, bf16[4,4,128,128]{3,2,1,0:T(8,128)(2,1)S(1)}, u32[]{:S(2)}, u32[]{:S(2)}) collective-permute-start(bf16[4,4,128,128]{3,2,1,0:T(8,128)(2,1)S(1)} %get-tuple-element.90), channel_id=1, source_target_pairs={{0,8},{1,33},{2,10},{3,35},{4,12},{5,37},{6,14},{7,39},{8,0},{9,41... | collective-permute-start | bytes 1572872 | tf_op jit(solution)/shard_map/ppermute | solution.py:80
  83.1 0.7 collective-permute-start.16
  83.8 0.2 multiply_add_fusion.1.value
  84.0 6.0 %collective-permute-done.17.b = bf16[4,4,128,128]{3,2,1,0:T(8,128)(2,1)S(1)} collective-permute-done((bf16[4,4,128,128]{3,2,1,0:T(8,128)(2,1)S(1)}, bf16[4,4,128,128]{3,2,1,0:T(8,128)(2,1)S(1)}, u32[]{:S(2)}, u32[]{:S(2)}) %collective-permute-start.17) | collective-permute-done | bytes 524320 | tf_op jit(solution)/shard_map/ppermute | solution.py:80
  90.0 6.3 %collective-permute-done.16.a = bf16[4,4,128,128]{3,2,1,0:T(8,128)(2,1)S(1)} collective-permute-done((bf16[4,4,128,128]{3,2,1,0:T(8,128)(2,1)S(1)}, bf16[4,4,128,128]{3,2,1,0:T(8,128)(2,1)S(1)}, u32[]{:S(2)}, u32[]{:S(2)}) %collective-permute-start.16) | collective-permute-done | bytes 524320 | tf_op jit(solution)/shard_map/ppermute | solution.py:80
  96.3 0.4 first_sum.5
  96.9 2.6 %collective-permute-start.20 = (f16[1056,128]{1,0:T(8,128)(2,1)S(1)}, f16[1056,128]{1,0:T(8,128)(2,1)S(1)}, u32[]{:S(2)}, u32[]{:S(2)}) collective-permute-start(f16[1056,128]{1,0:T(8,128)(2,1)S(1)} %pad_maximum_fusion.3), channel_id=1, source_target_pairs={{0,48},{1,13},{2,50},{3,15},{4,52},{5,9},{6,54},{7,11},{8,56},{9,5... | collective-permute-start | bytes 811016 | tf_op jit(solution)/shard_map/ppermute | solution.py:80
  99.6 0.6 collective-permute-start.19
  100.2 0.3 collective-permute-start.18
  100.8 1.3 collective-permute-start.14
  102.1 3.6 %collective-permute-done.20 = f16[1056,128]{1,0:T(8,128)(2,1)S(1)} collective-permute-done((f16[1056,128]{1,0:T(8,128)(2,1)S(1)}, f16[1056,128]{1,0:T(8,128)(2,1)S(1)}, u32[]{:S(2)}, u32[]{:S(2)}) %collective-permute-start.20) | collective-permute-done | bytes 270368 | tf_op jit(solution)/shard_map/ppermute | solution.py:80
  105.8 0.7 collective-permute-done.19
  106.5 1.0 collective-permute-done.18
  108.0 4.8 %collective-permute-start.21 = (f16[1040,128]{1,0:T(8,128)(2,1)S(1)}, f16[1040,128]{1,0:T(8,128)(2,1)S(1)}, u32[]{:S(2)}, u32[]{:S(2)}) collective-permute-start(f16[1040,128]{1,0:T(8,128)(2,1)S(1)} %convert_element_type.165), channel_id=1, source_target_pairs={{0,64},{1,65},{4,68},{5,69},{8,72},{9,73},{12,76},{13,77},{16,80},... | collective-permute-start | bytes 798728 | tf_op jit(solution)/shard_map/ppermute | solution.py:80
  112.9 3.6 %collective-permute-start.15 = (f32[512,128]{1,0:T(8,128)S(1)}, f32[512,128]{1,0:T(8,128)S(1)}, u32[]{:S(2)}, u32[]{:S(2)}) collective-permute-start(f32[512,128]{1,0:T(8,128)S(1)} %slice.144), channel_id=1, source_target_pairs={{1,0},{0,1},{3,2},{2,3},{5,4},{4,5},{7,6},{6,7},{9,8},{8,9},{11,10... | collective-permute-start | bytes 786440 | tf_op jit(solution)/shard_map/ppermute | solution.py:80
  116.6 1.1 collective-permute-done.15.twin
  117.7 1.0 pack.1
  118.7 5.3 %collective-permute-start.25 = (f16[528,128]{1,0:T(8,128)(2,1)S(1)}, f16[528,128]{1,0:T(8,128)(2,1)S(1)}, u32[]{:S(2)}, u32[]{:S(2)}) collective-permute-start(f16[528,128]{1,0:T(8,128)(2,1)S(1)} %convert_element_type.177), channel_id=1, source_target_pairs={{0,1},{1,32},{2,65},{3,96},{4,5},{5,36},{6,69},{7,100},{8,9},{9,40... | collective-permute-start | bytes 405512 | tf_op jit(solution)/shard_map/ppermute | solution.py:80
  124.1 2.2 %collective-permute-start.24 = (f16[528,128]{1,0:T(8,128)(2,1)S(1)}, f16[528,128]{1,0:T(8,128)(2,1)S(1)}, u32[]{:S(2)}, u32[]{:S(2)}) collective-permute-start(f16[528,128]{1,0:T(8,128)(2,1)S(1)} %convert_element_type.174), channel_id=1, source_target_pairs={{0,17},{1,48},{2,81},{3,112},{4,21},{5,52},{6,85},{7,116},{8,25},{... | collective-permute-start | bytes 405512 | tf_op jit(solution)/shard_map/ppermute | solution.py:80
  126.3 4.3 %collective-permute-start.22 = (f16[528,128]{1,0:T(8,128)(2,1)S(1)}, f16[528,128]{1,0:T(8,128)(2,1)S(1)}, u32[]{:S(2)}, u32[]{:S(2)}) collective-permute-start(f16[528,128]{1,0:T(8,128)(2,1)S(1)} %convert_element_type.168), channel_id=1, source_target_pairs={{0,0},{1,33},{2,34},{3,3},{4,4},{5,37},{6,38},{7,7},{8,8},{9,41},{... | collective-permute-start | bytes 405512 | tf_op jit(solution)/shard_map/ppermute | solution.py:80
  130.7 2.5 %collective-permute-done.24 = f16[528,128]{1,0:T(8,128)(2,1)S(1)} collective-permute-done((f16[528,128]{1,0:T(8,128)(2,1)S(1)}, f16[528,128]{1,0:T(8,128)(2,1)S(1)}, u32[]{:S(2)}, u32[]{:S(2)}) %collective-permute-start.24) | collective-permute-done | bytes 135200 | tf_op jit(solution)/shard_map/ppermute | solution.py:80
  133.2 1.4 %collective-permute-done.23 = f16[528,128]{1,0:T(8,128)(2,1)S(1)} collective-permute-done((f16[528,128]{1,0:T(8,128)(2,1)S(1)}, f16[528,128]{1,0:T(8,128)(2,1)S(1)}, u32[]{:S(2)}, u32[]{:S(2)}) %collective-permute-start.23) | collective-permute-done | bytes 135200 | tf_op jit(solution)/shard_map/ppermute | solution.py:80
  134.7 1.8 %collective-permute-done.22 = f16[528,128]{1,0:T(8,128)(2,1)S(1)} collective-permute-done((f16[528,128]{1,0:T(8,128)(2,1)S(1)}, f16[528,128]{1,0:T(8,128)(2,1)S(1)}, u32[]{:S(2)}, u32[]{:S(2)}) %collective-permute-start.22) | collective-permute-done | bytes 135200 | tf_op jit(solution)/shard_map/ppermute | solution.py:80
  136.5 2.2 %unpack.1 = f32[128,2,1024]{2,1,0:T(2,128)} custom-call(s32[13]{0:T(128)S(1)} %concatenate.16.place, f32[512,128]{1,0:T(8,128)S(1)} %convert_multiply_fusion.3.a, f32[512,128]{1,0:T(8,128)S(1)} %convert_multiply_fusion.2.b, f32[512,128]{1,0:T(8,128)S(1)} %convert_multiply_fusion.1.c, f32[512,128]{1,0:T(8,128)S(1)} %convert_multiply_fusion.d), custom_call_target="tpu_custom_call" | custom-call | flops 262144 | tf_op jit(solution)/shard_map/unpack/pallas_call | solution.py:86
  (68 shorter events, 2.2 us)
Async XLA Ops:
  0.0 2.8 %copy-start = (bf16[1536,1024]{1,0:T(8,128)(2,1)S(1)}, bf16[1536,1024]{1,0:T(8,128)(2,1)}, u32[]{:S(2)}) copy-start(bf16[1536,1024]{1,0:T(8,128)(2,1)} %own) | copy-start | bytes 9437188
  0.0 6.4 %copy-start.2 = (f32[1536]{0:T(1024)S(1)}, f32[1536]{0:T(1024)}, u32[]{:S(2)}) copy-start(f32[1536]{0:T(1024)} %param.5) | copy-start | bytes 18436
  0.0 6.4 %copy-start.1 = (f32[2]{0:T(128)S(1)}, f32[2]{0:T(128)}, u32[]{:S(2)}) copy-start(f32[2]{0:T(128)} %frequencies.1) | copy-start | bytes 28
  2.8 11.0 %collective-permute-start = (bf16[1536,1024]{1,0:T(8,128)(2,1)S(1)}, bf16[1536,1024]{1,0:T(8,128)(2,1)}, u32[]{:S(2)}, u32[]{:S(2)}) collective-permute-start(bf16[1536,1024]{1,0:T(8,128)(2,1)S(1)} %copy-done), channel_id=1, source_target_pairs={{1,0},{0,1},{3,2},{2,3},{5,4},{4,5},{7,6},{6,7},{9,8},{8,9},{11,10... | collective-permute-start | bytes 9437192 | tf_op jit(solution)/shard_map/ppermute | solution.py:80
  4.2 36.3 %collective-permute-start.4 = (bf16[1536,512]{1,0:T(8,128)(2,1)}, bf16[1536,512]{1,0:T(8,128)(2,1)}, u32[]{:S(2)}, u32[]{:S(2)}) collective-permute-start(bf16[1536,512]{1,0:T(8,128)(2,1)} %slice.102), channel_id=1, source_target_pairs={{2,0},{3,1},{1,2},{0,3},{6,4},{7,5},{5,6},{4,7},{10,8},{11,9},{9,1... | collective-permute-start | bytes 4718600 | tf_op jit(solution)/shard_map/ppermute | solution.py:80
  19.7 29.4 %collective-permute-start.3 = (bf16[4,10,128,128]{3,2,1,0:T(8,128)(2,1)S(1)}, bf16[4,10,128,128]{3,2,1,0:T(8,128)(2,1)S(1)}, u32[]{:S(2)}, u32[]{:S(2)}) collective-permute-start(bf16[4,10,128,128]{3,2,1,0:T(8,128)(2,1)S(1)} %get-tuple-element.62), channel_id=1, source_target_pairs={{0,12},{1,49},{2,14},{3,51},{4,8},{5,53},{6,10},{7,55},{8,4},{9,57... | collective-permute-start | bytes 3932168 | tf_op jit(solution)/shard_map/ppermute | solution.py:80
  23.5 29.4 %collective-permute-start.1 = (bf16[4,10,128,128]{3,2,1,0:T(8,128)(2,1)S(1)}, bf16[4,10,128,128]{3,2,1,0:T(8,128)(2,1)S(1)}, u32[]{:S(2)}, u32[]{:S(2)}) collective-permute-start(bf16[4,10,128,128]{3,2,1,0:T(8,128)(2,1)S(1)} %get-tuple-element.60), channel_id=1, source_target_pairs={{0,4},{1,17},{2,6},{3,19},{4,0},{5,21},{6,2},{7,23},{8,12},{9,25},... | collective-permute-start | bytes 3932168 | tf_op jit(solution)/shard_map/ppermute | solution.py:80
  23.5 30.6 %collective-permute-start.2 = (bf16[4,10,128,128]{3,2,1,0:T(8,128)(2,1)S(1)}, bf16[4,10,128,128]{3,2,1,0:T(8,128)(2,1)S(1)}, u32[]{:S(2)}, u32[]{:S(2)}) collective-permute-start(bf16[4,10,128,128]{3,2,1,0:T(8,128)(2,1)S(1)} %get-tuple-element.61), channel_id=1, source_target_pairs={{0,8},{1,33},{2,10},{3,35},{4,12},{5,37},{6,14},{7,39},{8,0},{9,41... | collective-permute-start | bytes 3932168 | tf_op jit(solution)/shard_map/ppermute | solution.py:80
  40.6 29.5 %collective-permute-start.12 = (bf16[1536,256]{1,0:T(8,128)(2,1)S(1)}, bf16[1536,256]{1,0:T(8,128)(2,1)S(1)}, u32[]{:S(2)}, u32[]{:S(2)}) collective-permute-start(bf16[1536,256]{1,0:T(8,128)(2,1)S(1)} %get-tuple-element.80), channel_id=1, source_target_pairs={{2,0},{3,1},{1,2},{0,3},{6,4},{7,5},{5,6},{4,7},{10,8},{11,9},{9,1... | collective-permute-start | bytes 2359304 | tf_op jit(solution)/shard_map/ppermute | solution.py:80
  47.9 28.1 %collective-permute-start.11 = (bf16[1536,256]{1,0:T(8,128)(2,1)S(1)}, bf16[1536,256]{1,0:T(8,128)(2,1)S(1)}, u32[]{:S(2)}, u32[]{:S(2)}) collective-permute-start(bf16[1536,256]{1,0:T(8,128)(2,1)S(1)} %get-tuple-element.79), channel_id=1, source_target_pairs={{2,0},{3,1},{1,2},{0,3},{6,4},{7,5},{5,6},{4,7},{10,8},{11,9},{9,1... | collective-permute-start | bytes 2359304 | tf_op jit(solution)/shard_map/ppermute | solution.py:80
  49.1 10.7 %collective-permute-start.9 = (bf16[4,4,128,128]{3,2,1,0:T(8,128)(2,1)S(1)}, bf16[4,4,128,128]{3,2,1,0:T(8,128)(2,1)S(1)}, u32[]{:S(2)}, u32[]{:S(2)}) collective-permute-start(bf16[4,4,128,128]{3,2,1,0:T(8,128)(2,1)S(1)} %get-tuple-element.75), channel_id=1, source_target_pairs={{0,12},{1,49},{2,14},{3,51},{4,8},{5,53},{6,10},{7,55},{8,4},{9,57... | collective-permute-start | bytes 1572872 | tf_op jit(solution)/shard_map/ppermute | solution.py:80
  52.9 9.3 %collective-permute-start.5 = (bf16[4,4,128,128]{3,2,1,0:T(8,128)(2,1)S(1)}, bf16[4,4,128,128]{3,2,1,0:T(8,128)(2,1)S(1)}, u32[]{:S(2)}, u32[]{:S(2)}) collective-permute-start(bf16[4,4,128,128]{3,2,1,0:T(8,128)(2,1)S(1)} %get-tuple-element.67), channel_id=1, source_target_pairs={{0,4},{1,17},{2,6},{3,19},{4,0},{5,21},{6,2},{7,23},{8,12},{9,25},... | collective-permute-start | bytes 1572872 | tf_op jit(solution)/shard_map/ppermute | solution.py:80
  54.1 12.3 %collective-permute-start.7 = (bf16[4,4,128,128]{3,2,1,0:T(8,128)(2,1)S(1)}, bf16[4,4,128,128]{3,2,1,0:T(8,128)(2,1)S(1)}, u32[]{:S(2)}, u32[]{:S(2)}) collective-permute-start(bf16[4,4,128,128]{3,2,1,0:T(8,128)(2,1)S(1)} %get-tuple-element.71), channel_id=1, source_target_pairs={{0,8},{1,33},{2,10},{3,35},{4,12},{5,37},{6,14},{7,39},{8,0},{9,41... | collective-permute-start | bytes 1572872 | tf_op jit(solution)/shard_map/ppermute | solution.py:80
  59.8 19.7 %collective-permute-start.10 = (f16[1296,128]{1,0:T(8,128)(2,1)S(1)}, f16[1296,128]{1,0:T(8,128)(2,1)S(1)}, u32[]{:S(2)}, u32[]{:S(2)}) collective-permute-start(f16[1296,128]{1,0:T(8,128)(2,1)S(1)} %convert_element_type.141), channel_id=1, source_target_pairs={{0,48},{1,13},{2,50},{3,15},{4,52},{5,9},{6,54},{7,11},{8,56},{9,5... | collective-permute-start | bytes 995336 | tf_op jit(solution)/shard_map/ppermute | solution.py:80
  62.3 17.2 %collective-permute-start.6 = (f16[1296,128]{1,0:T(8,128)(2,1)S(1)}, f16[1296,128]{1,0:T(8,128)(2,1)S(1)}, u32[]{:S(2)}, u32[]{:S(2)}) collective-permute-start(f16[1296,128]{1,0:T(8,128)(2,1)S(1)} %convert_element_type.135), channel_id=1, source_target_pairs={{0,16},{1,5},{2,18},{3,7},{4,20},{5,1},{6,22},{7,3},{8,24},{9,13},... | collective-permute-start | bytes 995336 | tf_op jit(solution)/shard_map/ppermute | solution.py:80
  66.5 13.0 %collective-permute-start.8 = (f16[1296,128]{1,0:T(8,128)(2,1)S(1)}, f16[1296,128]{1,0:T(8,128)(2,1)S(1)}, u32[]{:S(2)}, u32[]{:S(2)}) collective-permute-start(f16[1296,128]{1,0:T(8,128)(2,1)S(1)} %convert_element_type.138), channel_id=1, source_target_pairs={{0,32},{1,9},{2,34},{3,11},{4,36},{5,13},{6,38},{7,15},{8,40},{9,1... | collective-permute-start | bytes 995336 | tf_op jit(solution)/shard_map/ppermute | solution.py:80
  79.5 10.5 %collective-permute-start.17 = (bf16[4,4,128,128]{3,2,1,0:T(8,128)(2,1)S(1)}, bf16[4,4,128,128]{3,2,1,0:T(8,128)(2,1)S(1)}, u32[]{:S(2)}, u32[]{:S(2)}) collective-permute-start(bf16[4,4,128,128]{3,2,1,0:T(8,128)(2,1)S(1)} %get-tuple-element.90), channel_id=1, source_target_pairs={{0,8},{1,33},{2,10},{3,35},{4,12},{5,37},{6,14},{7,39},{8,0},{9,41... | collective-permute-start | bytes 1572872 | tf_op jit(solution)/shard_map/ppermute | solution.py:80
  83.1 13.2 %collective-permute-start.16 = (bf16[4,4,128,128]{3,2,1,0:T(8,128)(2,1)S(1)}, bf16[4,4,128,128]{3,2,1,0:T(8,128)(2,1)S(1)}, u32[]{:S(2)}, u32[]{:S(2)}) collective-permute-start(bf16[4,4,128,128]{3,2,1,0:T(8,128)(2,1)S(1)} %get-tuple-element.88), channel_id=1, source_target_pairs={{0,4},{1,17},{2,6},{3,19},{4,0},{5,21},{6,2},{7,23},{8,12},{9,25},... | collective-permute-start | bytes 1572872 | tf_op jit(solution)/shard_map/ppermute | solution.py:80
  83.8 12.5 %collective-permute-start.13 = (bf16[4,4,128,128]{3,2,1,0:T(8,128)(2,1)S(1)}, bf16[4,4,128,128]{3,2,1,0:T(8,128)(2,1)S(1)}, u32[]{:S(2)}, u32[]{:S(2)}) collective-permute-start(bf16[4,4,128,128]{3,2,1,0:T(8,128)(2,1)S(1)} %get-tuple-element.82), channel_id=1, source_target_pairs={{0,12},{1,49},{2,14},{3,51},{4,8},{5,53},{6,10},{7,55},{8,4},{9,57... | collective-permute-start | bytes 1572872 | tf_op jit(solution)/shard_map/ppermute | solution.py:80
  96.9 8.9 %collective-permute-start.20 = (f16[1056,128]{1,0:T(8,128)(2,1)S(1)}, f16[1056,128]{1,0:T(8,128)(2,1)S(1)}, u32[]{:S(2)}, u32[]{:S(2)}) collective-permute-start(f16[1056,128]{1,0:T(8,128)(2,1)S(1)} %pad_maximum_fusion.3), channel_id=1, source_target_pairs={{0,48},{1,13},{2,50},{3,15},{4,52},{5,9},{6,54},{7,11},{8,56},{9,5... | collective-permute-start | bytes 811016 | tf_op jit(solution)/shard_map/ppermute | solution.py:80
  99.6 6.9 %collective-permute-start.19 = (f16[1056,128]{1,0:T(8,128)(2,1)S(1)}, f16[1056,128]{1,0:T(8,128)(2,1)S(1)}, u32[]{:S(2)}, u32[]{:S(2)}) collective-permute-start(f16[1056,128]{1,0:T(8,128)(2,1)S(1)} %pad_maximum_fusion.2), channel_id=1, source_target_pairs={{0,32},{1,9},{2,34},{3,11},{4,36},{5,13},{6,38},{7,15},{8,40},{9,1... | collective-permute-start | bytes 811016 | tf_op jit(solution)/shard_map/ppermute | solution.py:80
  100.2 7.3 %collective-permute-start.18 = (f16[1056,128]{1,0:T(8,128)(2,1)S(1)}, f16[1056,128]{1,0:T(8,128)(2,1)S(1)}, u32[]{:S(2)}, u32[]{:S(2)}) collective-permute-start(f16[1056,128]{1,0:T(8,128)(2,1)S(1)} %pad_maximum_fusion.1), channel_id=1, source_target_pairs={{0,16},{1,5},{2,18},{3,7},{4,20},{5,1},{6,22},{7,3},{8,24},{9,13},... | collective-permute-start | bytes 811016 | tf_op jit(solution)/shard_map/ppermute | solution.py:80
  100.8 12.0 %collective-permute-start.14 = (f16[1296,128]{1,0:T(8,128)(2,1)S(1)}, f16[1296,128]{1,0:T(8,128)(2,1)S(1)}, u32[]{:S(2)}, u32[]{:S(2)}) collective-permute-start(f16[1296,128]{1,0:T(8,128)(2,1)S(1)} %convert_element_type.144), channel_id=1, source_target_pairs={{2,66},{3,67},{6,70},{7,71},{10,74},{11,75},{14,78},{15,79},{18,82... | collective-permute-start | bytes 995336 | tf_op jit(solution)/shard_map/ppermute | solution.py:80
  108.0 8.5 %collective-permute-start.21 = (f16[1040,128]{1,0:T(8,128)(2,1)S(1)}, f16[1040,128]{1,0:T(8,128)(2,1)S(1)}, u32[]{:S(2)}, u32[]{:S(2)}) collective-permute-start(f16[1040,128]{1,0:T(8,128)(2,1)S(1)} %convert_element_type.165), channel_id=1, source_target_pairs={{0,64},{1,65},{4,68},{5,69},{8,72},{9,73},{12,76},{13,77},{16,80},... | collective-permute-start | bytes 798728 | tf_op jit(solution)/shard_map/ppermute | solution.py:80
  112.9 4.7 %collective-permute-start.15 = (f32[512,128]{1,0:T(8,128)S(1)}, f32[512,128]{1,0:T(8,128)S(1)}, u32[]{:S(2)}, u32[]{:S(2)}) collective-permute-start(f32[512,128]{1,0:T(8,128)S(1)} %slice.144), channel_id=1, source_target_pairs={{1,0},{0,1},{3,2},{2,3},{5,4},{4,5},{7,6},{6,7},{9,8},{8,9},{11,10... | collective-permute-start | bytes 786440 | tf_op jit(solution)/shard_map/ppermute | solution.py:80
  118.7 12.0 %collective-permute-start.25 = (f16[528,128]{1,0:T(8,128)(2,1)S(1)}, f16[528,128]{1,0:T(8,128)(2,1)S(1)}, u32[]{:S(2)}, u32[]{:S(2)}) collective-permute-start(f16[528,128]{1,0:T(8,128)(2,1)S(1)} %convert_element_type.177), channel_id=1, source_target_pairs={{0,1},{1,32},{2,65},{3,96},{4,5},{5,36},{6,69},{7,100},{8,9},{9,40... | collective-permute-start | bytes 405512 | tf_op jit(solution)/shard_map/ppermute | solution.py:80
  124.1 9.1 %collective-permute-start.24 = (f16[528,128]{1,0:T(8,128)(2,1)S(1)}, f16[528,128]{1,0:T(8,128)(2,1)S(1)}, u32[]{:S(2)}, u32[]{:S(2)}) collective-permute-start(f16[528,128]{1,0:T(8,128)(2,1)S(1)} %convert_element_type.174), channel_id=1, source_target_pairs={{0,17},{1,48},{2,81},{3,112},{4,21},{5,52},{6,85},{7,116},{8,25},{... | collective-permute-start | bytes 405512 | tf_op jit(solution)/shard_map/ppermute | solution.py:80
  126.3 8.4 %collective-permute-start.23 = (f16[528,128]{1,0:T(8,128)(2,1)S(1)}, f16[528,128]{1,0:T(8,128)(2,1)S(1)}, u32[]{:S(2)}, u32[]{:S(2)}) collective-permute-start(f16[528,128]{1,0:T(8,128)(2,1)S(1)} %convert_element_type.171), channel_id=1, source_target_pairs={{0,16},{1,49},{2,50},{3,19},{4,20},{5,53},{6,54},{7,23},{8,24},{9,... | collective-permute-start | bytes 405512 | tf_op jit(solution)/shard_map/ppermute | solution.py:80
  126.3 10.1 %collective-permute-start.22 = (f16[528,128]{1,0:T(8,128)(2,1)S(1)}, f16[528,128]{1,0:T(8,128)(2,1)S(1)}, u32[]{:S(2)}, u32[]{:S(2)}) collective-permute-start(f16[528,128]{1,0:T(8,128)(2,1)S(1)} %convert_element_type.168), channel_id=1, source_target_pairs={{0,0},{1,33},{2,34},{3,3},{4,4},{5,37},{6,38},{7,7},{8,8},{9,41},{... | collective-permute-start | bytes 405512 | tf_op jit(solution)/shard_map/ppermute | solution.py:80

commit v8 on v7

--- a/solution.py
+++ b/solution.py
@@ -206,7 +206,7 @@
         [place],
         [other, scaled, early],
         [pltpu.VMEM((512, 512), jnp.float32)],
-        flops=2 * 4 * 256 * 512 * other.shape[0],
+        flops=2 * 4 * other.shape[1] * 512 * other.shape[0],
         name="late_products",
     )
 
@@ -385,10 +385,10 @@
     scaled, *blocks = own_products(here, frequencies, own, energy_gaps)
     near, *send = mate_products(place, other, scaled, blocks)
     rest = after(own, near)
-    far1 = permute(after(rest[:, 512:768], far0), far_perm)
+    far1 = permute(after(rest[:, 512:896], far0), far_perm)
     near_sent = send_first(send, [None, None, None])
     sum0, *send = far_products(place, far0, scaled)
-    far2 = permute(after(rest[:, 768:], sum0), far_perm)
+    far2 = permute(after(rest[:, 896:], sum0), far_perm)
     sum0_sent = send_first(send, near_sent)
     near, send = first_sum(near, *near_sent)
     near_sent = send_second(send, [sum0_sent[0], sum0_sent[1], sum0_sent[2]])

time: 141 us -> 141 us (level)
  starting transfers between devices: 51.4 us -> 46.4 us
  waiting for transfers between devices: 52.3 us -> 57 us
    ppermute x26, starting transfers between devices: 51.4 us -> 46.4 us  [permute(): return lax.ppermute(value, AXES, pairs)]
    ppermute x26, waiting for transfers between devices: 52.3 us -> 57 us  [permute(): return lax.ppermute(value, AXES, pairs)]
where the time goes in v8:
time: 141 us; the launch traced here: 139 us
  waiting for transfers between devices  57 us (40%)
  starting transfers between devices  46.4 us (33%)
  Pallas kernels  29.6 us (21%)
  local copies, waits for them, and re-layouts  3.97 us (3%)
    ppermute x26, waiting for transfers between devices, permute(): return lax.ppermute(value, AXES, pairs)  57 us
    ppermute x26, starting transfers between devices, permute(): return lax.ppermute(value, AXES, pairs)  46.4 us
    pallas_call x12, Pallas kernels, call(): pl.pallas_call(kernel, out_shape=out_shape, in_specs=[smem] * len(scalars...  29.6 us
  transfers between devices with their start and end apart: 26, of which 14 were waited for; matrix products, arithmetic and copies ran while one was open for 2% of the time, Pallas kernels for 19%

profile of v8, /device:TPU:1, one launch (start us, length us, event | category | flops | bytes accessed | tf_op | source)
XLA Modules:
  0.0 138.7 jit_solution(11620058222286986666)
XLA Ops:
  0.0 2.8 %slice.102 = bf16[1536,512]{1,0:T(8,128)(2,1)} slice(bf16[1536,1024]{1,0:T(8,128)(2,1)} %own), slice={[0:1536], [0:512]} | slice | bytes 3145728 | tf_op jit(solution)/shard_map/slice | solution.py:380
  2.8 1.4 %collective-permute-start = (bf16[1536,1024]{1,0:T(8,128)(2,1)S(1)}, bf16[1536,1024]{1,0:T(8,128)(2,1)}, u32[]{:S(2)}, u32[]{:S(2)}) collective-permute-start(bf16[1536,1024]{1,0:T(8,128)(2,1)S(1)} %copy-done), channel_id=1, source_target_pairs={{1,0},{0,1},{3,2},{2,3},{5,4},{4,5},{7,6},{6,7},{9,8},{8,9},{11,10... | collective-permute-start | bytes 9437192 | tf_op jit(solution)/shard_map/ppermute | solution.py:80
  4.2 1.3 collective-permute-start.4
  5.6 0.7 dynamic-slice_bitcast_fusion
  6.4 7.5 %own_products.1 = (bf16[4,1536,512]{2,1,0:T(8,128)(2,1)S(1)}, f32[4,10,128,128]{3,2,1,0:T(8,128)S(1)}, bf16[4,10,128,128]{3,2,1,0:T(8,128)(2,1)S(1)}, bf16[4,10,...) custom-call(s32[5]{0:T(128)S(1)} %stack.23.place, f32[2]{0:T(128)S(1)} %copy-done.1, ...), custom_call_target="tpu_custom_call" | custom-call | flops 4831838208 | tf_op jit(solution)/shard_map/own_products/pallas_call | solution.py:86
  13.9 5.8 %mate_products.1 = (f32[4,10,128,128]{3,2,1,0:T(8,128)S(1)}, bf16[4,10,128,128]{3,2,1,0:T(8,128)(2,1)S(1)}, bf16[4,10,128,128]{3,2,1,0:T(8,128)(2,1)S(1)}, bf16[4,10,128,128]{3,2,1,0:T(8,128)(2,1)S(1)}) custom-call(s32[13]{0:T(128)S(1)} %concatenate.16.place, ...), custom_call_target="tpu_custom_call", output_to_operand_aliasing={{0}: (3, {}), {1}: (4, {}), {2}: (5, {}), {3}: (6, {})} | custom-call | flops 3221225472 | tf_op jit(solution)/shard_map/mate_products/pallas_call | solution.py:86
  19.7 3.8 %collective-permute-start.3 = (bf16[4,10,128,128]{3,2,1,0:T(8,128)(2,1)S(1)}, bf16[4,10,128,128]{3,2,1,0:T(8,128)(2,1)S(1)}, u32[]{:S(2)}, u32[]{:S(2)}) collective-permute-start(bf16[4,10,128,128]{3,2,1,0:T(8,128)(2,1)S(1)} %get-tuple-element.62), channel_id=1, source_target_pairs={{0,12},{1,49},{2,14},{3,51},{4,8},{5,53},{6,10},{7,55},{8,4},{9,57... | collective-permute-start | bytes 3932168 | tf_op jit(solution)/shard_map/ppermute | solution.py:80
  23.5 0.7 collective-permute-start.1
  24.4 16.2 %collective-permute-done.4.other = bf16[1536,512]{1,0:T(8,128)(2,1)} collective-permute-done((bf16[1536,512]{1,0:T(8,128)(2,1)}, bf16[1536,512]{1,0:T(8,128)(2,1)}, u32[]{:S(2)}, u32[]{:S(2)}) %collective-permute-start.4) | collective-permute-done | bytes 1572896 | tf_op jit(solution)/shard_map/ppermute | solution.py:80
  40.6 1.3 collective-permute-start.12
  41.9 6.0 %far_products.1 = (f32[4,4,128,128]{3,2,1,0:T(8,128)S(1)}, bf16[4,4,128,128]{3,2,1,0:T(8,128)(2,1)S(1)}, bf16[4,4,128,128]{3,2,1,0:T(8,128)(2,1)S(1)}, bf16[4,4,128,128]{3,2,1,0:T(8,128)(2,1)S(1)}) custom-call(s32[13]{0:T(128)S(1)} %concatenate.16.place, bf16[1536,512]{1,0:T(8,128)(2,1)} %collective-permute-done.4.other, ...), custom_call_target="tpu_custom_call" | custom-call | flops 3221225472 | tf_op jit(solution)/shard_map/far_products/pallas_call | solution.py:86
  47.9 4.8 %collective-permute-done.3.c = bf16[4,10,128,128]{3,2,1,0:T(8,128)(2,1)S(1)} collective-permute-done((bf16[4,10,128,128]{3,2,1,0:T(8,128)(2,1)S(1)}, bf16[4,10,128,128]{3,2,1,0:T(8,128)(2,1)S(1)}, u32[]{:S(2)}, u32[]{:S(2)}) %collective-permute-start.3) | collective-permute-done | bytes 1310752 | tf_op jit(solution)/shard_map/ppermute | solution.py:80
  52.7 2.8 %collective-permute-start.9 = (bf16[4,4,128,128]{3,2,1,0:T(8,128)(2,1)S(1)}, bf16[4,4,128,128]{3,2,1,0:T(8,128)(2,1)S(1)}, u32[]{:S(2)}, u32[]{:S(2)}) collective-permute-start(bf16[4,4,128,128]{3,2,1,0:T(8,128)(2,1)S(1)} %get-tuple-element.75), channel_id=1, source_target_pairs={{0,12},{1,49},{2,14},{3,51},{4,8},{5,53},{6,10},{7,55},{8,4},{9,57... | collective-permute-start | bytes 1572872 | tf_op jit(solution)/shard_map/ppermute | solution.py:80
  55.5 0.6 collective-permute-start.5
  56.2 1.0 collective-permute-start.11
  57.2 0.9 first_sum.3
  58.2 9.8 %collective-permute-done.9.c = bf16[4,4,128,128]{3,2,1,0:T(8,128)(2,1)S(1)} collective-permute-done((bf16[4,4,128,128]{3,2,1,0:T(8,128)(2,1)S(1)}, bf16[4,4,128,128]{3,2,1,0:T(8,128)(2,1)S(1)}, u32[]{:S(2)}, u32[]{:S(2)}) %collective-permute-start.9) | collective-permute-done | bytes 524320 | tf_op jit(solution)/shard_map/ppermute | solution.py:80
  68.0 2.5 %collective-permute-start.10 = (f16[1296,128]{1,0:T(8,128)(2,1)S(1)}, f16[1296,128]{1,0:T(8,128)(2,1)S(1)}, u32[]{:S(2)}, u32[]{:S(2)}) collective-permute-start(f16[1296,128]{1,0:T(8,128)(2,1)S(1)} %convert_element_type.141), channel_id=1, source_target_pairs={{0,48},{1,13},{2,50},{3,15},{4,52},{5,9},{6,54},{7,11},{8,56},{9,5... | collective-permute-start | bytes 995336 | tf_op jit(solution)/shard_map/ppermute | solution.py:80
  70.5 0.9 collective-permute-start.6
  71.4 2.6 %early_products.1.early = f32[4,384,512]{2,1,0:T(8,128)S(1)} custom-call(bf16[1536,384]{1,0:T(8,128)(2,1)S(1)} %collective-permute-done.12.other, bf16[4,1536,512]{2,1,0:T(8,128)(2,1)S(1)} %get-tuple-element.54.scaled), custom_call_target="tpu_custom_call" | custom-call | flops 2415919104 | tf_op jit(solution)/shard_map/early_products/pallas_call | solution.py:86
  74.1 1.9 %collective-permute-done.11.other = bf16[1536,128]{1,0:T(8,128)(2,1)S(1)} collective-permute-done((bf16[1536,128]{1,0:T(8,128)(2,1)S(1)}, bf16[1536,128]{1,0:T(8,128)(2,1)S(1)}, u32[]{:S(2)}, u32[]{:S(2)}) %collective-permute-start.11) | collective-permute-done | bytes 393248 | tf_op jit(solution)/shard_map/ppermute | solution.py:80
  75.9 2.5 %late_products.1 = (f32[4,4,128,128]{3,2,1,0:T(8,128)S(1)}, bf16[4,4,128,128]{3,2,1,0:T(8,128)(2,1)S(1)}, bf16[4,4,128,128]{3,2,1,0:T(8,128)(2,1)S(1)}, bf16[4,4,128,128]{3,2,1,0:T(8,128)(2,1)S(1)}) custom-call(s32[13]{0:T(128)S(1)} %concatenate.16.place, bf16[1536,128]{1,0:T(8,128)(2,1)S(1)} %collective-permute-done.11.other, ...), custom_call_target="tpu_custom_call" | custom-call | flops 805306368 | tf_op jit(solution)/shard_map/late_products/pallas_call | solution.py:86
  78.4 0.4 first_sum.4
  79.0 3.6 %collective-permute-start.13 = (bf16[4,4,128,128]{3,2,1,0:T(8,128)(2,1)S(1)}, bf16[4,4,128,128]{3,2,1,0:T(8,128)(2,1)S(1)}, u32[]{:S(2)}, u32[]{:S(2)}) collective-permute-start(bf16[4,4,128,128]{3,2,1,0:T(8,128)(2,1)S(1)} %get-tuple-element.82), channel_id=1, source_target_pairs={{0,12},{1,49},{2,14},{3,51},{4,8},{5,53},{6,10},{7,55},{8,4},{9,57... | collective-permute-start | bytes 1572872 | tf_op jit(solution)/shard_map/ppermute | solution.py:80
  82.7 0.7 collective-permute-start.16
  83.3 0.2 multiply_add_fusion.1.value
  83.6 11.6 %collective-permute-done.13.c = bf16[4,4,128,128]{3,2,1,0:T(8,128)(2,1)S(1)} collective-permute-done((bf16[4,4,128,128]{3,2,1,0:T(8,128)(2,1)S(1)}, bf16[4,4,128,128]{3,2,1,0:T(8,128)(2,1)S(1)}, u32[]{:S(2)}, u32[]{:S(2)}) %collective-permute-start.13) | collective-permute-done | bytes 524320 | tf_op jit(solution)/shard_map/ppermute | solution.py:80
  95.1 0.7 collective-permute-done.16.a
  95.9 0.4 first_sum.5
  96.4 2.6 %collective-permute-start.20 = (f16[1056,128]{1,0:T(8,128)(2,1)S(1)}, f16[1056,128]{1,0:T(8,128)(2,1)S(1)}, u32[]{:S(2)}, u32[]{:S(2)}) collective-permute-start(f16[1056,128]{1,0:T(8,128)(2,1)S(1)} %pad_maximum_fusion.3), channel_id=1, source_target_pairs={{0,48},{1,13},{2,50},{3,15},{4,52},{5,9},{6,54},{7,11},{8,56},{9,5... | collective-permute-start | bytes 811016 | tf_op jit(solution)/shard_map/ppermute | solution.py:80
  99.1 0.6 collective-permute-start.19
  99.8 0.3 collective-permute-start.18
  100.1 0.2 seal.2
  100.3 1.3 collective-permute-start.14
  101.6 3.6 %collective-permute-done.20 = f16[1056,128]{1,0:T(8,128)(2,1)S(1)} collective-permute-done((f16[1056,128]{1,0:T(8,128)(2,1)S(1)}, f16[1056,128]{1,0:T(8,128)(2,1)S(1)}, u32[]{:S(2)}, u32[]{:S(2)}) %collective-permute-start.20) | collective-permute-done | bytes 270368 | tf_op jit(solution)/shard_map/ppermute | solution.py:80
  105.3 0.7 collective-permute-done.19
  106.0 0.7 collective-permute-done.18
  107.2 4.8 %collective-permute-start.21 = (f16[1040,128]{1,0:T(8,128)(2,1)S(1)}, f16[1040,128]{1,0:T(8,128)(2,1)S(1)}, u32[]{:S(2)}, u32[]{:S(2)}) collective-permute-start(f16[1040,128]{1,0:T(8,128)(2,1)S(1)} %convert_element_type.165), channel_id=1, source_target_pairs={{0,64},{1,65},{4,68},{5,69},{8,72},{9,73},{12,76},{13,77},{16,80},... | collective-permute-start | bytes 798728 | tf_op jit(solution)/shard_map/ppermute | solution.py:80
  112.1 4.4 %collective-permute-start.15 = (f32[512,128]{1,0:T(8,128)S(1)}, f32[512,128]{1,0:T(8,128)S(1)}, u32[]{:S(2)}, u32[]{:S(2)}) collective-permute-start(f32[512,128]{1,0:T(8,128)S(1)} %slice.144), channel_id=1, source_target_pairs={{1,0},{0,1},{3,2},{2,3},{5,4},{4,5},{7,6},{6,7},{9,8},{8,9},{11,10... | collective-permute-start | bytes 786440 | tf_op jit(solution)/shard_map/ppermute | solution.py:80
  116.6 1.1 collective-permute-done.15.twin
  117.7 1.0 pack.1
  118.7 5.2 %collective-permute-start.25 = (f16[528,128]{1,0:T(8,128)(2,1)S(1)}, f16[528,128]{1,0:T(8,128)(2,1)S(1)}, u32[]{:S(2)}, u32[]{:S(2)}) collective-permute-start(f16[528,128]{1,0:T(8,128)(2,1)S(1)} %convert_element_type.177), channel_id=1, source_target_pairs={{0,1},{1,32},{2,65},{3,96},{4,5},{5,36},{6,69},{7,100},{8,9},{9,40... | collective-permute-start | bytes 405512 | tf_op jit(solution)/shard_map/ppermute | solution.py:80
  124.0 2.3 %collective-permute-start.24 = (f16[528,128]{1,0:T(8,128)(2,1)S(1)}, f16[528,128]{1,0:T(8,128)(2,1)S(1)}, u32[]{:S(2)}, u32[]{:S(2)}) collective-permute-start(f16[528,128]{1,0:T(8,128)(2,1)S(1)} %convert_element_type.174), channel_id=1, source_target_pairs={{0,17},{1,48},{2,81},{3,112},{4,21},{5,52},{6,85},{7,116},{8,25},{... | collective-permute-start | bytes 405512 | tf_op jit(solution)/shard_map/ppermute | solution.py:80
  126.4 4.3 %collective-permute-start.22 = (f16[528,128]{1,0:T(8,128)(2,1)S(1)}, f16[528,128]{1,0:T(8,128)(2,1)S(1)}, u32[]{:S(2)}, u32[]{:S(2)}) collective-permute-start(f16[528,128]{1,0:T(8,128)(2,1)S(1)} %convert_element_type.168), channel_id=1, source_target_pairs={{0,0},{1,33},{2,34},{3,3},{4,4},{5,37},{6,38},{7,7},{8,8},{9,41},{... | collective-permute-start | bytes 405512 | tf_op jit(solution)/shard_map/ppermute | solution.py:80
  130.8 2.4 %collective-permute-done.24 = f16[528,128]{1,0:T(8,128)(2,1)S(1)} collective-permute-done((f16[528,128]{1,0:T(8,128)(2,1)S(1)}, f16[528,128]{1,0:T(8,128)(2,1)S(1)}, u32[]{:S(2)}, u32[]{:S(2)}) %collective-permute-start.24) | collective-permute-done | bytes 135200 | tf_op jit(solution)/shard_map/ppermute | solution.py:80
  133.2 1.5 %collective-permute-done.23 = f16[528,128]{1,0:T(8,128)(2,1)S(1)} collective-permute-done((f16[528,128]{1,0:T(8,128)(2,1)S(1)}, f16[528,128]{1,0:T(8,128)(2,1)S(1)}, u32[]{:S(2)}, u32[]{:S(2)}) %collective-permute-start.23) | collective-permute-done | bytes 135200 | tf_op jit(solution)/shard_map/ppermute | solution.py:80
  134.7 1.8 %collective-permute-done.22 = f16[528,128]{1,0:T(8,128)(2,1)S(1)} collective-permute-done((f16[528,128]{1,0:T(8,128)(2,1)S(1)}, f16[528,128]{1,0:T(8,128)(2,1)S(1)}, u32[]{:S(2)}, u32[]{:S(2)}) %collective-permute-start.22) | collective-permute-done | bytes 135200 | tf_op jit(solution)/shard_map/ppermute | solution.py:80
  136.5 2.2 %unpack.1 = f32[128,2,1024]{2,1,0:T(2,128)} custom-call(s32[13]{0:T(128)S(1)} %concatenate.16.place, f32[512,128]{1,0:T(8,128)S(1)} %convert_multiply_fusion.3.a, f32[512,128]{1,0:T(8,128)S(1)} %convert_multiply_fusion.2.b, f32[512,128]{1,0:T(8,128)S(1)} %convert_multiply_fusion.1.c, f32[512,128]{1,0:T(8,128)S(1)} %convert_multiply_fusion.d), custom_call_target="tpu_custom_call" | custom-call | flops 262144 | tf_op jit(solution)/shard_map/unpack/pallas_call | solution.py:86
  (69 shorter events, 2.1 us)
Async XLA Ops:
  0.0 2.8 %copy-start = (bf16[1536,1024]{1,0:T(8,128)(2,1)S(1)}, bf16[1536,1024]{1,0:T(8,128)(2,1)}, u32[]{:S(2)}) copy-start(bf16[1536,1024]{1,0:T(8,128)(2,1)} %own) | copy-start | bytes 9437188
  0.0 6.4 %copy-start.2 = (f32[1536]{0:T(1024)S(1)}, f32[1536]{0:T(1024)}, u32[]{:S(2)}) copy-start(f32[1536]{0:T(1024)} %param.5) | copy-start | bytes 18436
  0.0 6.4 %copy-start.1 = (f32[2]{0:T(128)S(1)}, f32[2]{0:T(128)}, u32[]{:S(2)}) copy-start(f32[2]{0:T(128)} %frequencies.1) | copy-start | bytes 28
  2.8 11.0 %collective-permute-start = (bf16[1536,1024]{1,0:T(8,128)(2,1)S(1)}, bf16[1536,1024]{1,0:T(8,128)(2,1)}, u32[]{:S(2)}, u32[]{:S(2)}) collective-permute-start(bf16[1536,1024]{1,0:T(8,128)(2,1)S(1)} %copy-done), channel_id=1, source_target_pairs={{1,0},{0,1},{3,2},{2,3},{5,4},{4,5},{7,6},{6,7},{9,8},{8,9},{11,10... | collective-permute-start | bytes 9437192 | tf_op jit(solution)/shard_map/ppermute | solution.py:80
  4.2 36.3 %collective-permute-start.4 = (bf16[1536,512]{1,0:T(8,128)(2,1)}, bf16[1536,512]{1,0:T(8,128)(2,1)}, u32[]{:S(2)}, u32[]{:S(2)}) collective-permute-start(bf16[1536,512]{1,0:T(8,128)(2,1)} %slice.102), channel_id=1, source_target_pairs={{2,0},{3,1},{1,2},{0,3},{6,4},{7,5},{5,6},{4,7},{10,8},{11,9},{9,1... | collective-permute-start | bytes 4718600 | tf_op jit(solution)/shard_map/ppermute | solution.py:80
  19.7 33.0 %collective-permute-start.3 = (bf16[4,10,128,128]{3,2,1,0:T(8,128)(2,1)S(1)}, bf16[4,10,128,128]{3,2,1,0:T(8,128)(2,1)S(1)}, u32[]{:S(2)}, u32[]{:S(2)}) collective-permute-start(bf16[4,10,128,128]{3,2,1,0:T(8,128)(2,1)S(1)} %get-tuple-element.62), channel_id=1, source_target_pairs={{0,12},{1,49},{2,14},{3,51},{4,8},{5,53},{6,10},{7,55},{8,4},{9,57... | collective-permute-start | bytes 3932168 | tf_op jit(solution)/shard_map/ppermute | solution.py:80
  23.5 32.0 %collective-permute-start.2 = (bf16[4,10,128,128]{3,2,1,0:T(8,128)(2,1)S(1)}, bf16[4,10,128,128]{3,2,1,0:T(8,128)(2,1)S(1)}, u32[]{:S(2)}, u32[]{:S(2)}) collective-permute-start(bf16[4,10,128,128]{3,2,1,0:T(8,128)(2,1)S(1)} %get-tuple-element.61), channel_id=1, source_target_pairs={{0,8},{1,33},{2,10},{3,35},{4,12},{5,37},{6,14},{7,39},{8,0},{9,41... | collective-permute-start | bytes 3932168 | tf_op jit(solution)/shard_map/ppermute | solution.py:80
  23.5 32.0 %collective-permute-start.1 = (bf16[4,10,128,128]{3,2,1,0:T(8,128)(2,1)S(1)}, bf16[4,10,128,128]{3,2,1,0:T(8,128)(2,1)S(1)}, u32[]{:S(2)}, u32[]{:S(2)}) collective-permute-start(bf16[4,10,128,128]{3,2,1,0:T(8,128)(2,1)S(1)} %get-tuple-element.60), channel_id=1, source_target_pairs={{0,4},{1,17},{2,6},{3,19},{4,0},{5,21},{6,2},{7,23},{8,12},{9,25},... | collective-permute-start | bytes 3932168 | tf_op jit(solution)/shard_map/ppermute | solution.py:80
  40.6 30.8 %collective-permute-start.12 = (bf16[1536,384]{1,0:T(8,128)(2,1)S(1)}, bf16[1536,384]{1,0:T(8,128)(2,1)S(1)}, u32[]{:S(2)}, u32[]{:S(2)}) collective-permute-start(bf16[1536,384]{1,0:T(8,128)(2,1)S(1)} %slice.110), channel_id=1, source_target_pairs={{2,0},{3,1},{1,2},{0,3},{6,4},{7,5},{5,6},{4,7},{10,8},{11,9},{9,1... | collective-permute-start | bytes 3538952 | tf_op jit(solution)/shard_map/ppermute | solution.py:80
  52.7 15.3 %collective-permute-start.9 = (bf16[4,4,128,128]{3,2,1,0:T(8,128)(2,1)S(1)}, bf16[4,4,128,128]{3,2,1,0:T(8,128)(2,1)S(1)}, u32[]{:S(2)}, u32[]{:S(2)}) collective-permute-start(bf16[4,4,128,128]{3,2,1,0:T(8,128)(2,1)S(1)} %get-tuple-element.75), channel_id=1, source_target_pairs={{0,12},{1,49},{2,14},{3,51},{4,8},{5,53},{6,10},{7,55},{8,4},{9,57... | collective-permute-start | bytes 1572872 | tf_op jit(solution)/shard_map/ppermute | solution.py:80
  55.5 14.9 %collective-permute-start.7 = (bf16[4,4,128,128]{3,2,1,0:T(8,128)(2,1)S(1)}, bf16[4,4,128,128]{3,2,1,0:T(8,128)(2,1)S(1)}, u32[]{:S(2)}, u32[]{:S(2)}) collective-permute-start(bf16[4,4,128,128]{3,2,1,0:T(8,128)(2,1)S(1)} %get-tuple-element.71), channel_id=1, source_target_pairs={{0,8},{1,33},{2,10},{3,35},{4,12},{5,37},{6,14},{7,39},{8,0},{9,41... | collective-permute-start | bytes 1572872 | tf_op jit(solution)/shard_map/ppermute | solution.py:80
  55.5 15.0 %collective-permute-start.5 = (bf16[4,4,128,128]{3,2,1,0:T(8,128)(2,1)S(1)}, bf16[4,4,128,128]{3,2,1,0:T(8,128)(2,1)S(1)}, u32[]{:S(2)}, u32[]{:S(2)}) collective-permute-start(bf16[4,4,128,128]{3,2,1,0:T(8,128)(2,1)S(1)} %get-tuple-element.67), channel_id=1, source_target_pairs={{0,4},{1,17},{2,6},{3,19},{4,0},{5,21},{6,2},{7,23},{8,12},{9,25},... | collective-permute-start | bytes 1572872 | tf_op jit(solution)/shard_map/ppermute | solution.py:80
  56.2 19.7 %collective-permute-start.11 = (bf16[1536,128]{1,0:T(8,128)(2,1)S(1)}, bf16[1536,128]{1,0:T(8,128)(2,1)S(1)}, u32[]{:S(2)}, u32[]{:S(2)}) collective-permute-start(bf16[1536,128]{1,0:T(8,128)(2,1)S(1)} %slice.109), channel_id=1, source_target_pairs={{2,0},{3,1},{1,2},{0,3},{6,4},{7,5},{5,6},{4,7},{10,8},{11,9},{9,1... | collective-permute-start | bytes 1179656 | tf_op jit(solution)/shard_map/ppermute | solution.py:80
  68.0 11.0 %collective-permute-start.10 = (f16[1296,128]{1,0:T(8,128)(2,1)S(1)}, f16[1296,128]{1,0:T(8,128)(2,1)S(1)}, u32[]{:S(2)}, u32[]{:S(2)}) collective-permute-start(f16[1296,128]{1,0:T(8,128)(2,1)S(1)} %convert_element_type.141), channel_id=1, source_target_pairs={{0,48},{1,13},{2,50},{3,15},{4,52},{5,9},{6,54},{7,11},{8,56},{9,5... | collective-permute-start | bytes 995336 | tf_op jit(solution)/shard_map/ppermute | solution.py:80
  70.5 12.2 %collective-permute-start.8 = (f16[1296,128]{1,0:T(8,128)(2,1)S(1)}, f16[1296,128]{1,0:T(8,128)(2,1)S(1)}, u32[]{:S(2)}, u32[]{:S(2)}) collective-permute-start(f16[1296,128]{1,0:T(8,128)(2,1)S(1)} %convert_element_type.138), channel_id=1, source_target_pairs={{0,32},{1,9},{2,34},{3,11},{4,36},{5,13},{6,38},{7,15},{8,40},{9,1... | collective-permute-start | bytes 995336 | tf_op jit(solution)/shard_map/ppermute | solution.py:80
  70.5 12.1 %collective-permute-start.6 = (f16[1296,128]{1,0:T(8,128)(2,1)S(1)}, f16[1296,128]{1,0:T(8,128)(2,1)S(1)}, u32[]{:S(2)}, u32[]{:S(2)}) collective-permute-start(f16[1296,128]{1,0:T(8,128)(2,1)S(1)} %convert_element_type.135), channel_id=1, source_target_pairs={{0,16},{1,5},{2,18},{3,7},{4,20},{5,1},{6,22},{7,3},{8,24},{9,13},... | collective-permute-start | bytes 995336 | tf_op jit(solution)/shard_map/ppermute | solution.py:80
  79.0 16.1 %collective-permute-start.13 = (bf16[4,4,128,128]{3,2,1,0:T(8,128)(2,1)S(1)}, bf16[4,4,128,128]{3,2,1,0:T(8,128)(2,1)S(1)}, u32[]{:S(2)}, u32[]{:S(2)}) collective-permute-start(bf16[4,4,128,128]{3,2,1,0:T(8,128)(2,1)S(1)} %get-tuple-element.82), channel_id=1, source_target_pairs={{0,12},{1,49},{2,14},{3,51},{4,8},{5,53},{6,10},{7,55},{8,4},{9,57... | collective-permute-start | bytes 1572872 | tf_op jit(solution)/shard_map/ppermute | solution.py:80
  82.7 12.5 %collective-permute-start.17 = (bf16[4,4,128,128]{3,2,1,0:T(8,128)(2,1)S(1)}, bf16[4,4,128,128]{3,2,1,0:T(8,128)(2,1)S(1)}, u32[]{:S(2)}, u32[]{:S(2)}) collective-permute-start(bf16[4,4,128,128]{3,2,1,0:T(8,128)(2,1)S(1)} %get-tuple-element.90), channel_id=1, source_target_pairs={{0,8},{1,33},{2,10},{3,35},{4,12},{5,37},{6,14},{7,39},{8,0},{9,41... | collective-permute-start | bytes 1572872 | tf_op jit(solution)/shard_map/ppermute | solution.py:80
  82.7 13.2 %collective-permute-start.16 = (bf16[4,4,128,128]{3,2,1,0:T(8,128)(2,1)S(1)}, bf16[4,4,128,128]{3,2,1,0:T(8,128)(2,1)S(1)}, u32[]{:S(2)}, u32[]{:S(2)}) collective-permute-start(bf16[4,4,128,128]{3,2,1,0:T(8,128)(2,1)S(1)} %get-tuple-element.88), channel_id=1, source_target_pairs={{0,4},{1,17},{2,6},{3,19},{4,0},{5,21},{6,2},{7,23},{8,12},{9,25},... | collective-permute-start | bytes 1572872 | tf_op jit(solution)/shard_map/ppermute | solution.py:80
  96.4 8.9 %collective-permute-start.20 = (f16[1056,128]{1,0:T(8,128)(2,1)S(1)}, f16[1056,128]{1,0:T(8,128)(2,1)S(1)}, u32[]{:S(2)}, u32[]{:S(2)}) collective-permute-start(f16[1056,128]{1,0:T(8,128)(2,1)S(1)} %pad_maximum_fusion.3), channel_id=1, source_target_pairs={{0,48},{1,13},{2,50},{3,15},{4,52},{5,9},{6,54},{7,11},{8,56},{9,5... | collective-permute-start | bytes 811016 | tf_op jit(solution)/shard_map/ppermute | solution.py:80
  99.1 6.9 %collective-permute-start.19 = (f16[1056,128]{1,0:T(8,128)(2,1)S(1)}, f16[1056,128]{1,0:T(8,128)(2,1)S(1)}, u32[]{:S(2)}, u32[]{:S(2)}) collective-permute-start(f16[1056,128]{1,0:T(8,128)(2,1)S(1)} %pad_maximum_fusion.2), channel_id=1, source_target_pairs={{0,32},{1,9},{2,34},{3,11},{4,36},{5,13},{6,38},{7,15},{8,40},{9,1... | collective-permute-start | bytes 811016 | tf_op jit(solution)/shard_map/ppermute | solution.py:80
  99.8 7.0 %collective-permute-start.18 = (f16[1056,128]{1,0:T(8,128)(2,1)S(1)}, f16[1056,128]{1,0:T(8,128)(2,1)S(1)}, u32[]{:S(2)}, u32[]{:S(2)}) collective-permute-start(f16[1056,128]{1,0:T(8,128)(2,1)S(1)} %pad_maximum_fusion.1), channel_id=1, source_target_pairs={{0,16},{1,5},{2,18},{3,7},{4,20},{5,1},{6,22},{7,3},{8,24},{9,13},... | collective-permute-start | bytes 811016 | tf_op jit(solution)/shard_map/ppermute | solution.py:80
  100.3 11.7 %collective-permute-start.14 = (f16[1296,128]{1,0:T(8,128)(2,1)S(1)}, f16[1296,128]{1,0:T(8,128)(2,1)S(1)}, u32[]{:S(2)}, u32[]{:S(2)}) collective-permute-start(f16[1296,128]{1,0:T(8,128)(2,1)S(1)} %convert_element_type.144), channel_id=1, source_target_pairs={{2,66},{3,67},{6,70},{7,71},{10,74},{11,75},{14,78},{15,79},{18,82... | collective-permute-start | bytes 995336 | tf_op jit(solution)/shard_map/ppermute | solution.py:80
  107.2 9.3 %collective-permute-start.21 = (f16[1040,128]{1,0:T(8,128)(2,1)S(1)}, f16[1040,128]{1,0:T(8,128)(2,1)S(1)}, u32[]{:S(2)}, u32[]{:S(2)}) collective-permute-start(f16[1040,128]{1,0:T(8,128)(2,1)S(1)} %convert_element_type.165), channel_id=1, source_target_pairs={{0,64},{1,65},{4,68},{5,69},{8,72},{9,73},{12,76},{13,77},{16,80},... | collective-permute-start | bytes 798728 | tf_op jit(solution)/shard_map/ppermute | solution.py:80
  112.1 5.5 %collective-permute-start.15 = (f32[512,128]{1,0:T(8,128)S(1)}, f32[512,128]{1,0:T(8,128)S(1)}, u32[]{:S(2)}, u32[]{:S(2)}) collective-permute-start(f32[512,128]{1,0:T(8,128)S(1)} %slice.144), channel_id=1, source_target_pairs={{1,0},{0,1},{3,2},{2,3},{5,4},{4,5},{7,6},{6,7},{9,8},{8,9},{11,10... | collective-permute-start | bytes 786440 | tf_op jit(solution)/shard_map/ppermute | solution.py:80
  118.7 12.0 %collective-permute-start.25 = (f16[528,128]{1,0:T(8,128)(2,1)S(1)}, f16[528,128]{1,0:T(8,128)(2,1)S(1)}, u32[]{:S(2)}, u32[]{:S(2)}) collective-permute-start(f16[528,128]{1,0:T(8,128)(2,1)S(1)} %convert_element_type.177), channel_id=1, source_target_pairs={{0,1},{1,32},{2,65},{3,96},{4,5},{5,36},{6,69},{7,100},{8,9},{9,40... | collective-permute-start | bytes 405512 | tf_op jit(solution)/shard_map/ppermute | solution.py:80
  124.0 9.2 %collective-permute-start.24 = (f16[528,128]{1,0:T(8,128)(2,1)S(1)}, f16[528,128]{1,0:T(8,128)(2,1)S(1)}, u32[]{:S(2)}, u32[]{:S(2)}) collective-permute-start(f16[528,128]{1,0:T(8,128)(2,1)S(1)} %convert_element_type.174), channel_id=1, source_target_pairs={{0,17},{1,48},{2,81},{3,112},{4,21},{5,52},{6,85},{7,116},{8,25},{... | collective-permute-start | bytes 405512 | tf_op jit(solution)/shard_map/ppermute | solution.py:80
  126.3 8.4 %collective-permute-start.23 = (f16[528,128]{1,0:T(8,128)(2,1)S(1)}, f16[528,128]{1,0:T(8,128)(2,1)S(1)}, u32[]{:S(2)}, u32[]{:S(2)}) collective-permute-start(f16[528,128]{1,0:T(8,128)(2,1)S(1)} %convert_element_type.171), channel_id=1, source_target_pairs={{0,16},{1,49},{2,50},{3,19},{4,20},{5,53},{6,54},{7,23},{8,24},{9,... | collective-permute-start | bytes 405512 | tf_op jit(solution)/shard_map/ppermute | solution.py:80
  126.4 10.1 %collective-permute-start.22 = (f16[528,128]{1,0:T(8,128)(2,1)S(1)}, f16[528,128]{1,0:T(8,128)(2,1)S(1)}, u32[]{:S(2)}, u32[]{:S(2)}) collective-permute-start(f16[528,128]{1,0:T(8,128)(2,1)S(1)} %convert_element_type.168), channel_id=1, source_target_pairs={{0,0},{1,33},{2,34},{3,3},{4,4},{5,37},{6,38},{7,7},{8,8},{9,41},{... | collective-permute-start | bytes 405512 | tf_op jit(solution)/shard_map/ppermute | solution.py:80

commit v9 on v8

--- a/solution.py
+++ b/solution.py
@@ -171,12 +171,9 @@
 def far_kernel(place, other, scaled, *rest):
     outs, total = rest[:4], rest[4]
 
-    def step(t, _):
+    for t in range(4):
         total[...] = product(other[...], scaled[t])
         scatter_blocks(place, total, outs, t)
-        return 0
-
-    lax.fori_loop(0, 4, step, 0)
 
 
 def early_kernel(other, scaled, out):

time: 141 us -> 141 us (level)
  transfers between devices with their start and end apart: 26 -> 26, of which waited for: 14 -> 14; matrix products, arithmetic and copies ran while one was open for 2% -> 2% of each run, Pallas kernels for 19% -> 18%
where the time goes in v9:
time: 141 us; the launch traced here: 139 us
  waiting for transfers between devices  57.7 us (41%)
  starting transfers between devices  46.6 us (33%)
  Pallas kernels  28.9 us (20%)
  local copies, waits for them, and re-layouts  3.97 us (3%)
    ppermute x26, waiting for transfers between devices, permute(): return lax.ppermute(value, AXES, pairs)  57.7 us
    ppermute x26, starting transfers between devices, permute(): return lax.ppermute(value, AXES, pairs)  46.6 us
    pallas_call x12, Pallas kernels, call(): pl.pallas_call(kernel, out_shape=out_shape, in_specs=[smem] * len(scalars...  28.9 us
  transfers between devices with their start and end apart: 26, of which 14 were waited for; matrix products, arithmetic and copies ran while one was open for 2% of the time, Pallas kernels for 18%

profile of v9, /device:TPU:1, one launch (start us, length us, event | category | flops | bytes accessed | tf_op | source)
XLA Modules:
  0.0 138.9 jit_solution(398994969824431457)
XLA Ops:
  0.0 2.8 %slice.102 = bf16[1536,512]{1,0:T(8,128)(2,1)} slice(bf16[1536,1024]{1,0:T(8,128)(2,1)} %own), slice={[0:1536], [0:512]} | slice | bytes 3145728 | tf_op jit(solution)/shard_map/slice | solution.py:377
  2.8 1.4 %collective-permute-start = (bf16[1536,1024]{1,0:T(8,128)(2,1)S(1)}, bf16[1536,1024]{1,0:T(8,128)(2,1)}, u32[]{:S(2)}, u32[]{:S(2)}) collective-permute-start(bf16[1536,1024]{1,0:T(8,128)(2,1)S(1)} %copy-done), channel_id=1, source_target_pairs={{1,0},{0,1},{3,2},{2,3},{5,4},{4,5},{7,6},{6,7},{9,8},{8,9},{11,10... | collective-permute-start | bytes 9437192 | tf_op jit(solution)/shard_map/ppermute | solution.py:80
  4.2 1.3 collective-permute-start.4
  5.6 0.7 dynamic-slice_bitcast_fusion
  6.4 7.5 %own_products.1 = (bf16[4,1536,512]{2,1,0:T(8,128)(2,1)S(1)}, f32[4,10,128,128]{3,2,1,0:T(8,128)S(1)}, bf16[4,10,128,128]{3,2,1,0:T(8,128)(2,1)S(1)}, bf16[4,10,...) custom-call(s32[5]{0:T(128)S(1)} %stack.23.place, f32[2]{0:T(128)S(1)} %copy-done.1, ...), custom_call_target="tpu_custom_call" | custom-call | flops 4831838208 | tf_op jit(solution)/shard_map/own_products/pallas_call | solution.py:86
  13.9 5.8 %mate_products.1 = (f32[4,10,128,128]{3,2,1,0:T(8,128)S(1)}, bf16[4,10,128,128]{3,2,1,0:T(8,128)(2,1)S(1)}, bf16[4,10,128,128]{3,2,1,0:T(8,128)(2,1)S(1)}, bf16[4,10,128,128]{3,2,1,0:T(8,128)(2,1)S(1)}) custom-call(s32[13]{0:T(128)S(1)} %concatenate.16.place, ...), custom_call_target="tpu_custom_call", output_to_operand_aliasing={{0}: (3, {}), {1}: (4, {}), {2}: (5, {}), {3}: (6, {})} | custom-call | flops 3221225472 | tf_op jit(solution)/shard_map/mate_products/pallas_call | solution.py:86
  19.7 3.8 %collective-permute-start.3 = (bf16[4,10,128,128]{3,2,1,0:T(8,128)(2,1)S(1)}, bf16[4,10,128,128]{3,2,1,0:T(8,128)(2,1)S(1)}, u32[]{:S(2)}, u32[]{:S(2)}) collective-permute-start(bf16[4,10,128,128]{3,2,1,0:T(8,128)(2,1)S(1)} %get-tuple-element.62), channel_id=1, source_target_pairs={{0,12},{1,49},{2,14},{3,51},{4,8},{5,53},{6,10},{7,55},{8,4},{9,57... | collective-permute-start | bytes 3932168 | tf_op jit(solution)/shard_map/ppermute | solution.py:80
  23.5 0.7 collective-permute-start.1
  24.4 16.2 %collective-permute-done.4.other = bf16[1536,512]{1,0:T(8,128)(2,1)} collective-permute-done((bf16[1536,512]{1,0:T(8,128)(2,1)}, bf16[1536,512]{1,0:T(8,128)(2,1)}, u32[]{:S(2)}, u32[]{:S(2)}) %collective-permute-start.4) | collective-permute-done | bytes 1572896 | tf_op jit(solution)/shard_map/ppermute | solution.py:80
  40.6 1.3 collective-permute-start.12
  41.9 5.3 %far_products.1 = (f32[4,4,128,128]{3,2,1,0:T(8,128)S(1)}, bf16[4,4,128,128]{3,2,1,0:T(8,128)(2,1)S(1)}, bf16[4,4,128,128]{3,2,1,0:T(8,128)(2,1)S(1)}, bf16[4,4,128,128]{3,2,1,0:T(8,128)(2,1)S(1)}) custom-call(s32[13]{0:T(128)S(1)} %concatenate.16.place, bf16[1536,512]{1,0:T(8,128)(2,1)} %collective-permute-done.4.other, ...), custom_call_target="tpu_custom_call" | custom-call | flops 3221225472 | tf_op jit(solution)/shard_map/far_products/pallas_call | solution.py:86
  47.1 5.5 %collective-permute-done.3.c = bf16[4,10,128,128]{3,2,1,0:T(8,128)(2,1)S(1)} collective-permute-done((bf16[4,10,128,128]{3,2,1,0:T(8,128)(2,1)S(1)}, bf16[4,10,128,128]{3,2,1,0:T(8,128)(2,1)S(1)}, u32[]{:S(2)}, u32[]{:S(2)}) %collective-permute-start.3) | collective-permute-done | bytes 1310752 | tf_op jit(solution)/shard_map/ppermute | solution.py:80
  52.7 2.8 %collective-permute-start.9 = (bf16[4,4,128,128]{3,2,1,0:T(8,128)(2,1)S(1)}, bf16[4,4,128,128]{3,2,1,0:T(8,128)(2,1)S(1)}, u32[]{:S(2)}, u32[]{:S(2)}) collective-permute-start(bf16[4,4,128,128]{3,2,1,0:T(8,128)(2,1)S(1)} %get-tuple-element.75), channel_id=1, source_target_pairs={{0,12},{1,49},{2,14},{3,51},{4,8},{5,53},{6,10},{7,55},{8,4},{9,57... | collective-permute-start | bytes 1572872 | tf_op jit(solution)/shard_map/ppermute | solution.py:80
  55.5 0.6 collective-permute-start.5
  56.2 1.0 collective-permute-start.11
  57.2 0.9 first_sum.3
  58.2 9.8 %collective-permute-done.9.c = bf16[4,4,128,128]{3,2,1,0:T(8,128)(2,1)S(1)} collective-permute-done((bf16[4,4,128,128]{3,2,1,0:T(8,128)(2,1)S(1)}, bf16[4,4,128,128]{3,2,1,0:T(8,128)(2,1)S(1)}, u32[]{:S(2)}, u32[]{:S(2)}) %collective-permute-start.9) | collective-permute-done | bytes 524320 | tf_op jit(solution)/shard_map/ppermute | solution.py:80
  68.0 2.5 %collective-permute-start.10 = (f16[1296,128]{1,0:T(8,128)(2,1)S(1)}, f16[1296,128]{1,0:T(8,128)(2,1)S(1)}, u32[]{:S(2)}, u32[]{:S(2)}) collective-permute-start(f16[1296,128]{1,0:T(8,128)(2,1)S(1)} %convert_element_type.141), channel_id=1, source_target_pairs={{0,48},{1,13},{2,50},{3,15},{4,52},{5,9},{6,54},{7,11},{8,56},{9,5... | collective-permute-start | bytes 995336 | tf_op jit(solution)/shard_map/ppermute | solution.py:80
  70.5 0.9 collective-permute-start.6
  71.4 2.6 %early_products.1.early = f32[4,384,512]{2,1,0:T(8,128)S(1)} custom-call(bf16[1536,384]{1,0:T(8,128)(2,1)S(1)} %collective-permute-done.12.other, bf16[4,1536,512]{2,1,0:T(8,128)(2,1)S(1)} %get-tuple-element.54.scaled), custom_call_target="tpu_custom_call" | custom-call | flops 2415919104 | tf_op jit(solution)/shard_map/early_products/pallas_call | solution.py:86
  74.1 1.9 %collective-permute-done.11.other = bf16[1536,128]{1,0:T(8,128)(2,1)S(1)} collective-permute-done((bf16[1536,128]{1,0:T(8,128)(2,1)S(1)}, bf16[1536,128]{1,0:T(8,128)(2,1)S(1)}, u32[]{:S(2)}, u32[]{:S(2)}) %collective-permute-start.11) | collective-permute-done | bytes 393248 | tf_op jit(solution)/shard_map/ppermute | solution.py:80
  75.9 2.5 %late_products.1 = (f32[4,4,128,128]{3,2,1,0:T(8,128)S(1)}, bf16[4,4,128,128]{3,2,1,0:T(8,128)(2,1)S(1)}, bf16[4,4,128,128]{3,2,1,0:T(8,128)(2,1)S(1)}, bf16[4,4,128,128]{3,2,1,0:T(8,128)(2,1)S(1)}) custom-call(s32[13]{0:T(128)S(1)} %concatenate.16.place, bf16[1536,128]{1,0:T(8,128)(2,1)S(1)} %collective-permute-done.11.other, ...), custom_call_target="tpu_custom_call" | custom-call | flops 805306368 | tf_op jit(solution)/shard_map/late_products/pallas_call | solution.py:86
  78.4 0.4 first_sum.4
  79.0 3.6 %collective-permute-start.13 = (bf16[4,4,128,128]{3,2,1,0:T(8,128)(2,1)S(1)}, bf16[4,4,128,128]{3,2,1,0:T(8,128)(2,1)S(1)}, u32[]{:S(2)}, u32[]{:S(2)}) collective-permute-start(bf16[4,4,128,128]{3,2,1,0:T(8,128)(2,1)S(1)} %get-tuple-element.82), channel_id=1, source_target_pairs={{0,12},{1,49},{2,14},{3,51},{4,8},{5,53},{6,10},{7,55},{8,4},{9,57... | collective-permute-start | bytes 1572872 | tf_op jit(solution)/shard_map/ppermute | solution.py:80
  82.7 0.7 collective-permute-start.16
  83.3 0.2 multiply_add_fusion.1.value
  83.6 11.6 %collective-permute-done.13.c = bf16[4,4,128,128]{3,2,1,0:T(8,128)(2,1)S(1)} collective-permute-done((bf16[4,4,128,128]{3,2,1,0:T(8,128)(2,1)S(1)}, bf16[4,4,128,128]{3,2,1,0:T(8,128)(2,1)S(1)}, u32[]{:S(2)}, u32[]{:S(2)}) %collective-permute-start.13) | collective-permute-done | bytes 524320 | tf_op jit(solution)/shard_map/ppermute | solution.py:80
  95.1 0.7 collective-permute-done.16.a
  95.9 0.4 first_sum.5
  96.4 2.8 %collective-permute-start.20 = (f16[1056,128]{1,0:T(8,128)(2,1)S(1)}, f16[1056,128]{1,0:T(8,128)(2,1)S(1)}, u32[]{:S(2)}, u32[]{:S(2)}) collective-permute-start(f16[1056,128]{1,0:T(8,128)(2,1)S(1)} %pad_maximum_fusion.3), channel_id=1, source_target_pairs={{0,48},{1,13},{2,50},{3,15},{4,52},{5,9},{6,54},{7,11},{8,56},{9,5... | collective-permute-start | bytes 811016 | tf_op jit(solution)/shard_map/ppermute | solution.py:80
  99.3 0.6 collective-permute-start.19
  100.0 0.3 collective-permute-start.18
  100.3 0.2 seal.2
  100.6 1.3 collective-permute-start.14
  101.9 3.6 %collective-permute-done.20 = f16[1056,128]{1,0:T(8,128)(2,1)S(1)} collective-permute-done((f16[1056,128]{1,0:T(8,128)(2,1)S(1)}, f16[1056,128]{1,0:T(8,128)(2,1)S(1)}, u32[]{:S(2)}, u32[]{:S(2)}) %collective-permute-start.20) | collective-permute-done | bytes 270368 | tf_op jit(solution)/shard_map/ppermute | solution.py:80
  105.5 0.7 collective-permute-done.19
  106.2 0.7 collective-permute-done.18
  107.4 4.8 %collective-permute-start.21 = (f16[1040,128]{1,0:T(8,128)(2,1)S(1)}, f16[1040,128]{1,0:T(8,128)(2,1)S(1)}, u32[]{:S(2)}, u32[]{:S(2)}) collective-permute-start(f16[1040,128]{1,0:T(8,128)(2,1)S(1)} %convert_element_type.165), channel_id=1, source_target_pairs={{0,64},{1,65},{4,68},{5,69},{8,72},{9,73},{12,76},{13,77},{16,80},... | collective-permute-start | bytes 798728 | tf_op jit(solution)/shard_map/ppermute | solution.py:80
  112.4 4.4 %collective-permute-start.15 = (f32[512,128]{1,0:T(8,128)S(1)}, f32[512,128]{1,0:T(8,128)S(1)}, u32[]{:S(2)}, u32[]{:S(2)}) collective-permute-start(f32[512,128]{1,0:T(8,128)S(1)} %slice.144), channel_id=1, source_target_pairs={{1,0},{0,1},{3,2},{2,3},{5,4},{4,5},{7,6},{6,7},{9,8},{8,9},{11,10... | collective-permute-start | bytes 786440 | tf_op jit(solution)/shard_map/ppermute | solution.py:80
  116.8 1.1 collective-permute-done.15.twin
  117.9 1.0 pack.1
  119.0 5.2 %collective-permute-start.25 = (f16[528,128]{1,0:T(8,128)(2,1)S(1)}, f16[528,128]{1,0:T(8,128)(2,1)S(1)}, u32[]{:S(2)}, u32[]{:S(2)}) collective-permute-start(f16[528,128]{1,0:T(8,128)(2,1)S(1)} %convert_element_type.177), channel_id=1, source_target_pairs={{0,1},{1,32},{2,65},{3,96},{4,5},{5,36},{6,69},{7,100},{8,9},{9,40... | collective-permute-start | bytes 405512 | tf_op jit(solution)/shard_map/ppermute | solution.py:80
  124.2 2.3 %collective-permute-start.24 = (f16[528,128]{1,0:T(8,128)(2,1)S(1)}, f16[528,128]{1,0:T(8,128)(2,1)S(1)}, u32[]{:S(2)}, u32[]{:S(2)}) collective-permute-start(f16[528,128]{1,0:T(8,128)(2,1)S(1)} %convert_element_type.174), channel_id=1, source_target_pairs={{0,17},{1,48},{2,81},{3,112},{4,21},{5,52},{6,85},{7,116},{8,25},{... | collective-permute-start | bytes 405512 | tf_op jit(solution)/shard_map/ppermute | solution.py:80
  126.6 4.3 %collective-permute-start.22 = (f16[528,128]{1,0:T(8,128)(2,1)S(1)}, f16[528,128]{1,0:T(8,128)(2,1)S(1)}, u32[]{:S(2)}, u32[]{:S(2)}) collective-permute-start(f16[528,128]{1,0:T(8,128)(2,1)S(1)} %convert_element_type.168), channel_id=1, source_target_pairs={{0,0},{1,33},{2,34},{3,3},{4,4},{5,37},{6,38},{7,7},{8,8},{9,41},{... | collective-permute-start | bytes 405512 | tf_op jit(solution)/shard_map/ppermute | solution.py:80
  131.0 2.4 %collective-permute-done.24 = f16[528,128]{1,0:T(8,128)(2,1)S(1)} collective-permute-done((f16[528,128]{1,0:T(8,128)(2,1)S(1)}, f16[528,128]{1,0:T(8,128)(2,1)S(1)}, u32[]{:S(2)}, u32[]{:S(2)}) %collective-permute-start.24) | collective-permute-done | bytes 135200 | tf_op jit(solution)/shard_map/ppermute | solution.py:80
  133.5 1.5 %collective-permute-done.23 = f16[528,128]{1,0:T(8,128)(2,1)S(1)} collective-permute-done((f16[528,128]{1,0:T(8,128)(2,1)S(1)}, f16[528,128]{1,0:T(8,128)(2,1)S(1)}, u32[]{:S(2)}, u32[]{:S(2)}) %collective-permute-start.23) | collective-permute-done | bytes 135200 | tf_op jit(solution)/shard_map/ppermute | solution.py:80
  135.0 1.8 %collective-permute-done.22 = f16[528,128]{1,0:T(8,128)(2,1)S(1)} collective-permute-done((f16[528,128]{1,0:T(8,128)(2,1)S(1)}, f16[528,128]{1,0:T(8,128)(2,1)S(1)}, u32[]{:S(2)}, u32[]{:S(2)}) %collective-permute-start.22) | collective-permute-done | bytes 135200 | tf_op jit(solution)/shard_map/ppermute | solution.py:80
  136.8 2.2 %unpack.1 = f32[128,2,1024]{2,1,0:T(2,128)} custom-call(s32[13]{0:T(128)S(1)} %concatenate.16.place, f32[512,128]{1,0:T(8,128)S(1)} %convert_multiply_fusion.3.a, f32[512,128]{1,0:T(8,128)S(1)} %convert_multiply_fusion.2.b, f32[512,128]{1,0:T(8,128)S(1)} %convert_multiply_fusion.1.c, f32[512,128]{1,0:T(8,128)S(1)} %convert_multiply_fusion.d), custom_call_target="tpu_custom_call" | custom-call | flops 262144 | tf_op jit(solution)/shard_map/unpack/pallas_call | solution.py:86
  (69 shorter events, 2.1 us)
Async XLA Ops:
  0.0 2.8 %copy-start = (bf16[1536,1024]{1,0:T(8,128)(2,1)S(1)}, bf16[1536,1024]{1,0:T(8,128)(2,1)}, u32[]{:S(2)}) copy-start(bf16[1536,1024]{1,0:T(8,128)(2,1)} %own) | copy-start | bytes 9437188
  0.0 6.4 %copy-start.2 = (f32[1536]{0:T(1024)S(1)}, f32[1536]{0:T(1024)}, u32[]{:S(2)}) copy-start(f32[1536]{0:T(1024)} %param.5) | copy-start | bytes 18436
  0.0 6.4 %copy-start.1 = (f32[2]{0:T(128)S(1)}, f32[2]{0:T(128)}, u32[]{:S(2)}) copy-start(f32[2]{0:T(128)} %frequencies.1) | copy-start | bytes 28
  2.8 11.0 %collective-permute-start = (bf16[1536,1024]{1,0:T(8,128)(2,1)S(1)}, bf16[1536,1024]{1,0:T(8,128)(2,1)}, u32[]{:S(2)}, u32[]{:S(2)}) collective-permute-start(bf16[1536,1024]{1,0:T(8,128)(2,1)S(1)} %copy-done), channel_id=1, source_target_pairs={{1,0},{0,1},{3,2},{2,3},{5,4},{4,5},{7,6},{6,7},{9,8},{8,9},{11,10... | collective-permute-start | bytes 9437192 | tf_op jit(solution)/shard_map/ppermute | solution.py:80
  4.2 36.3 %collective-permute-start.4 = (bf16[1536,512]{1,0:T(8,128)(2,1)}, bf16[1536,512]{1,0:T(8,128)(2,1)}, u32[]{:S(2)}, u32[]{:S(2)}) collective-permute-start(bf16[1536,512]{1,0:T(8,128)(2,1)} %slice.102), channel_id=1, source_target_pairs={{2,0},{3,1},{1,2},{0,3},{6,4},{7,5},{5,6},{4,7},{10,8},{11,9},{9,1... | collective-permute-start | bytes 4718600 | tf_op jit(solution)/shard_map/ppermute | solution.py:80
  19.7 33.0 %collective-permute-start.3 = (bf16[4,10,128,128]{3,2,1,0:T(8,128)(2,1)S(1)}, bf16[4,10,128,128]{3,2,1,0:T(8,128)(2,1)S(1)}, u32[]{:S(2)}, u32[]{:S(2)}) collective-permute-start(bf16[4,10,128,128]{3,2,1,0:T(8,128)(2,1)S(1)} %get-tuple-element.62), channel_id=1, source_target_pairs={{0,12},{1,49},{2,14},{3,51},{4,8},{5,53},{6,10},{7,55},{8,4},{9,57... | collective-permute-start | bytes 3932168 | tf_op jit(solution)/shard_map/ppermute | solution.py:80
  23.5 32.0 %collective-permute-start.2 = (bf16[4,10,128,128]{3,2,1,0:T(8,128)(2,1)S(1)}, bf16[4,10,128,128]{3,2,1,0:T(8,128)(2,1)S(1)}, u32[]{:S(2)}, u32[]{:S(2)}) collective-permute-start(bf16[4,10,128,128]{3,2,1,0:T(8,128)(2,1)S(1)} %get-tuple-element.61), channel_id=1, source_target_pairs={{0,8},{1,33},{2,10},{3,35},{4,12},{5,37},{6,14},{7,39},{8,0},{9,41... | collective-permute-start | bytes 3932168 | tf_op jit(solution)/shard_map/ppermute | solution.py:80
  23.5 32.0 %collective-permute-start.1 = (bf16[4,10,128,128]{3,2,1,0:T(8,128)(2,1)S(1)}, bf16[4,10,128,128]{3,2,1,0:T(8,128)(2,1)S(1)}, u32[]{:S(2)}, u32[]{:S(2)}) collective-permute-start(bf16[4,10,128,128]{3,2,1,0:T(8,128)(2,1)S(1)} %get-tuple-element.60), channel_id=1, source_target_pairs={{0,4},{1,17},{2,6},{3,19},{4,0},{5,21},{6,2},{7,23},{8,12},{9,25},... | collective-permute-start | bytes 3932168 | tf_op jit(solution)/shard_map/ppermute | solution.py:80
  40.6 30.8 %collective-permute-start.12 = (bf16[1536,384]{1,0:T(8,128)(2,1)S(1)}, bf16[1536,384]{1,0:T(8,128)(2,1)S(1)}, u32[]{:S(2)}, u32[]{:S(2)}) collective-permute-start(bf16[1536,384]{1,0:T(8,128)(2,1)S(1)} %slice.110), channel_id=1, source_target_pairs={{2,0},{3,1},{1,2},{0,3},{6,4},{7,5},{5,6},{4,7},{10,8},{11,9},{9,1... | collective-permute-start | bytes 3538952 | tf_op jit(solution)/shard_map/ppermute | solution.py:80
  52.7 15.3 %collective-permute-start.9 = (bf16[4,4,128,128]{3,2,1,0:T(8,128)(2,1)S(1)}, bf16[4,4,128,128]{3,2,1,0:T(8,128)(2,1)S(1)}, u32[]{:S(2)}, u32[]{:S(2)}) collective-permute-start(bf16[4,4,128,128]{3,2,1,0:T(8,128)(2,1)S(1)} %get-tuple-element.75), channel_id=1, source_target_pairs={{0,12},{1,49},{2,14},{3,51},{4,8},{5,53},{6,10},{7,55},{8,4},{9,57... | collective-permute-start | bytes 1572872 | tf_op jit(solution)/shard_map/ppermute | solution.py:80
  55.5 14.9 %collective-permute-start.7 = (bf16[4,4,128,128]{3,2,1,0:T(8,128)(2,1)S(1)}, bf16[4,4,128,128]{3,2,1,0:T(8,128)(2,1)S(1)}, u32[]{:S(2)}, u32[]{:S(2)}) collective-permute-start(bf16[4,4,128,128]{3,2,1,0:T(8,128)(2,1)S(1)} %get-tuple-element.71), channel_id=1, source_target_pairs={{0,8},{1,33},{2,10},{3,35},{4,12},{5,37},{6,14},{7,39},{8,0},{9,41... | collective-permute-start | bytes 1572872 | tf_op jit(solution)/shard_map/ppermute | solution.py:80
  55.5 15.0 %collective-permute-start.5 = (bf16[4,4,128,128]{3,2,1,0:T(8,128)(2,1)S(1)}, bf16[4,4,128,128]{3,2,1,0:T(8,128)(2,1)S(1)}, u32[]{:S(2)}, u32[]{:S(2)}) collective-permute-start(bf16[4,4,128,128]{3,2,1,0:T(8,128)(2,1)S(1)} %get-tuple-element.67), channel_id=1, source_target_pairs={{0,4},{1,17},{2,6},{3,19},{4,0},{5,21},{6,2},{7,23},{8,12},{9,25},... | collective-permute-start | bytes 1572872 | tf_op jit(solution)/shard_map/ppermute | solution.py:80
  56.2 19.7 %collective-permute-start.11 = (bf16[1536,128]{1,0:T(8,128)(2,1)S(1)}, bf16[1536,128]{1,0:T(8,128)(2,1)S(1)}, u32[]{:S(2)}, u32[]{:S(2)}) collective-permute-start(bf16[1536,128]{1,0:T(8,128)(2,1)S(1)} %slice.109), channel_id=1, source_target_pairs={{2,0},{3,1},{1,2},{0,3},{6,4},{7,5},{5,6},{4,7},{10,8},{11,9},{9,1... | collective-permute-start | bytes 1179656 | tf_op jit(solution)/shard_map/ppermute | solution.py:80
  68.0 11.0 %collective-permute-start.10 = (f16[1296,128]{1,0:T(8,128)(2,1)S(1)}, f16[1296,128]{1,0:T(8,128)(2,1)S(1)}, u32[]{:S(2)}, u32[]{:S(2)}) collective-permute-start(f16[1296,128]{1,0:T(8,128)(2,1)S(1)} %convert_element_type.141), channel_id=1, source_target_pairs={{0,48},{1,13},{2,50},{3,15},{4,52},{5,9},{6,54},{7,11},{8,56},{9,5... | collective-permute-start | bytes 995336 | tf_op jit(solution)/shard_map/ppermute | solution.py:80
  70.5 12.2 %collective-permute-start.8 = (f16[1296,128]{1,0:T(8,128)(2,1)S(1)}, f16[1296,128]{1,0:T(8,128)(2,1)S(1)}, u32[]{:S(2)}, u32[]{:S(2)}) collective-permute-start(f16[1296,128]{1,0:T(8,128)(2,1)S(1)} %convert_element_type.138), channel_id=1, source_target_pairs={{0,32},{1,9},{2,34},{3,11},{4,36},{5,13},{6,38},{7,15},{8,40},{9,1... | collective-permute-start | bytes 995336 | tf_op jit(solution)/shard_map/ppermute | solution.py:80
  70.5 12.1 %collective-permute-start.6 = (f16[1296,128]{1,0:T(8,128)(2,1)S(1)}, f16[1296,128]{1,0:T(8,128)(2,1)S(1)}, u32[]{:S(2)}, u32[]{:S(2)}) collective-permute-start(f16[1296,128]{1,0:T(8,128)(2,1)S(1)} %convert_element_type.135), channel_id=1, source_target_pairs={{0,16},{1,5},{2,18},{3,7},{4,20},{5,1},{6,22},{7,3},{8,24},{9,13},... | collective-permute-start | bytes 995336 | tf_op jit(solution)/shard_map/ppermute | solution.py:80
  79.0 16.1 %collective-permute-start.13 = (bf16[4,4,128,128]{3,2,1,0:T(8,128)(2,1)S(1)}, bf16[4,4,128,128]{3,2,1,0:T(8,128)(2,1)S(1)}, u32[]{:S(2)}, u32[]{:S(2)}) collective-permute-start(bf16[4,4,128,128]{3,2,1,0:T(8,128)(2,1)S(1)} %get-tuple-element.82), channel_id=1, source_target_pairs={{0,12},{1,49},{2,14},{3,51},{4,8},{5,53},{6,10},{7,55},{8,4},{9,57... | collective-permute-start | bytes 1572872 | tf_op jit(solution)/shard_map/ppermute | solution.py:80
  82.7 12.5 %collective-permute-start.17 = (bf16[4,4,128,128]{3,2,1,0:T(8,128)(2,1)S(1)}, bf16[4,4,128,128]{3,2,1,0:T(8,128)(2,1)S(1)}, u32[]{:S(2)}, u32[]{:S(2)}) collective-permute-start(bf16[4,4,128,128]{3,2,1,0:T(8,128)(2,1)S(1)} %get-tuple-element.90), channel_id=1, source_target_pairs={{0,8},{1,33},{2,10},{3,35},{4,12},{5,37},{6,14},{7,39},{8,0},{9,41... | collective-permute-start | bytes 1572872 | tf_op jit(solution)/shard_map/ppermute | solution.py:80
  82.7 13.2 %collective-permute-start.16 = (bf16[4,4,128,128]{3,2,1,0:T(8,128)(2,1)S(1)}, bf16[4,4,128,128]{3,2,1,0:T(8,128)(2,1)S(1)}, u32[]{:S(2)}, u32[]{:S(2)}) collective-permute-start(bf16[4,4,128,128]{3,2,1,0:T(8,128)(2,1)S(1)} %get-tuple-element.88), channel_id=1, source_target_pairs={{0,4},{1,17},{2,6},{3,19},{4,0},{5,21},{6,2},{7,23},{8,12},{9,25},... | collective-permute-start | bytes 1572872 | tf_op jit(solution)/shard_map/ppermute | solution.py:80
  96.4 9.1 %collective-permute-start.20 = (f16[1056,128]{1,0:T(8,128)(2,1)S(1)}, f16[1056,128]{1,0:T(8,128)(2,1)S(1)}, u32[]{:S(2)}, u32[]{:S(2)}) collective-permute-start(f16[1056,128]{1,0:T(8,128)(2,1)S(1)} %pad_maximum_fusion.3), channel_id=1, source_target_pairs={{0,48},{1,13},{2,50},{3,15},{4,52},{5,9},{6,54},{7,11},{8,56},{9,5... | collective-permute-start | bytes 811016 | tf_op jit(solution)/shard_map/ppermute | solution.py:80
  99.3 6.9 %collective-permute-start.19 = (f16[1056,128]{1,0:T(8,128)(2,1)S(1)}, f16[1056,128]{1,0:T(8,128)(2,1)S(1)}, u32[]{:S(2)}, u32[]{:S(2)}) collective-permute-start(f16[1056,128]{1,0:T(8,128)(2,1)S(1)} %pad_maximum_fusion.2), channel_id=1, source_target_pairs={{0,32},{1,9},{2,34},{3,11},{4,36},{5,13},{6,38},{7,15},{8,40},{9,1... | collective-permute-start | bytes 811016 | tf_op jit(solution)/shard_map/ppermute | solution.py:80
  100.0 7.0 %collective-permute-start.18 = (f16[1056,128]{1,0:T(8,128)(2,1)S(1)}, f16[1056,128]{1,0:T(8,128)(2,1)S(1)}, u32[]{:S(2)}, u32[]{:S(2)}) collective-permute-start(f16[1056,128]{1,0:T(8,128)(2,1)S(1)} %pad_maximum_fusion.1), channel_id=1, source_target_pairs={{0,16},{1,5},{2,18},{3,7},{4,20},{5,1},{6,22},{7,3},{8,24},{9,13},... | collective-permute-start | bytes 811016 | tf_op jit(solution)/shard_map/ppermute | solution.py:80
  100.6 11.7 %collective-permute-start.14 = (f16[1296,128]{1,0:T(8,128)(2,1)S(1)}, f16[1296,128]{1,0:T(8,128)(2,1)S(1)}, u32[]{:S(2)}, u32[]{:S(2)}) collective-permute-start(f16[1296,128]{1,0:T(8,128)(2,1)S(1)} %convert_element_type.144), channel_id=1, source_target_pairs={{2,66},{3,67},{6,70},{7,71},{10,74},{11,75},{14,78},{15,79},{18,82... | collective-permute-start | bytes 995336 | tf_op jit(solution)/shard_map/ppermute | solution.py:80
  107.4 9.3 %collective-permute-start.21 = (f16[1040,128]{1,0:T(8,128)(2,1)S(1)}, f16[1040,128]{1,0:T(8,128)(2,1)S(1)}, u32[]{:S(2)}, u32[]{:S(2)}) collective-permute-start(f16[1040,128]{1,0:T(8,128)(2,1)S(1)} %convert_element_type.165), channel_id=1, source_target_pairs={{0,64},{1,65},{4,68},{5,69},{8,72},{9,73},{12,76},{13,77},{16,80},... | collective-permute-start | bytes 798728 | tf_op jit(solution)/shard_map/ppermute | solution.py:80
  112.4 5.5 %collective-permute-start.15 = (f32[512,128]{1,0:T(8,128)S(1)}, f32[512,128]{1,0:T(8,128)S(1)}, u32[]{:S(2)}, u32[]{:S(2)}) collective-permute-start(f32[512,128]{1,0:T(8,128)S(1)} %slice.144), channel_id=1, source_target_pairs={{1,0},{0,1},{3,2},{2,3},{5,4},{4,5},{7,6},{6,7},{9,8},{8,9},{11,10... | collective-permute-start | bytes 786440 | tf_op jit(solution)/shard_map/ppermute | solution.py:80
  119.0 12.0 %collective-permute-start.25 = (f16[528,128]{1,0:T(8,128)(2,1)S(1)}, f16[528,128]{1,0:T(8,128)(2,1)S(1)}, u32[]{:S(2)}, u32[]{:S(2)}) collective-permute-start(f16[528,128]{1,0:T(8,128)(2,1)S(1)} %convert_element_type.177), channel_id=1, source_target_pairs={{0,1},{1,32},{2,65},{3,96},{4,5},{5,36},{6,69},{7,100},{8,9},{9,40... | collective-permute-start | bytes 405512 | tf_op jit(solution)/shard_map/ppermute | solution.py:80
  124.2 9.2 %collective-permute-start.24 = (f16[528,128]{1,0:T(8,128)(2,1)S(1)}, f16[528,128]{1,0:T(8,128)(2,1)S(1)}, u32[]{:S(2)}, u32[]{:S(2)}) collective-permute-start(f16[528,128]{1,0:T(8,128)(2,1)S(1)} %convert_element_type.174), channel_id=1, source_target_pairs={{0,17},{1,48},{2,81},{3,112},{4,21},{5,52},{6,85},{7,116},{8,25},{... | collective-permute-start | bytes 405512 | tf_op jit(solution)/shard_map/ppermute | solution.py:80
  126.5 8.4 %collective-permute-start.23 = (f16[528,128]{1,0:T(8,128)(2,1)S(1)}, f16[528,128]{1,0:T(8,128)(2,1)S(1)}, u32[]{:S(2)}, u32[]{:S(2)}) collective-permute-start(f16[528,128]{1,0:T(8,128)(2,1)S(1)} %convert_element_type.171), channel_id=1, source_target_pairs={{0,16},{1,49},{2,50},{3,19},{4,20},{5,53},{6,54},{7,23},{8,24},{9,... | collective-permute-start | bytes 405512 | tf_op jit(solution)/shard_map/ppermute | solution.py:80
  126.6 10.1 %collective-permute-start.22 = (f16[528,128]{1,0:T(8,128)(2,1)S(1)}, f16[528,128]{1,0:T(8,128)(2,1)S(1)}, u32[]{:S(2)}, u32[]{:S(2)}) collective-permute-start(f16[528,128]{1,0:T(8,128)(2,1)S(1)} %convert_element_type.168), channel_id=1, source_target_pairs={{0,0},{1,33},{2,34},{3,3},{4,4},{5,37},{6,38},{7,7},{8,8},{9,41},{... | collective-permute-start | bytes 405512 | tf_op jit(solution)/shard_map/ppermute | solution.py:80
